TPU v7x, 32 devices: a whole 2x2x4 slice. The times are simulated.
32 devices in a mesh: row: 8 (over z, core), col: 4 (over y, x).
Axes of the slice: x: 2, y: 2, z: 4, core: 2. Of those that a mesh axis runs over, the one named last changes fastest.
Arguments:
- cells: float32 [1024, 1024], P(('row', 'col')), may hold values from 0 to 1
- instance_cell: int32 [32, 128], P('row', 'col'), may hold values from 0 to 1023, as said below
- target: float32 [1024, 4096], P('row', 'col'), may hold values from 0 to 1
- row_taps: float32 [8, 65], replicated, may hold values from -0.75 to 0.75
- col_taps: float32 [8, 65], replicated, may hold values from -0.75 to 0.75
- kernel_weight: float32 [8], replicated, may hold values from 0.05 to 0.5
Outputs:
- cells_out: float32 [1024, 1024], P(('row', 'col'))
Inputs may be any that keep to these rules, and one draw needn't show every extreme that they name: `instance_cell`: each entry is the index of the device that holds the cell, along row+col with row slowest, times 32, plus the cell's place there. Tile (a, b) lies on device (a // 4, b // 32). Among one device's tiles at most 8 name cells held by any one device, and one holding device is named by exactly 8 tiles of every device.
All inputs are finite; a program needn't handle non-finite values.
Results may differ from a plain program's by a relative error of at most 0.00016.
Values sent between devices are 32-bit elements; how exact they have to be, the bound alone decides.
No kernel may reach another device: no remote copies, remote signals or barrier semaphores. Data moves between devices by JAX's collectives and lax.ppermute only.
A program may use at most 128 MiB of HBM per device.

v0:
```python
import jax
import jax.numpy as jnp
from jax import lax
from jax.experimental import pallas as pl
from jax.experimental.pallas import tpu as pltpu
from jax.sharding import Mesh
from jax.sharding import PartitionSpec as P

TILE = 32
TAPS = 65
HALF = 32
KERNELS = 8
LANES = 128
WIDE = 256

STEEPNESS = 4.0
THRESHOLD = 0.3
STEP_RATE = 0.5

F32 = jnp.float32
BF16 = jnp.bfloat16


def split(x):
    high = x.astype(BF16)
    return high, (x - high.astype(F32)).astype(BF16)


def mm(a, b):
    return jnp.dot(a, b, preferred_element_type=F32)


def build_bands(wave_ref, fcol_ref, frow_ref, brow_ref, bcol_ref):
    rows = lax.broadcasted_iota(jnp.int32, (LANES, LANES), 0)
    lanes = lax.broadcasted_iota(jnp.int32, (LANES, LANES), 1)
    zero = jnp.zeros((LANES, LANES), F32)

    def circular(index, start):
        base = jnp.broadcast_to(wave_ref[pl.ds(index, 1), :], (LANES, LANES))
        return pltpu.roll(base, start, 1, stride=1, stride_axis=0)

    def put(ref, kernel, r0, c0, block, height=LANES, breadth=LANES):
        high, low = split(block)
        ref[kernel, 0, r0 : r0 + height, c0 : c0 + breadth] = high[:height, :breadth]
        ref[kernel, 1, r0 : r0 + height, c0 : c0 + breadth] = low[:height, :breadth]

    half = lanes < LANES // 2

    @pl.loop(0, KERNELS)
    def _(k):
        near = circular(k, 0)
        put(frow_ref, k, 0, 0, jnp.where(lanes >= rows, near, zero))
        put(frow_ref, k, 0, LANES, jnp.where(lanes < rows, near, zero))
        put(frow_ref, k, LANES, 0, zero, 64)
        put(frow_ref, k, LANES, LANES, jnp.where(lanes >= rows, near, zero), 64)
        near = circular(2 * KERNELS + k, 0)
        put(brow_ref, k, 0, 0, jnp.where(lanes >= rows, near, zero))
        put(brow_ref, k, 0, LANES, jnp.where(lanes < rows, near, zero))
        near = circular(KERNELS + k, LANES // 2)
        diagonal = jnp.where(rows >= lanes, near, zero)
        beyond = jnp.where(rows < lanes, near, zero)
        for c0, blocks in ((0, (diagonal, beyond, zero)), (LANES, (zero, diagonal, beyond))):
            for n, block in enumerate(blocks):
                height = LANES if n < 2 else LANES // 2
                high, low = split(block)
                for start, piece in ((0, high), (320, high), (640, low)):
                    r0 = start + n * LANES
                    bcol_ref[k, r0 : r0 + height, c0 : c0 + LANES] = piece[:height]
        bcol_ref[k, 960:, :] = jnp.zeros((64, WIDE), BF16)

    @pl.loop(0, KERNELS // 2)
    def _(pair):
        first, second = 3 * KERNELS + 2 * pair, 3 * KERNELS + 2 * pair + 1
        for order, (one, other) in enumerate(((first, second), (second, first))):
            block = jnp.where(half, circular(one, LANES // 2), circular(other, 0))
            high, low = split(block)
            fcol_ref[pair, order, 0] = high
            fcol_ref[pair, order, 1] = low


def make_waves(row_taps, col_taps):
    taps = jnp.concatenate([row_taps, col_taps], axis=0)
    taps = jnp.concatenate([taps, taps[:, ::-1]], axis=0)
    return jnp.pad(taps, [(0, 0), (0, LANES - TAPS)])


def transpose_blocks(parts, block):
    turned = []
    for d in range(4):
        x = parts[d]
        for s in range(1, 4):
            x = jnp.where(block == s, parts[(s + d) % 4], x)
        turned.append(pltpu.roll(x, 32 * d, 1) if d else x)
    out = []
    for s in range(4):
        x = turned[(-s) % 4]
        for b in range(1, 4):
            x = jnp.where(block == b, turned[(b - s) % 4], x)
        out.append(x)
    return out


def spread_kernel(cells_ref, instance_ref, out_ref, named_ref):
    own = cells_ref.shape[0]
    for c in range(own // 8):
        tile = cells_ref[pl.ds((c // 8) * 64 + c % 8, 8, stride=8), :]
        for d in range(out_ref.shape[0] // own):
            out_ref[d * own + c * 8 : d * own + c * 8 + 8, :] = tile
    rows = [instance_ref[a : a + 1, :] for a in range(instance_ref.shape[0])]
    named_ref[...] = jnp.concatenate(rows, axis=1)


def pack_kernel(asked_ref, me_ref, cells_ref, *rest):
    out_ref = rest[-1]
    peers, capacity = asked_ref.shape

    @pl.loop(0, peers)
    def _(i):
        base = (me_ref[0] ^ i) * capacity
        for j in range(capacity):
            asked = jnp.maximum(asked_ref[i, j], 0)
            tile = cells_ref[pl.ds(pl.multiple_of(asked * 8, 8), 8), :]
            out_ref[pl.ds(pl.multiple_of((base + j) * 8, 8), 8), :] = tile


def step_kernel(asked_ref, me_ref, cells_ref, tiles_ref, out_ref, *totals):
    owners, capacity = asked_ref.shape
    nothing = jnp.zeros((8, LANES), F32)
    for total in totals:
        total[...] = jnp.zeros_like(total)

    @pl.loop(0, owners)
    def _(i):
        base = (me_ref[1] ^ i) * capacity
        for j in range(capacity):
            asked = asked_ref[i, j]
            tile = tiles_ref[pl.ds(pl.multiple_of((base + j) * 8, 8), 8), :]
            there = pl.ds(pl.multiple_of(jnp.maximum(asked, 0) * 8, 8), 8)
            total = totals[j % len(totals)]
            total[there, :] += jnp.where(asked >= 0, tile, nothing)

    for c in range(out_ref.shape[0] // 8):
        rows = slice(c * 8, c * 8 + 8)
        total = totals[0][rows, :]
        for other in totals[1:]:
            total = total + other[rows, :]
        there = pl.ds((c // 8) * 64 + c % 8, 8, stride=8)
        out_ref[there, :] = cells_ref[there, :] - STEP_RATE * total


def assemble_kernel(index_ref, tiles_ref, target_ref, *rest):
    mask_ref, first_ref, last_ref, turned_ref = rest[-4:]
    tile_rows, tile_cols = index_ref.shape
    height = tile_rows * TILE
    groups = tile_cols // 4
    block = lax.broadcasted_iota(jnp.int32, (8, LANES), 1) // 32

    @pl.loop(0, tile_rows)
    def _(a):
        for g in range(groups):
            parts = [
                tiles_ref[pl.ds(pl.multiple_of(index_ref[a, 4 * g + b] * 8, 8), 8), :]
                for b in range(4)
            ]
            for s, piece in enumerate(transpose_blocks(parts, block)):
                turned_ref[pl.ds(g * height + a * TILE + s, 8, stride=4), :] = piece

    for g in range(groups):
        lanes = slice(LANES * g, LANES * (g + 1))
        piece = turned_ref[g * height : (g + 1) * height, :]
        mask_ref[:, lanes] = piece
        first_ref[: 2 * HALF, lanes] = piece[: 2 * HALF]
        last_ref[: 2 * HALF, lanes] = piece[height - 2 * HALF :]
    first_ref[2 * HALF :, :] = target_ref[:HALF, :]
    last_ref[2 * HALF :, :] = target_ref[height - HALF :, :]


def target_strips(target_ref, top_ref, bottom_ref, strip):
    height = target_ref.shape[0]
    quarter = (height + 2 * HALF) // 4
    for row in range(0, height + 2 * HALF, 16):
        if row < HALF:
            ref, start = top_ref, 2 * HALF + row
        elif row < HALF + height:
            ref, start = target_ref, row - HALF
        else:
            ref, start = bottom_ref, 2 * HALF + row - HALF - height
        strip(row, ref, slice(start, start + 16), row // quarter, row % quarter)


def edges_kernel(mask_ref, target_ref, top_ref, bottom_ref, first_ref, last_ref, pack_ref):
    height, breadth = mask_ref.shape
    wide = 2 * HALF
    half = height // 2
    packed = half + wide
    lane = lax.broadcasted_iota(jnp.int32, (packed, LANES), 1)
    head, tail = slice(0, LANES), slice(breadth - LANES, breadth)

    def sides(lanes):
        upper = jnp.concatenate([top_ref[:wide, lanes], mask_ref[:half, lanes]], axis=0)
        lower = jnp.concatenate([mask_ref[half:, lanes], bottom_ref[:wide, lanes]], axis=0)
        return upper, lower

    upper, lower = sides(head)
    first_ref[:packed, :] = jnp.where(lane < wide, upper, pltpu.roll(lower, wide, 1))
    upper, lower = sides(tail)
    last_ref[:packed, :] = jnp.where(lane < wide, pltpu.roll(upper, wide, 1), lower)

    quarter = (height + 2 * HALF) // 4

    def strip(row, ref, rows, part, inner):
        for side, lanes in enumerate((head, tail)):
            shift = (HALF * (part + side)) % LANES
            piece = ref[rows, lanes]
            pack_ref[side, part, inner : inner + 16, :] = (
                pltpu.roll(piece, shift, 1) if shift else piece
            )

    target_strips(target_ref, top_ref, bottom_ref, strip)
    part_of = lax.broadcasted_iota(jnp.int32, (quarter, LANES), 1) // HALF
    for side, ref in enumerate((first_ref, last_ref)):
        piece = pack_ref[side, 0]
        for part in range(1, 4):
            piece = jnp.where(part_of == part, pack_ref[side, part], piece)
        ref[packed:, :] = piece


def image_kernel(
    index_ref,
    where_ref,
    weight_ref,
    mask_ref,
    top_ref,
    bottom_ref,
    before_ref,
    after_ref,
    own_ref,
    wave_ref,
    out_ref,
    fcol_ref,
    frow_ref,
    brow_ref,
    bcol_ref,
    target_ref,
    mhigh_ref,
    mlow_ref,
    nhigh_ref,
    nlow_ref,
    field_ref,
    ghigh_ref,
    gturn_ref,
    grad_ref,
):
    tile_rows, tile_cols = index_ref.shape
    rows_here = tile_rows * TILE
    high_rows = rows_here + 4 * HALF
    field_rows = rows_here + 2 * HALF
    groups = tile_cols // 4
    wide = 2 * HALF
    block = lax.broadcasted_iota(jnp.int32, (8, LANES), 1) // 32
    build_bands(wave_ref, fcol_ref, frow_ref, brow_ref, bcol_ref)

    lane = lax.broadcasted_iota(jnp.int32, (wide, LANES), 1)
    for rows in range(0, high_rows, wide):
        if rows == 0:
            ref, start = top_ref, 0
        elif rows == high_rows - wide:
            ref, start = bottom_ref, 0
        else:
            ref, start = mask_ref, rows - wide
        half = high_rows // 2
        edge = slice(rows % half, rows % half + wide)
        turned = before_ref[edge, :]
        final = after_ref[edge, :]
        if rows < half:
            final = pltpu.roll(final, wide, 1)
        else:
            turned = pltpu.roll(turned, wide, 1)
        for g in range(groups + 1):
            fresh = final
            if g < groups:
                piece = ref[start : start + wide, LANES * g : LANES * (g + 1)]
                high, low = split(piece)
                nhigh_ref[rows : rows + wide, LANES * g : LANES * (g + 1)] = high
                nlow_ref[rows : rows + wide, LANES * g : LANES * (g + 1)] = low
                fresh = pltpu.roll(piece, wide, 1)
            high, low = split(jnp.where(lane < wide, turned, fresh))
            mhigh_ref[rows : rows + wide, LANES * g : LANES * (g + 1)] = high
            mlow_ref[rows : rows + wide, LANES * g : LANES * (g + 1)] = low
            turned = fresh
    packed = high_rows // 2
    near_lane = lax.broadcasted_iota(jnp.int32, (16, LANES), 1)

    def strip(row, ref, rows, part, inner):
        edge = slice(packed + inner, packed + inner + 16)
        back, ahead = (-HALF * part) % LANES, (HALF - HALF * part) % LANES
        turned = pltpu.roll(before_ref[edge, :], back, 1) if back else before_ref[edge, :]
        final = pltpu.roll(after_ref[edge, :], ahead, 1) if ahead else after_ref[edge, :]
        for g in range(groups + 1):
            fresh = final
            if g < groups:
                fresh = pltpu.roll(ref[rows, LANES * g : LANES * (g + 1)], HALF, 1)
            target_ref[row : row + 16, LANES * g : LANES * (g + 1)] = jnp.where(
                near_lane < HALF, turned, fresh
            )
            turned = fresh

    target_strips(own_ref, top_ref, bottom_ref, strip)

    def swapped(x):
        pieces = [
            pltpu.roll(x[:, c : c + LANES], LANES // 2, 1) for c in range(0, x.shape[1], LANES)
        ]
        return pieces[0] if len(pieces) == 1 else jnp.concatenate(pieces, axis=1)

    def columns(offset, width):
        blocks = width // LANES
        last = blocks == 1

        def windows(high_ref, low_ref):
            rows = []
            for j in range(blocks):
                place = pl.ds(pl.multiple_of(offset + j * LANES, LANES), LANES)
                high, low = high_ref[:, place], low_ref[:, place]
                rows.append(jnp.concatenate([high, low, high], axis=1))
            return rows[0] if last else jnp.concatenate(rows, axis=0)

        even_rows = windows(mhigh_ref, mlow_ref)
        odd_rows = None if last else windows(nhigh_ref, nlow_ref)
        left = lax.broadcasted_iota(jnp.int32, (high_rows, LANES), 1) < LANES // 2

        def band(quad, order):
            both = [
                jnp.concatenate(
                    [fcol_ref[2 * quad, order, v], fcol_ref[2 * quad + 1, order, v]], axis=1
                )
                for v in range(2)
            ]
            return jnp.concatenate([both[0], both[0], both[1]], axis=0)

        sums = [None, None]
        for quad in range(KERNELS // 4):
            even = mm(even_rows, band(quad, 0))
            odd = even if last else mm(odd_rows, band(quad, 1))
            for h in range(4):
                k = 4 * quad + h
                pieces = []
                for j in range(blocks):
                    rows = slice(j * high_rows, (j + 1) * high_rows)
                    lanes = slice((h // 2) * LANES, (h // 2 + 1) * LANES)
                    if last:
                        pieces.append(even[rows, lanes])
                    elif h % 2 == 0:
                        pieces.append(jnp.where(left, even[rows, lanes], odd[rows, lanes]))
                    else:
                        pieces.append(jnp.where(left, odd[rows, lanes], even[rows, lanes]))
                high, low = split(pieces[0] if last else jnp.concatenate(pieces, axis=1))
                both = mm(jnp.concatenate([frow_ref[k, 0], frow_ref[k, 1]], axis=0), high)
                field = both[:field_rows] + both[field_rows:] + mm(frow_ref[k, 0], low)
                field_ref[k, :, :width] = field
                term = weight_ref[k] * field * field
                sums[h % 2] = term if sums[h % 2] is None else sums[h % 2] + term
        intensity = sums[0] + swapped(sums[1])
        resist = 1.0 / (1.0 + jnp.exp(-STEEPNESS * (intensity - THRESHOLD)))
        place = pl.ds(pl.multiple_of(offset, LANES), width)
        target = target_ref[:, place]
        sensitivity = 2.0 * (resist - target) * STEEPNESS * resist * (1.0 - resist)
        row = where_ref[0] + lax.broadcasted_iota(jnp.int32, (field_rows, width), 0)
        col = where_ref[1] + offset + lax.broadcasted_iota(jnp.int32, (field_rows, width), 1)
        inside = (row >= 0) & (row < where_ref[2]) & (col >= 0) & (col < where_ref[3])
        sensitivity = jnp.where(inside, sensitivity, 0.0)
        ordered = (sensitivity, swapped(sensitivity))
        for k in range(KERNELS):
            product = (2.0 * weight_ref[k]) * ordered[k % 2] * field_ref[k, :, :width]
            high, low = split(product)
            near = brow_ref[k, 0, :, :field_rows]
            both = mm(jnp.concatenate([near, brow_ref[k, 1, :, :field_rows]], axis=0), high)
            part = both[:rows_here] + both[rows_here:] + mm(near, low)
            straight, turned = (part, swapped(part))[:: 1 - 2 * (k % 2)]
            ghigh_ref[k, :, place] = straight.astype(BF16)
            gturn_ref[k, :, place] = split(turned)[1]

    supers = tile_cols * TILE // WIDE

    @pl.loop(0, supers)
    def _(jj):
        columns(jj * WIDE, WIDE)

    columns(supers * WIDE, LANES)

    lower = lax.broadcasted_iota(jnp.int32, (rows_here, LANES), 1) < LANES // 2

    def spread_back(k):
        stacked = []
        for jj in range(supers):
            c0 = WIDE * jj
            high = [ghigh_ref[k, :, c0 + LANES * n : c0 + LANES * (n + 1)] for n in range(3)]
            turn = [gturn_ref[k, :, c0 + LANES * n : c0 + LANES * (n + 1)] for n in range(3)]
            row = [
                high[0],
                high[1],
                jnp.where(lower, high[2], turn[0]),
                jnp.where(lower, turn[0], turn[1]),
                jnp.where(lower, turn[1], turn[2]),
                *high,
            ]
            stacked.append(jnp.concatenate(row, axis=1))
        return mm(jnp.concatenate(stacked, axis=0), bcol_ref[k])

    def add(part, fresh):
        for g in range(groups):
            rows = slice(g * rows_here, (g + 1) * rows_here)
            top = (g // 2) * rows_here
            piece = part[top : top + rows_here, LANES * (g % 2) : LANES * (g % 2 + 1)]
            grad_ref[rows, :] = piece if fresh else grad_ref[rows, :] + piece

    add(spread_back(0), True)

    @pl.loop(1, KERNELS)
    def _(k):
        add(spread_back(k), False)

    @pl.loop(0, tile_rows)
    def _(a):
        for g in range(groups):
            base = g * rows_here + a * TILE
            parts = [grad_ref[pl.ds(base + s, 8, stride=4), :] for s in range(4)]
            for b, tile in enumerate(transpose_blocks(parts, block)):
                place = pl.multiple_of(index_ref[a, 4 * g + b] * 8, 8)
                out_ref[pl.ds(place, 8), :] = tile


def to_rows(x):
    count = x.shape[0]
    return x.reshape(count // 8, 8, 8, LANES).transpose(0, 2, 1, 3).reshape(count * 8, LANES)


def from_rows(x):
    count = x.shape[0] // 8
    return x.reshape(count // 8, 8, 8, LANES).transpose(0, 2, 1, 3).reshape(count, 8 * LANES)


def kernel_call(body, name, shapes, scratch, scalars, inputs, unread=(), megabytes=8):
    single = not isinstance(shapes, list)
    spec = pl.BlockSpec(memory_space=pltpu.VMEM)
    outs = [shapes] if single else shapes
    result = pl.pallas_call(
        body,
        out_shape=outs,
        in_specs=[pl.BlockSpec(memory_space=pltpu.SMEM)] * len(scalars)
        + [spec] * len(inputs)
        + [pl.BlockSpec(memory_space=pl.ANY)] * len(unread),
        out_specs=[spec] * len(outs),
        scratch_shapes=scratch,
        compiler_params=pltpu.CompilerParams(vmem_limit_bytes=megabytes * 2**20),
        name=name,
    )(*scalars, *inputs, *unread)
    return result[0] if single else result


def neighbours(first, last, axis):
    count = lax.axis_size(axis)
    up = [(i, i + 1) for i in range(count - 1)]
    down = [(j, i) for i, j in up]
    return lax.ppermute(last, axis, up), lax.ppermute(first, axis, down)


def doubled(table, axis):
    count = lax.axis_size(axis)
    bit = 1
    while bit < count:
        got = lax.ppermute(table, axis, [(i, i ^ bit) for i in range(count)])
        table = jnp.concatenate([table, got], axis=0)
        bit *= 2
    return table


def requests(match, value, capacity):
    rank = jnp.cumsum(match.astype(jnp.int32), axis=1) - 1
    hit = match[:, None, :] & (rank[:, None, :] == jnp.arange(capacity)[None, :, None])
    return jnp.max(jnp.where(hit, value[:, None, :], -1), axis=2)


def shards(cells, instance_cell, target, row_taps, col_taps, kernel_weight):
    deep, cores, cols = lax.axis_size("deep"), lax.axis_size("core"), lax.axis_size("col")
    everyone = ("deep", "core", "col")
    plane = ("core", "col")
    peers = cores * cols
    slots = cells.shape[0]
    tile_rows, tile_cols = instance_cell.shape
    tiles_here = tile_rows * tile_cols
    height, breadth = target.shape
    owners = deep * peers
    capacity = 2 * ((tiles_here + owners - 1) // owners)
    wide_capacity = min(tiles_here, deep * capacity)
    f32 = lambda *shape: jax.ShapeDtypeStruct(shape, F32)

    flat = to_rows(cells)
    copies, named = kernel_call(
        spread_kernel,
        "spread",
        [
            f32(deep * slots * 8, LANES),
            jax.ShapeDtypeStruct((1, tiles_here), jnp.int32),
        ],
        [],
        [],
        [flat, instance_cell],
    )
    stack = lax.all_to_all(copies, "deep", split_axis=0, concat_axis=0, tiled=True)

    near = doubled(doubled(named, "col"), "core")
    me = jnp.stack([lax.axis_index(plane), lax.axis_index(everyone)]).astype(jnp.int32)
    owner = near // slots
    asked = requests(
        owner % peers == me[0], (owner // peers) * slots + near % slots, wide_capacity
    )
    waves = make_waves(row_taps, col_taps)
    packed = kernel_call(
        pack_kernel,
        "pack",
        f32(peers * wide_capacity * 8, LANES),
        [],
        [asked, me],
        [stack],
        [waves],
    )
    packed, near = lax.optimization_barrier((packed, near))
    arrived = lax.all_to_all(packed, plane, split_axis=0, concat_axis=0, tiled=True)

    everything = doubled(near, "deep")
    wanted = requests(everything // slots == me[1], everything % slots, capacity)
    mine = named[0] // slots
    earlier = jnp.tri(tiles_here, k=-1, dtype=bool)

    def place(group, size):
        same = (group[:, None] == group[None, :]) & earlier
        where = group * size + jnp.sum(same.astype(jnp.int32), axis=1)
        return where.reshape(tile_rows, tile_cols)

    mask, first, last = kernel_call(
        assemble_kernel,
        "assemble",
        [f32(height, breadth), f32(3 * HALF, breadth), f32(3 * HALF, breadth)],
        [pltpu.VMEM((height * (breadth // LANES), LANES), F32)],
        [place(mine % peers, wide_capacity)],
        [arrived, target],
        [wanted],
    )
    top, bottom = neighbours(first, last, ("deep", "core"))
    quarter = (height + 2 * HALF) // 4
    edge = f32(height // 2 + 2 * HALF + quarter, LANES)
    first, last = kernel_call(
        edges_kernel,
        "edges",
        [edge, edge],
        [pltpu.VMEM((2, 4, quarter, LANES), F32)],
        [],
        [mask, target, top, bottom],
    )
    before, after = neighbours(first, last, "col")
    my_row = lax.axis_index(("deep", "core"))
    my_col = lax.axis_index("col")
    where = jnp.stack(
        [
            my_row * height - HALF,
            my_col * breadth - HALF,
            jnp.int32(deep * cores * height),
            jnp.int32(cols * breadth),
        ]
    ).astype(jnp.int32)
    field_rows = height + 2 * HALF
    returned = kernel_call(
        image_kernel,
        "image",
        f32(owners * capacity * 8, LANES),
        [
            pltpu.VMEM((KERNELS // 2, 2, 2, LANES, LANES), BF16),
            pltpu.VMEM((KERNELS, 2, field_rows, 256), BF16),
            pltpu.VMEM((KERNELS, 2, LANES, 256), BF16),
            pltpu.VMEM((KERNELS, 1024, WIDE), BF16),
            pltpu.VMEM((field_rows, breadth + 128), F32),
            pltpu.VMEM((height + 4 * HALF, breadth + 128), BF16),
            pltpu.VMEM((height + 4 * HALF, breadth + 128), BF16),
            pltpu.VMEM((height + 4 * HALF, breadth), BF16),
            pltpu.VMEM((height + 4 * HALF, breadth), BF16),
            pltpu.VMEM((KERNELS, field_rows, WIDE), F32),
            pltpu.VMEM((KERNELS, height, breadth + 128), BF16),
            pltpu.VMEM((KERNELS, height, breadth + 128), BF16),
            pltpu.VMEM((height * (breadth // LANES), LANES), F32),
        ],
        [place(mine, capacity), where, kernel_weight],
        [mask, top, bottom, before, after, target, waves],
        megabytes=36,
    )
    back = lax.all_to_all(returned, everyone, split_axis=0, concat_axis=0, tiled=True)
    stepped = kernel_call(
        step_kernel,
        "step",
        f32(slots * 8, LANES),
        [pltpu.VMEM((slots * 8, LANES), F32)] * 4,
        [wanted, me],
        [flat, back],
    )
    return from_rows(stepped)


def solution(mesh):
    rows, cols = mesh.devices.shape
    finer = Mesh(mesh.devices.reshape(rows // 2, 2, cols), ("deep", "core", "col"))
    row = ("deep", "core")
    placed = (P((*row, "col"), None), P(row, "col"), P(row, "col"), P(), P(), P())
    return jax.shard_map(
        shards, mesh=finer, in_specs=placed, out_specs=P((*row, "col"), None), check_vma=False
    )
```

profile of v0, /device:TPU:0, one launch (start us, length us, event | category | flops | bytes accessed | tf_op | source)
XLA Modules:
  0.0 118.0 jit_solution(10774097063764683486)
XLA Ops:
  0.0 0.9 copy-done.1
  0.9 0.7 copy-done.3
  1.6 0.8 spread.1
  2.4 6.3 %all-to-all-start = ((f32[4,256,128]{2,1,0:T(8,128)}), f32[4,256,128]{2,1,0:T(8,128)S(1)}, u32[]{:S(2)}, u32[]{:S(2)}) async-start(f32[4,256,128]{2,1,0:T(8,128)} %bitcast.5), calls=%async_computation | async-start | bytes 1048576 | tf_op jit(solution)/shard_map/all_to_all | solution.py:510
  8.7 1.5 %collective-permute-start = (s32[1,128]{1,0:T(1,128)S(1)}, s32[1,128]{1,0:T(1,128)S(1)}, u32[]{:S(2)}, u32[]{:S(2)}) collective-permute-start(s32[1,128]{1,0:T(1,128)S(1)} %get-tuple-element.14), channel_id=1, source_target_pairs={{0,1},{1,0},{2,3},{3,2},{4,5},{5,4},{6,7},{7,6},{8,9},{9,8},{10,11... | collective-permute-start | bytes 1544 | tf_op jit(solution)/shard_map/ppermute | solution.py:472
  10.3 0.5 broadcast.472
  10.8 0.7 fusion.19
  11.9 0.7 copy-done.5
  12.7 1.6 %collective-permute-start.1 = (s32[2,128]{1,0:T(2,128)S(1)}, s32[2,128]{1,0:T(2,128)S(1)}, u32[]{:S(2)}, u32[]{:S(2)}) collective-permute-start(s32[2,128]{1,0:T(2,128)S(1)} %pad_add_fusion.3), channel_id=1, source_target_pairs={{0,2},{1,3},{2,0},{3,1},{4,6},{5,7},{6,4},{7,5},{8,10},{9,11},{10,... | collective-permute-start | bytes 3080 | tf_op jit(solution)/shard_map/ppermute | solution.py:472
  14.3 2.0 %collective-permute-done.1 = s32[2,128]{1,0:T(2,128)S(1)} collective-permute-done((s32[2,128]{1,0:T(2,128)S(1)}, s32[2,128]{1,0:T(2,128)S(1)}, u32[]{:S(2)}, u32[]{:S(2)}) %collective-permute-start.1) | collective-permute-done | bytes 1056 | tf_op jit(solution)/shard_map/ppermute | solution.py:472
  16.5 1.1 collective-permute-done.2
  17.6 0.3 reduce_window_sum.22
  17.9 0.2 select_reduce_fusion.1.asked_ref
  18.1 5.1 %all-to-all-done = f32[4,256,128]{2,1,0:T(8,128)S(1)} async-done(((f32[4,256,128]{2,1,0:T(8,128)}), f32[4,256,128]{2,1,0:T(8,128)S(1)}, u32[]{:S(2)}, u32[]{:S(2)}) %all-to-all-start) | async-done | bytes 524320 | tf_op jit(solution)/shard_map/all_to_all | solution.py:510
  23.2 2.0 %pack.1 = f32[2048,128]{1,0:T(8,128)} custom-call(s32[8,32]{1,0:T(8,128)S(1)} %select_reduce_fusion.1.asked_ref, s32[2]{0:T(128)S(1)} %pad_add_fusion.4.me_ref, f32[1024,128]{1,0:T(8,128)S(1)} %bitcast.35, f32[32,128]{1,0:T(8,128)S(1)} %select_maximum_fusion.rest_0_.wave_ref), custom_call_target="tpu_custom_call" | custom-call | tf_op jit(solution)/shard_map/pack/pallas_call | solution.py:447
  25.3 3.9 %all-to-all-start.1 = ((f32[8,256,128]{2,1,0:T(8,128)}), f32[8,256,128]{2,1,0:T(8,128)S(1)}, u32[]{:S(2)}, u32[]{:S(2)}) async-start(f32[8,256,128]{2,1,0:T(8,128)} %bitcast.12), calls=%async_computation.1 | async-start | bytes 2097152 | tf_op jit(solution)/shard_map/all_to_all | solution.py:529
  29.1 2.1 %collective-permute-start.4 = (s32[16,128]{1,0:T(8,128)S(1)}, s32[16,128]{1,0:T(8,128)S(1)}, u32[]{:S(2)}, u32[]{:S(2)}) collective-permute-start(s32[16,128]{1,0:T(8,128)S(1)} %pad_add_fusion), channel_id=1, source_target_pairs={{0,16},{8,24},{16,0},{24,8},{1,17},{9,25},{17,1},{25,9},{2,18},{10... | collective-permute-start | bytes 24584 | tf_op jit(solution)/shard_map/ppermute | solution.py:472
  31.2 2.5 %collective-permute-done.4 = s32[16,128]{1,0:T(8,128)S(1)} collective-permute-done((s32[16,128]{1,0:T(8,128)S(1)}, s32[16,128]{1,0:T(8,128)S(1)}, u32[]{:S(2)}, u32[]{:S(2)}) %collective-permute-start.4) | collective-permute-done | bytes 8224 | tf_op jit(solution)/shard_map/ppermute | solution.py:472
  33.8 0.3 reduce_window_sum.23
  34.1 0.6 select_reduce_fusion.rest_0_.asked_ref
  34.7 9.3 %all-to-all-done.1 = f32[8,256,128]{2,1,0:T(8,128)S(1)} async-done(((f32[8,256,128]{2,1,0:T(8,128)}), f32[8,256,128]{2,1,0:T(8,128)S(1)}, u32[]{:S(2)}, u32[]{:S(2)}) %all-to-all-start.1) | async-done | bytes 1048608 | tf_op jit(solution)/shard_map/all_to_all | solution.py:529
  44.0 1.1 assemble.1
  45.1 2.2 %collective-permute-start.5 = (f32[96,1024]{1,0:T(8,128)S(1)}, f32[96,1024]{1,0:T(8,128)S(1)}, u32[]{:S(2)}, u32[]{:S(2)}) collective-permute-start(f32[96,1024]{1,0:T(8,128)S(1)} %get-tuple-element.19), channel_id=1, source_target_pairs={{0,4},{4,8},{8,12},{12,16},{16,20},{20,24},{24,28},{1,5},{5,9},{9,... | collective-permute-start | bytes 1179656 | tf_op jit(solution)/shard_map/ppermute | solution.py:465
  47.3 1.3 %collective-permute-start.6 = (f32[96,1024]{1,0:T(8,128)S(1)}, f32[96,1024]{1,0:T(8,128)S(1)}, u32[]{:S(2)}, u32[]{:S(2)}) collective-permute-start(f32[96,1024]{1,0:T(8,128)S(1)} %get-tuple-element.20), channel_id=1, source_target_pairs={{4,0},{8,4},{12,8},{16,12},{20,16},{24,20},{28,24},{5,1},{9,5},{13... | collective-permute-start | bytes 1179656 | tf_op jit(solution)/shard_map/ppermute | solution.py:465
  48.7 3.6 %collective-permute-done.6.bottom_ref = f32[96,1024]{1,0:T(8,128)S(1)} collective-permute-done((f32[96,1024]{1,0:T(8,128)S(1)}, f32[96,1024]{1,0:T(8,128)S(1)}, u32[]{:S(2)}, u32[]{:S(2)}) %collective-permute-start.6) | collective-permute-done | bytes 393248 | tf_op jit(solution)/shard_map/ppermute | solution.py:465
  52.4 2.9 %collective-permute-start.7 = (f32[176,128]{1,0:T(8,128)S(1)}, f32[176,128]{1,0:T(8,128)S(1)}, u32[]{:S(2)}, u32[]{:S(2)}) collective-permute-start(f32[176,128]{1,0:T(8,128)S(1)} %get-tuple-element.21), channel_id=1, source_target_pairs={{0,1},{1,2},{2,3},{4,5},{5,6},{6,7},{8,9},{9,10},{10,11},{12,13},{... | collective-permute-start | bytes 270344 | tf_op jit(solution)/shard_map/ppermute | solution.py:465
  55.3 1.3 %collective-permute-start.8 = (f32[176,128]{1,0:T(8,128)S(1)}, f32[176,128]{1,0:T(8,128)S(1)}, u32[]{:S(2)}, u32[]{:S(2)}) collective-permute-start(f32[176,128]{1,0:T(8,128)S(1)} %get-tuple-element.22), channel_id=1, source_target_pairs={{1,0},{2,1},{3,2},{5,4},{6,5},{7,6},{9,8},{10,9},{11,10},{13,12},{... | collective-permute-start | bytes 270344 | tf_op jit(solution)/shard_map/ppermute | solution.py:465
  56.7 0.7 collective-permute-done.7.before_ref
  57.4 4.3 %collective-permute-done.8.after_ref = f32[176,128]{1,0:T(8,128)S(1)} collective-permute-done((f32[176,128]{1,0:T(8,128)S(1)}, f32[176,128]{1,0:T(8,128)S(1)}, u32[]{:S(2)}, u32[]{:S(2)}) %collective-permute-start.8) | collective-permute-done | bytes 90144 | tf_op jit(solution)/shard_map/ppermute | solution.py:465
  61.7 19.2 %image.1 = f32[2048,128]{1,0:T(8,128)S(1)} custom-call(s32[4,32]{1,0:T(4,128)S(1)} %get-tuple-element.36.index_ref, s32[4]{0:T(128)S(1)} %pad_add_fusion.5.where_ref, f32[8]{0:T(128)S(1)} %copy-done.4, f32[128,1024]{1,0:T(8,128)S(1)} %get-tuple-element.18.mask_ref, f32[96,1024]{1,0:T(8,128)S(1)} %collective-permute-done.5.top_ref, ...), custom_call_target="tpu_custom_call" | custom-call | tf_op jit(solution)/shard_map/image/pallas_call | solution.py:447
  80.9 34.7 %all_to_all.33 = f32[32,64,128]{2,1,0:T(8,128)S(1)} all-to-all(f32[32,64,128]{2,1,0:T(8,128)S(1)} %bitcast.32), channel_id=1, replica_groups=mesh['deep'=4,'core'=2,'col'=4] {'deep','core','col'}, dimensions={0} | all-to-all | bytes 2097152 | tf_op jit(solution)/shard_map/all_to_all | solution.py:596
  115.6 2.4 %step.1 = f32[256,128]{1,0:T(8,128)} custom-call(s32[32,8]{1,0:T(8,128)S(1)} %select_reduce_fusion.rest_0_.asked_ref, s32[2]{0:T(128)S(1)} %pad_add_fusion.4.me_ref, f32[256,128]{1,0:T(8,128)S(1)} %bitcast.37, f32[2048,128]{1,0:T(8,128)S(1)} %bitcast.34), custom_call_target="tpu_custom_call" | custom-call | tf_op jit(solution)/shard_map/step/pallas_call | solution.py:447
  (40 shorter events, 1.1 us)
Async XLA Ops:
  0.0 0.9 copy-start.1
  0.9 0.7 copy-start.3
  2.4 20.8 %all-to-all-start = ((f32[4,256,128]{2,1,0:T(8,128)}), f32[4,256,128]{2,1,0:T(8,128)S(1)}, u32[]{:S(2)}, u32[]{:S(2)}) async-start(f32[4,256,128]{2,1,0:T(8,128)} %bitcast.5), calls=%async_computation | async-start | bytes 1048576 | tf_op jit(solution)/shard_map/all_to_all | solution.py:510
  8.7 3.9 %collective-permute-start = (s32[1,128]{1,0:T(1,128)S(1)}, s32[1,128]{1,0:T(1,128)S(1)}, u32[]{:S(2)}, u32[]{:S(2)}) collective-permute-start(s32[1,128]{1,0:T(1,128)S(1)} %get-tuple-element.14), channel_id=1, source_target_pairs={{0,1},{1,0},{2,3},{3,2},{4,5},{5,4},{6,7},{7,6},{8,9},{9,8},{10,11... | collective-permute-start | bytes 1544 | tf_op jit(solution)/shard_map/ppermute | solution.py:472
  11.9 0.7 copy-start.5
  11.9 0.7 copy-start.6
  12.7 3.6 %collective-permute-start.1 = (s32[2,128]{1,0:T(2,128)S(1)}, s32[2,128]{1,0:T(2,128)S(1)}, u32[]{:S(2)}, u32[]{:S(2)}) collective-permute-start(s32[2,128]{1,0:T(2,128)S(1)} %pad_add_fusion.3), channel_id=1, source_target_pairs={{0,2},{1,3},{2,0},{3,1},{4,6},{5,7},{6,4},{7,5},{8,10},{9,11},{10,... | collective-permute-start | bytes 3080 | tf_op jit(solution)/shard_map/ppermute | solution.py:472
  16.3 1.2 %collective-permute-start.2 = (s32[4,128]{1,0:T(4,128)S(1)}, s32[4,128]{1,0:T(4,128)S(1)}, u32[]{:S(2)}, u32[]{:S(2)}) collective-permute-start(s32[4,128]{1,0:T(4,128)S(1)} %pad_add_fusion.2), channel_id=1, source_target_pairs={{0,4},{4,0},{1,5},{5,1},{2,6},{6,2},{3,7},{7,3},{8,12},{12,8},{9,1... | collective-permute-start | bytes 6152 | tf_op jit(solution)/shard_map/ppermute | solution.py:472
  25.2 3.9 %collective-permute-start.3 = (s32[8,128]{1,0:T(8,128)S(1)}, s32[8,128]{1,0:T(8,128)S(1)}, u32[]{:S(2)}, u32[]{:S(2)}) collective-permute-start(s32[8,128]{1,0:T(8,128)S(1)} %get-tuple-element.16), channel_id=1, source_target_pairs={{0,8},{8,0},{16,24},{24,16},{1,9},{9,1},{17,25},{25,17},{2,10},{10... | collective-permute-start | bytes 12296 | tf_op jit(solution)/shard_map/ppermute | solution.py:472
  25.3 18.8 %copy-start = (f32[128,1024]{1,0:T(8,128)S(1)}, f32[128,1024]{1,0:T(8,128)}, u32[]{:S(2)}) copy-start(f32[128,1024]{1,0:T(8,128)} %own_ref.1) | copy-start | bytes 1572868
  25.3 18.8 %all-to-all-start.1 = ((f32[8,256,128]{2,1,0:T(8,128)}), f32[8,256,128]{2,1,0:T(8,128)S(1)}, u32[]{:S(2)}, u32[]{:S(2)}) async-start(f32[8,256,128]{2,1,0:T(8,128)} %bitcast.12), calls=%async_computation.1 | async-start | bytes 2097152 | tf_op jit(solution)/shard_map/all_to_all | solution.py:529
  29.1 4.6 %collective-permute-start.4 = (s32[16,128]{1,0:T(8,128)S(1)}, s32[16,128]{1,0:T(8,128)S(1)}, u32[]{:S(2)}, u32[]{:S(2)}) collective-permute-start(s32[16,128]{1,0:T(8,128)S(1)} %pad_add_fusion), channel_id=1, source_target_pairs={{0,16},{8,24},{16,0},{24,8},{1,17},{9,25},{17,1},{25,9},{2,18},{10... | collective-permute-start | bytes 24584 | tf_op jit(solution)/shard_map/ppermute | solution.py:472
  45.1 3.6 %collective-permute-start.5 = (f32[96,1024]{1,0:T(8,128)S(1)}, f32[96,1024]{1,0:T(8,128)S(1)}, u32[]{:S(2)}, u32[]{:S(2)}) collective-permute-start(f32[96,1024]{1,0:T(8,128)S(1)} %get-tuple-element.19), channel_id=1, source_target_pairs={{0,4},{4,8},{8,12},{12,16},{16,20},{20,24},{24,28},{1,5},{5,9},{9,... | collective-permute-start | bytes 1179656 | tf_op jit(solution)/shard_map/ppermute | solution.py:465
  47.3 4.9 %collective-permute-start.6 = (f32[96,1024]{1,0:T(8,128)S(1)}, f32[96,1024]{1,0:T(8,128)S(1)}, u32[]{:S(2)}, u32[]{:S(2)}) collective-permute-start(f32[96,1024]{1,0:T(8,128)S(1)} %get-tuple-element.20), channel_id=1, source_target_pairs={{4,0},{8,4},{12,8},{16,12},{20,16},{24,20},{28,24},{5,1},{9,5},{13... | collective-permute-start | bytes 1179656 | tf_op jit(solution)/shard_map/ppermute | solution.py:465
  52.4 5.0 %collective-permute-start.7 = (f32[176,128]{1,0:T(8,128)S(1)}, f32[176,128]{1,0:T(8,128)S(1)}, u32[]{:S(2)}, u32[]{:S(2)}) collective-permute-start(f32[176,128]{1,0:T(8,128)S(1)} %get-tuple-element.21), channel_id=1, source_target_pairs={{0,1},{1,2},{2,3},{4,5},{5,6},{6,7},{8,9},{9,10},{10,11},{12,13},{... | collective-permute-start | bytes 270344 | tf_op jit(solution)/shard_map/ppermute | solution.py:465
  55.3 6.4 %collective-permute-start.8 = (f32[176,128]{1,0:T(8,128)S(1)}, f32[176,128]{1,0:T(8,128)S(1)}, u32[]{:S(2)}, u32[]{:S(2)}) collective-permute-start(f32[176,128]{1,0:T(8,128)S(1)} %get-tuple-element.22), channel_id=1, source_target_pairs={{1,0},{2,1},{3,2},{5,4},{6,5},{7,6},{9,8},{10,9},{11,10},{13,12},{... | collective-permute-start | bytes 270344 | tf_op jit(solution)/shard_map/ppermute | solution.py:465
  56.7 5.0 %copy-start.4 = (f32[8]{0:T(128)S(1)}, f32[8]{0:T(128)}, u32[]{:S(2)}) copy-start(f32[8]{0:T(128)} %weight_ref.1) | copy-start | bytes 100
  80.9 34.7 %copy-start.2 = (f32[32,1024]{1,0:T(8,128)S(1)}, f32[32,1024]{1,0:T(8,128)}, u32[]{:S(2)}) copy-start(f32[32,1024]{1,0:T(8,128)} %param.6) | copy-start | bytes 393220
where the time goes:
time: 118 us
  blocking collectives  34.7 us (29%)
  waiting for transfers between devices  28.7 us (24%)
  Pallas kernels  25.6 us (22%)
  starting transfers between devices  23.1 us (20%)
  local copies, waits for them, and re-layouts  3.12 us (3%)
  other arithmetic  2.57 us (2%)
    all_to_all x1, blocking collectives, shards(): lax.all_to_all(returned, everyone, split_axis=0, concat_axis=0, tiled=True)  34.7 us
    pallas_call x6, Pallas kernels, kernel_call(): pl.pallas_call(body, out_shape=outs, in_specs=[pl.BlockSpec(memory_space=...  25.6 us
    all_to_all x1, waiting for transfers between devices, shards(): lax.all_to_all(packed, plane, split_axis=0, concat_axis=0, tiled=True)  9.29 us
    ppermute x4, waiting for transfers between devices, neighbours(): return (lax.ppermute(last, axis, up), lax.ppermute(first, axis, down))  8.64 us
    ppermute x4, starting transfers between devices, neighbours(): return (lax.ppermute(last, axis, up), lax.ppermute(first, axis, down))  7.71 us
    all_to_all x1, starting transfers between devices, shards(): lax.all_to_all(copies, 'deep', split_axis=0, concat_axis=0, tiled=True)  6.32 us
    ppermute x5, waiting for transfers between devices, doubled(): got = lax.ppermute(table, axis, [(i, i ^ bit) for i in range(count)])  5.65 us
    ppermute x5, starting transfers between devices, doubled(): got = lax.ppermute(table, axis, [(i, i ^ bit) for i in range(count)])  5.22 us
  transfers between devices with their start and end apart: 11, of which 8 were waited for; matrix products, arithmetic and copies ran while one was open for 3% of the time, Pallas kernels for 0%

commit v1 on v0

--- a/solution.py
+++ b/solution.py
@@ -111,8 +111,13 @@
 
 
 def pack_kernel(asked_ref, me_ref, cells_ref, *rest):
-    out_ref = rest[-1]
+    out_ref, stage_ref, sems = rest[-3:]
     peers, capacity = asked_ref.shape
+    chunk = capacity * 8
+
+    def send(i):
+        rows = pl.ds(pl.multiple_of((me_ref[0] ^ i) * chunk, chunk), chunk)
+        return pltpu.make_async_copy(stage_ref.at[rows, :], out_ref.at[rows, :], sems.at[i])
 
     @pl.loop(0, peers)
     def _(i):
@@ -120,7 +125,12 @@
         for j in range(capacity):
             asked = jnp.maximum(asked_ref[i, j], 0)
             tile = cells_ref[pl.ds(pl.multiple_of(asked * 8, 8), 8), :]
-            out_ref[pl.ds(pl.multiple_of((base + j) * 8, 8), 8), :] = tile
+            stage_ref[pl.ds(pl.multiple_of((base + j) * 8, 8), 8), :] = tile
+        send(i).start()
+
+    @pl.loop(0, peers)
+    def _(i):
+        send(i).wait()
 
 
 def step_kernel(asked_ref, me_ref, cells_ref, tiles_ref, out_ref, *totals):
@@ -148,10 +158,25 @@
         out_ref[there, :] = cells_ref[there, :] - STEP_RATE * total
 
 
-def assemble_kernel(index_ref, tiles_ref, target_ref, *rest):
-    mask_ref, first_ref, last_ref, turned_ref = rest[-4:]
+def target_strips(target_ref, top_ref, bottom_ref, strip):
+    height = target_ref.shape[0]
+    quarter = (height + 2 * HALF) // 4
+    for row in range(0, height + 2 * HALF, 16):
+        if row < HALF:
+            ref, start = top_ref, row
+        elif row < HALF + height:
+            ref, start = target_ref, row - HALF
+        else:
+            ref, start = bottom_ref, row - HALF - height
+        strip(row, ref, slice(start, start + 16), row // quarter, row % quarter)
+
+
+def assemble_kernel(index_ref, tiles_ref, target_ref, ttop_ref, tbottom_ref, *rest):
+    mask_ref, first_ref, last_ref, left_ref, right_ref, turned_ref, pack_ref = rest[-7:]
     tile_rows, tile_cols = index_ref.shape
-    height = tile_rows * TILE
+    height, breadth = target_ref.shape
+    wide = 2 * HALF
+    half = height // 2
     groups = tile_cols // 4
     block = lax.broadcasted_iota(jnp.int32, (8, LANES), 1) // 32
 
@@ -165,64 +190,44 @@
             for s, piece in enumerate(transpose_blocks(parts, block)):
                 turned_ref[pl.ds(g * height + a * TILE + s, 8, stride=4), :] = piece
 
+    lane = lax.broadcasted_iota(jnp.int32, (half, LANES), 1)
     for g in range(groups):
         lanes = slice(LANES * g, LANES * (g + 1))
         piece = turned_ref[g * height : (g + 1) * height, :]
         mask_ref[:, lanes] = piece
-        first_ref[: 2 * HALF, lanes] = piece[: 2 * HALF]
-        last_ref[: 2 * HALF, lanes] = piece[height - 2 * HALF :]
-    first_ref[2 * HALF :, :] = target_ref[:HALF, :]
-    last_ref[2 * HALF :, :] = target_ref[height - HALF :, :]
-
-
-def target_strips(target_ref, top_ref, bottom_ref, strip):
-    height = target_ref.shape[0]
+        first_ref[:, lanes] = piece[:wide]
+        last_ref[:, lanes] = piece[height - wide :]
+        upper, lower = piece[:half], piece[half:]
+        if g == 0:
+            left_ref[:half, :] = jnp.where(lane < wide, upper, pltpu.roll(lower, wide, 1))
+        if g == groups - 1:
+            right_ref[:half, :] = jnp.where(lane < wide, pltpu.roll(upper, wide, 1), lower)
+
     quarter = (height + 2 * HALF) // 4
-    for row in range(0, height + 2 * HALF, 16):
-        if row < HALF:
-            ref, start = top_ref, 2 * HALF + row
-        elif row < HALF + height:
-            ref, start = target_ref, row - HALF
-        else:
-            ref, start = bottom_ref, 2 * HALF + row - HALF - height
-        strip(row, ref, slice(start, start + 16), row // quarter, row % quarter)
-
-
-def edges_kernel(mask_ref, target_ref, top_ref, bottom_ref, first_ref, last_ref, pack_ref):
-    height, breadth = mask_ref.shape
-    wide = 2 * HALF
-    half = height // 2
-    packed = half + wide
-    lane = lax.broadcasted_iota(jnp.int32, (packed, LANES), 1)
-    head, tail = slice(0, LANES), slice(breadth - LANES, breadth)
-
-    def sides(lanes):
-        upper = jnp.concatenate([top_ref[:wide, lanes], mask_ref[:half, lanes]], axis=0)
-        lower = jnp.concatenate([mask_ref[half:, lanes], bottom_ref[:wide, lanes]], axis=0)
-        return upper, lower
-
-    upper, lower = sides(head)
-    first_ref[:packed, :] = jnp.where(lane < wide, upper, pltpu.roll(lower, wide, 1))
-    upper, lower = sides(tail)
-    last_ref[:packed, :] = jnp.where(lane < wide, pltpu.roll(upper, wide, 1), lower)
-
-    quarter = (height + 2 * HALF) // 4
 
     def strip(row, ref, rows, part, inner):
-        for side, lanes in enumerate((head, tail)):
+        for side, lanes in enumerate((slice(0, LANES), slice(breadth - LANES, breadth))):
             shift = (HALF * (part + side)) % LANES
             piece = ref[rows, lanes]
             pack_ref[side, part, inner : inner + 16, :] = (
                 pltpu.roll(piece, shift, 1) if shift else piece
             )
 
-    target_strips(target_ref, top_ref, bottom_ref, strip)
+    target_strips(target_ref, ttop_ref, tbottom_ref, strip)
     part_of = lax.broadcasted_iota(jnp.int32, (quarter, LANES), 1) // HALF
-    for side, ref in enumerate((first_ref, last_ref)):
+    for side, ref in enumerate((left_ref, right_ref)):
         piece = pack_ref[side, 0]
         for part in range(1, 4):
             piece = jnp.where(part_of == part, pack_ref[side, part], piece)
-        ref[packed:, :] = piece
+        ref[half:, :] = piece
+
+
+def corners_kernel(before_ref, after_ref, first_ref, last_ref):
+    wide = 2 * HALF
+    lane = lax.broadcasted_iota(jnp.int32, (wide, LANES), 1)
+    before, after = before_ref[:wide, :], after_ref[:wide, :]
+    first_ref[...] = jnp.where(lane < wide, before, pltpu.roll(after, wide, 1))
+    last_ref[...] = jnp.where(lane < wide, pltpu.roll(before, wide, 1), after)
 
 
 def image_kernel(
@@ -234,7 +239,11 @@
     bottom_ref,
     before_ref,
     after_ref,
+    ctop_ref,
+    cbottom_ref,
     own_ref,
+    ttop_ref,
+    tbottom_ref,
     wave_ref,
     out_ref,
     fcol_ref,
@@ -268,14 +277,15 @@
             ref, start = bottom_ref, 0
         else:
             ref, start = mask_ref, rows - wide
-        half = high_rows // 2
-        edge = slice(rows % half, rows % half + wide)
-        turned = before_ref[edge, :]
-        final = after_ref[edge, :]
-        if rows < half:
-            final = pltpu.roll(final, wide, 1)
+        if rows == 0 or rows == high_rows - wide:
+            corner = ctop_ref if rows == 0 else cbottom_ref
+            turned = final = corner[...]
         else:
-            turned = pltpu.roll(turned, wide, 1)
+            turned, final = before_ref[:wide, :], after_ref[:wide, :]
+            if rows == wide:
+                final = pltpu.roll(final, wide, 1)
+            else:
+                turned = pltpu.roll(turned, wide, 1)
         for g in range(groups + 1):
             fresh = final
             if g < groups:
@@ -288,7 +298,7 @@
             mhigh_ref[rows : rows + wide, LANES * g : LANES * (g + 1)] = high
             mlow_ref[rows : rows + wide, LANES * g : LANES * (g + 1)] = low
             turned = fresh
-    packed = high_rows // 2
+    packed = rows_here // 2
     near_lane = lax.broadcasted_iota(jnp.int32, (16, LANES), 1)
 
     def strip(row, ref, rows, part, inner):
@@ -305,7 +315,7 @@
             )
             turned = fresh
 
-    target_strips(own_ref, top_ref, bottom_ref, strip)
+    target_strips(own_ref, ttop_ref, tbottom_ref, strip)
 
     def swapped(x):
         pieces = [
@@ -440,7 +450,7 @@
     return x.reshape(count // 8, 8, 8, LANES).transpose(0, 2, 1, 3).reshape(count, 8 * LANES)
 
 
-def kernel_call(body, name, shapes, scratch, scalars, inputs, unread=(), megabytes=8):
+def kernel_call(body, name, shapes, scratch, scalars, inputs, unread=(), megabytes=8, out_space=pltpu.VMEM):
     single = not isinstance(shapes, list)
     spec = pl.BlockSpec(memory_space=pltpu.VMEM)
     outs = [shapes] if single else shapes
@@ -450,7 +460,7 @@
         in_specs=[pl.BlockSpec(memory_space=pltpu.SMEM)] * len(scalars)
         + [spec] * len(inputs)
         + [pl.BlockSpec(memory_space=pl.ANY)] * len(unread),
-        out_specs=[spec] * len(outs),
+        out_specs=[pl.BlockSpec(memory_space=out_space)] * len(outs),
         scratch_shapes=scratch,
         compiler_params=pltpu.CompilerParams(vmem_limit_bytes=megabytes * 2**20),
         name=name,
@@ -520,12 +530,20 @@
         pack_kernel,
         "pack",
         f32(peers * wide_capacity * 8, LANES),
-        [],
+        [
+            pltpu.VMEM((peers * wide_capacity * 8, LANES), F32),
+            pltpu.SemaphoreType.DMA((peers,)),
+        ],
         [asked, me],
         [stack],
         [waves],
-    )
-    packed, near = lax.optimization_barrier((packed, near))
+        out_space=pl.ANY,
+    )
+    packed, near, above, below = lax.optimization_barrier(
+        (packed, near, target[:HALF], target[height - HALF :])
+    )
+    row_axes = ("deep", "core")
+    above, below = neighbours(above, below, row_axes)
     arrived = lax.all_to_all(packed, plane, split_axis=0, concat_axis=0, tiled=True)
 
     everything = doubled(near, "deep")
@@ -538,27 +556,26 @@
         where = group * size + jnp.sum(same.astype(jnp.int32), axis=1)
         return where.reshape(tile_rows, tile_cols)
 
-    mask, first, last = kernel_call(
+    wide = 2 * HALF
+    quarter = (height + wide) // 4
+    edge = f32(height // 2 + quarter, LANES)
+    mask, first, last, left, right = kernel_call(
         assemble_kernel,
         "assemble",
-        [f32(height, breadth), f32(3 * HALF, breadth), f32(3 * HALF, breadth)],
-        [pltpu.VMEM((height * (breadth // LANES), LANES), F32)],
+        [f32(height, breadth), f32(wide, breadth), f32(wide, breadth), edge, edge],
+        [
+            pltpu.VMEM((height * (breadth // LANES), LANES), F32),
+            pltpu.VMEM((2, 4, quarter, LANES), F32),
+        ],
         [place(mine % peers, wide_capacity)],
-        [arrived, target],
+        [arrived, target, above, below],
         [wanted],
     )
-    top, bottom = neighbours(first, last, ("deep", "core"))
-    quarter = (height + 2 * HALF) // 4
-    edge = f32(height // 2 + 2 * HALF + quarter, LANES)
-    first, last = kernel_call(
-        edges_kernel,
-        "edges",
-        [edge, edge],
-        [pltpu.VMEM((2, 4, quarter, LANES), F32)],
-        [],
-        [mask, target, top, bottom],
-    )
-    before, after = neighbours(first, last, "col")
+    before, after = neighbours(left, right, "col")
+    top, bottom = neighbours(first, last, row_axes)
+    corner = f32(wide, LANES)
+    first, last = kernel_call(corners_kernel, "corners", [corner, corner], [], [], [before, after])
+    corner_top, corner_bottom = neighbours(first, last, row_axes)
     my_row = lax.axis_index(("deep", "core"))
     my_col = lax.axis_index("col")
     where = jnp.stack(
@@ -590,7 +607,8 @@
             pltpu.VMEM((height * (breadth // LANES), LANES), F32),
         ],
         [place(mine, capacity), where, kernel_weight],
-        [mask, top, bottom, before, after, target, waves],
+        [mask, top, bottom, before, after, corner_top, corner_bottom]
+        + [target, above, below, waves],
         megabytes=36,
     )
     back = lax.all_to_all(returned, everyone, split_axis=0, concat_axis=0, tiled=True)

time: 118 us -> 120 us (1.017)
  starting transfers between devices: 23.1 us -> 32.9 us
  waiting for transfers between devices: 28.7 us -> 23.6 us
  blocking collectives: 34.7 us -> 31.2 us
    ppermute x4 -> x8, starting transfers between devices: 7.71 us -> 15.6 us  [neighbours(): return (lax.ppermute(last, axis, up), lax.ppermute(first, axis, down))]
    all_to_all x1, waiting for transfers between devices: 9.29 us -> 3.16 us  [shards(): lax.all_to_all(packed, plane, split_axis=0, concat_axis=0, tiled=True)]
    all_to_all x1, blocking collectives: 34.7 us -> 31.2 us  [shards(): lax.all_to_all(returned, everyone, split_axis=0, concat_axis=0, tiled=True)]
    ppermute x5, starting transfers between devices: 5.22 us -> 7.12 us  [doubled(): got = lax.ppermute(table, axis, [(i, i ^ bit) for i in range(count)])]
    ppermute x4 -> x8, waiting for transfers between devices: 8.64 us -> 9.16 us  [neighbours(): return (lax.ppermute(last, axis, up), lax.ppermute(first, axis, down))]
  transfers between devices with their start and end apart: 11 -> 15, of which waited for: 8 -> 8; matrix products, arithmetic and copies ran while one was open for 3% -> 3% of each run, Pallas kernels for 0% -> 0%
where the time goes in v1:
time: 120 us
  starting transfers between devices  32.9 us (27%)
  blocking collectives  31.2 us (26%)
  Pallas kernels  25.3 us (21%)
  waiting for transfers between devices  23.6 us (20%)
  local copies, waits for them, and re-layouts  3.8 us (3%)
  other arithmetic  2.57 us (2%)
    all_to_all x1, blocking collectives, shards(): lax.all_to_all(returned, everyone, split_axis=0, concat_axis=0, tiled=True)  31.2 us
    pallas_call x6, Pallas kernels, kernel_call(): pl.pallas_call(body, out_shape=outs, in_specs=[pl.BlockSpec(memory_space=...  25.3 us
    ppermute x8, starting transfers between devices, neighbours(): return (lax.ppermute(last, axis, up), lax.ppermute(first, axis, down))  15.6 us
    ppermute x8, waiting for transfers between devices, neighbours(): return (lax.ppermute(last, axis, up), lax.ppermute(first, axis, down))  9.16 us
    ppermute x5, starting transfers between devices, doubled(): got = lax.ppermute(table, axis, [(i, i ^ bit) for i in range(count)])  7.12 us
    all_to_all x1, starting transfers between devices, shards(): lax.all_to_all(copies, 'deep', split_axis=0, concat_axis=0, tiled=True)  6.45 us
    ppermute x5, waiting for transfers between devices, doubled(): got = lax.ppermute(table, axis, [(i, i ^ bit) for i in range(count)])  6.2 us
    all_to_all x1, waiting for transfers between devices, shards(): lax.all_to_all(copies, 'deep', split_axis=0, concat_axis=0, tiled=True)  5.09 us
  transfers between devices with their start and end apart: 15, of which 8 were waited for; matrix products, arithmetic and copies ran while one was open for 3% of the time, Pallas kernels for 0%

profile of v1, /device:TPU:0, one launch (start us, length us, event | category | flops | bytes accessed | tf_op | source)
XLA Modules:
  0.0 119.7 jit_solution(11836868583257308605)
XLA Ops:
  0.0 0.9 copy-done.1
  0.9 0.7 copy-done.3
  1.6 0.8 spread.1
  2.4 6.4 %all-to-all-start = ((f32[4,256,128]{2,1,0:T(8,128)}), f32[4,256,128]{2,1,0:T(8,128)S(1)}, u32[]{:S(2)}, u32[]{:S(2)}) async-start(f32[4,256,128]{2,1,0:T(8,128)} %bitcast.5), calls=%async_computation | async-start | bytes 1048576 | tf_op jit(solution)/shard_map/all_to_all | solution.py:520
  8.9 1.5 %collective-permute-start = (s32[1,128]{1,0:T(1,128)S(1)}, s32[1,128]{1,0:T(1,128)S(1)}, u32[]{:S(2)}, u32[]{:S(2)}) collective-permute-start(s32[1,128]{1,0:T(1,128)S(1)} %get-tuple-element.18), channel_id=1, source_target_pairs={{0,1},{1,0},{2,3},{3,2},{4,5},{5,4},{6,7},{7,6},{8,9},{9,8},{10,11... | collective-permute-start | bytes 1544 | tf_op jit(solution)/shard_map/ppermute | solution.py:482
  10.9 0.7 fusion.19
  12.1 0.7 copy-done.5
  12.8 1.6 %collective-permute-start.1 = (s32[2,128]{1,0:T(2,128)S(1)}, s32[2,128]{1,0:T(2,128)S(1)}, u32[]{:S(2)}, u32[]{:S(2)}) collective-permute-start(s32[2,128]{1,0:T(2,128)S(1)} %pad_add_fusion.3), channel_id=1, source_target_pairs={{0,2},{1,3},{2,0},{3,1},{4,6},{5,7},{6,4},{7,5},{8,10},{9,11},{10,... | collective-permute-start | bytes 3080 | tf_op jit(solution)/shard_map/ppermute | solution.py:482
  14.4 2.0 %collective-permute-done.1 = s32[2,128]{1,0:T(2,128)S(1)} collective-permute-done((s32[2,128]{1,0:T(2,128)S(1)}, s32[2,128]{1,0:T(2,128)S(1)}, u32[]{:S(2)}, u32[]{:S(2)}) %collective-permute-start.1) | collective-permute-done | bytes 1056 | tf_op jit(solution)/shard_map/ppermute | solution.py:482
  16.6 1.1 collective-permute-done.2
  18.3 5.1 %all-to-all-done = f32[4,256,128]{2,1,0:T(8,128)S(1)} async-done(((f32[4,256,128]{2,1,0:T(8,128)}), f32[4,256,128]{2,1,0:T(8,128)S(1)}, u32[]{:S(2)}, u32[]{:S(2)}) %all-to-all-start) | async-done | bytes 524320 | tf_op jit(solution)/shard_map/all_to_all | solution.py:520
  23.4 1.8 %pack.1 = f32[2048,128]{1,0:T(8,128)} custom-call(s32[8,32]{1,0:T(8,128)S(1)} %select_reduce_fusion.1.asked_ref, s32[2]{0:T(128)S(1)} %pad_add_fusion.4.me_ref, f32[1024,128]{1,0:T(8,128)S(1)} %bitcast.35, f32[32,128]{1,0:T(8,128)S(1)} %select_maximum_fusion.rest_0_.wave_ref), custom_call_target="tpu_custom_call" | custom-call | tf_op jit(solution)/shard_map/pack/pallas_call | solution.py:457
  25.2 3.7 %all-to-all-start.1 = ((f32[8,256,128]{2,1,0:T(8,128)}), f32[8,256,128]{2,1,0:T(8,128)S(1)}, u32[]{:S(2)}, u32[]{:S(2)}) async-start(f32[8,256,128]{2,1,0:T(8,128)} %bitcast.12), calls=%async_computation.1 | async-start | bytes 2097152 | tf_op jit(solution)/shard_map/all_to_all | solution.py:547
  29.0 2.4 %collective-permute-start.5 = (f32[32,1024]{1,0:T(8,128)S(1)}, f32[32,1024]{1,0:T(8,128)S(1)}, u32[]{:S(2)}, u32[]{:S(2)}) collective-permute-start(f32[32,1024]{1,0:T(8,128)S(1)} %get-tuple-element.22), channel_id=1, source_target_pairs={{0,4},{4,8},{8,12},{12,16},{16,20},{20,24},{24,28},{1,5},{5,9},{9,... | collective-permute-start | bytes 393224 | tf_op jit(solution)/shard_map/ppermute | solution.py:475
  31.4 1.3 %collective-permute-start.6 = (f32[32,1024]{1,0:T(8,128)S(1)}, f32[32,1024]{1,0:T(8,128)S(1)}, u32[]{:S(2)}, u32[]{:S(2)}) collective-permute-start(f32[32,1024]{1,0:T(8,128)S(1)} %get-tuple-element.23), channel_id=1, source_target_pairs={{4,0},{8,4},{12,8},{16,12},{20,16},{24,20},{28,24},{5,1},{9,5},{13... | collective-permute-start | bytes 393224 | tf_op jit(solution)/shard_map/ppermute | solution.py:475
  32.7 3.9 %collective-permute-start.4 = (s32[16,128]{1,0:T(8,128)S(1)}, s32[16,128]{1,0:T(8,128)S(1)}, u32[]{:S(2)}, u32[]{:S(2)}) collective-permute-start(s32[16,128]{1,0:T(8,128)S(1)} %pad_add_fusion), channel_id=1, source_target_pairs={{0,16},{8,24},{16,0},{24,8},{1,17},{9,25},{17,1},{25,9},{2,18},{10... | collective-permute-start | bytes 24584 | tf_op jit(solution)/shard_map/ppermute | solution.py:482
  36.6 3.1 %collective-permute-done.4 = s32[16,128]{1,0:T(8,128)S(1)} collective-permute-done((s32[16,128]{1,0:T(8,128)S(1)}, s32[16,128]{1,0:T(8,128)S(1)}, u32[]{:S(2)}, u32[]{:S(2)}) %collective-permute-start.4) | collective-permute-done | bytes 8224 | tf_op jit(solution)/shard_map/ppermute | solution.py:482
  40.1 0.6 select_reduce_fusion.rest_0_.asked_ref
  40.7 3.2 %all-to-all-done.1 = f32[8,256,128]{2,1,0:T(8,128)S(1)} async-done(((f32[8,256,128]{2,1,0:T(8,128)}), f32[8,256,128]{2,1,0:T(8,128)S(1)}, u32[]{:S(2)}, u32[]{:S(2)}) %all-to-all-start.1) | async-done | bytes 1048608 | tf_op jit(solution)/shard_map/all_to_all | solution.py:547
  43.9 1.1 assemble.1
  45.0 2.2 %collective-permute-start.7 = (f32[64,1024]{1,0:T(8,128)S(1)}, f32[64,1024]{1,0:T(8,128)S(1)}, u32[]{:S(2)}, u32[]{:S(2)}) collective-permute-start(f32[64,1024]{1,0:T(8,128)S(1)} %get-tuple-element.25), channel_id=1, source_target_pairs={{0,4},{4,8},{8,12},{12,16},{16,20},{20,24},{24,28},{1,5},{5,9},{9,... | collective-permute-start | bytes 786440 | tf_op jit(solution)/shard_map/ppermute | solution.py:475
  47.2 1.3 %collective-permute-start.8 = (f32[64,1024]{1,0:T(8,128)S(1)}, f32[64,1024]{1,0:T(8,128)S(1)}, u32[]{:S(2)}, u32[]{:S(2)}) collective-permute-start(f32[64,1024]{1,0:T(8,128)S(1)} %get-tuple-element.26), channel_id=1, source_target_pairs={{4,0},{8,4},{12,8},{16,12},{20,16},{24,20},{28,24},{5,1},{9,5},{13... | collective-permute-start | bytes 786440 | tf_op jit(solution)/shard_map/ppermute | solution.py:475
  48.5 2.7 %collective-permute-start.9 = (f32[112,128]{1,0:T(8,128)S(1)}, f32[112,128]{1,0:T(8,128)S(1)}, u32[]{:S(2)}, u32[]{:S(2)}) collective-permute-start(f32[112,128]{1,0:T(8,128)S(1)} %get-tuple-element.27), channel_id=1, source_target_pairs={{0,1},{1,2},{2,3},{4,5},{5,6},{6,7},{8,9},{9,10},{10,11},{12,13},{... | collective-permute-start | bytes 172040 | tf_op jit(solution)/shard_map/ppermute | solution.py:475
  51.2 1.3 %collective-permute-start.10 = (f32[112,128]{1,0:T(8,128)S(1)}, f32[112,128]{1,0:T(8,128)S(1)}, u32[]{:S(2)}, u32[]{:S(2)}) collective-permute-start(f32[112,128]{1,0:T(8,128)S(1)} %get-tuple-element.28), channel_id=1, source_target_pairs={{1,0},{2,1},{3,2},{5,4},{6,5},{7,6},{9,8},{10,9},{11,10},{13,12},{... | collective-permute-start | bytes 172040 | tf_op jit(solution)/shard_map/ppermute | solution.py:475
  53.0 4.3 %collective-permute-done.10.after_ref = f32[112,128]{1,0:T(8,128)S(1)} collective-permute-done((f32[112,128]{1,0:T(8,128)S(1)}, f32[112,128]{1,0:T(8,128)S(1)}, u32[]{:S(2)}, u32[]{:S(2)}) %collective-permute-start.10) | collective-permute-done | bytes 57376 | tf_op jit(solution)/shard_map/ppermute | solution.py:475
  57.4 3.1 %collective-permute-start.11 = (f32[64,128]{1,0:T(8,128)S(1)}, f32[64,128]{1,0:T(8,128)S(1)}, u32[]{:S(2)}, u32[]{:S(2)}) collective-permute-start(f32[64,128]{1,0:T(8,128)S(1)} %get-tuple-element.29), channel_id=1, source_target_pairs={{0,4},{4,8},{8,12},{12,16},{16,20},{20,24},{24,28},{1,5},{5,9},{9,... | collective-permute-start | bytes 98312 | tf_op jit(solution)/shard_map/ppermute | solution.py:475
  60.5 1.3 %collective-permute-start.12 = (f32[64,128]{1,0:T(8,128)S(1)}, f32[64,128]{1,0:T(8,128)S(1)}, u32[]{:S(2)}, u32[]{:S(2)}) collective-permute-start(f32[64,128]{1,0:T(8,128)S(1)} %get-tuple-element.30), channel_id=1, source_target_pairs={{4,0},{8,4},{12,8},{16,12},{20,16},{24,20},{28,24},{5,1},{9,5},{13... | collective-permute-start | bytes 98312 | tf_op jit(solution)/shard_map/ppermute | solution.py:475
  61.9 4.4 %collective-permute-done.12.cbottom_ref = f32[64,128]{1,0:T(8,128)S(1)} collective-permute-done((f32[64,128]{1,0:T(8,128)S(1)}, f32[64,128]{1,0:T(8,128)S(1)}, u32[]{:S(2)}, u32[]{:S(2)}) %collective-permute-start.12) | collective-permute-done | bytes 32800 | tf_op jit(solution)/shard_map/ppermute | solution.py:475
  66.3 0.7 copy-done.4
  66.9 19.1 %image.1 = f32[2048,128]{1,0:T(8,128)S(1)} custom-call(s32[4,32]{1,0:T(4,128)S(1)} %get-tuple-element.46.index_ref, s32[4]{0:T(128)S(1)} %pad_add_fusion.5.where_ref, f32[8]{0:T(128)S(1)} %copy-done.4, f32[128,1024]{1,0:T(8,128)S(1)} %get-tuple-element.24.mask_ref, f32[64,1024]{1,0:T(8,128)S(1)} %collective-permute-done.7.top_ref, ...), custom_call_target="tpu_custom_call" | custom-call | tf_op jit(solution)/shard_map/image/pallas_call | solution.py:457
  86.1 31.2 %all_to_all.33 = f32[32,64,128]{2,1,0:T(8,128)S(1)} all-to-all(f32[32,64,128]{2,1,0:T(8,128)S(1)} %bitcast.32), channel_id=1, replica_groups=mesh['deep'=4,'core'=2,'col'=4] {'deep','core','col'}, dimensions={0} | all-to-all | bytes 2097152 | tf_op jit(solution)/shard_map/all_to_all | solution.py:614
  117.3 2.4 %step.1 = f32[256,128]{1,0:T(8,128)} custom-call(s32[32,8]{1,0:T(8,128)S(1)} %select_reduce_fusion.rest_0_.asked_ref, s32[2]{0:T(128)S(1)} %pad_add_fusion.4.me_ref, f32[256,128]{1,0:T(8,128)S(1)} %bitcast.37, f32[2048,128]{1,0:T(8,128)S(1)} %bitcast.34), custom_call_target="tpu_custom_call" | custom-call | tf_op jit(solution)/shard_map/step/pallas_call | solution.py:457
  (49 shorter events, 2.9 us)
Async XLA Ops:
  0.0 0.9 copy-start.1
  0.9 0.7 copy-start.3
  2.4 8.0 %copy-start = (f32[128,1024]{1,0:T(8,128)S(1)}, f32[128,1024]{1,0:T(8,128)}, u32[]{:S(2)}) copy-start(f32[128,1024]{1,0:T(8,128)} %own_ref.1) | copy-start | bytes 1572868
  2.4 20.9 %all-to-all-start = ((f32[4,256,128]{2,1,0:T(8,128)}), f32[4,256,128]{2,1,0:T(8,128)S(1)}, u32[]{:S(2)}, u32[]{:S(2)}) async-start(f32[4,256,128]{2,1,0:T(8,128)} %bitcast.5), calls=%async_computation | async-start | bytes 1048576 | tf_op jit(solution)/shard_map/all_to_all | solution.py:520
  8.9 4.0 %collective-permute-start = (s32[1,128]{1,0:T(1,128)S(1)}, s32[1,128]{1,0:T(1,128)S(1)}, u32[]{:S(2)}, u32[]{:S(2)}) collective-permute-start(s32[1,128]{1,0:T(1,128)S(1)} %get-tuple-element.18), channel_id=1, source_target_pairs={{0,1},{1,0},{2,3},{3,2},{4,5},{5,4},{6,7},{7,6},{8,9},{9,8},{10,11... | collective-permute-start | bytes 1544 | tf_op jit(solution)/shard_map/ppermute | solution.py:482
  12.0 0.7 copy-start.5
  12.0 0.7 copy-start.6
  12.8 3.6 %collective-permute-start.1 = (s32[2,128]{1,0:T(2,128)S(1)}, s32[2,128]{1,0:T(2,128)S(1)}, u32[]{:S(2)}, u32[]{:S(2)}) collective-permute-start(s32[2,128]{1,0:T(2,128)S(1)} %pad_add_fusion.3), channel_id=1, source_target_pairs={{0,2},{1,3},{2,0},{3,1},{4,6},{5,7},{6,4},{7,5},{8,10},{9,11},{10,... | collective-permute-start | bytes 3080 | tf_op jit(solution)/shard_map/ppermute | solution.py:482
  16.5 1.2 %collective-permute-start.2 = (s32[4,128]{1,0:T(4,128)S(1)}, s32[4,128]{1,0:T(4,128)S(1)}, u32[]{:S(2)}, u32[]{:S(2)}) collective-permute-start(s32[4,128]{1,0:T(4,128)S(1)} %pad_add_fusion.2), channel_id=1, source_target_pairs={{0,4},{4,0},{1,5},{5,1},{2,6},{6,2},{3,7},{7,3},{8,12},{12,8},{9,1... | collective-permute-start | bytes 6152 | tf_op jit(solution)/shard_map/ppermute | solution.py:482
  25.2 7.5 %collective-permute-start.3 = (s32[8,128]{1,0:T(8,128)S(1)}, s32[8,128]{1,0:T(8,128)S(1)}, u32[]{:S(2)}, u32[]{:S(2)}) collective-permute-start(s32[8,128]{1,0:T(8,128)S(1)} %get-tuple-element.20), channel_id=1, source_target_pairs={{0,8},{8,0},{16,24},{24,16},{1,9},{9,1},{17,25},{25,17},{2,10},{10... | collective-permute-start | bytes 12296 | tf_op jit(solution)/shard_map/ppermute | solution.py:482
  25.2 18.6 %all-to-all-start.1 = ((f32[8,256,128]{2,1,0:T(8,128)}), f32[8,256,128]{2,1,0:T(8,128)S(1)}, u32[]{:S(2)}, u32[]{:S(2)}) async-start(f32[8,256,128]{2,1,0:T(8,128)} %bitcast.12), calls=%async_computation.1 | async-start | bytes 2097152 | tf_op jit(solution)/shard_map/all_to_all | solution.py:547
  29.0 11.7 %collective-permute-start.5 = (f32[32,1024]{1,0:T(8,128)S(1)}, f32[32,1024]{1,0:T(8,128)S(1)}, u32[]{:S(2)}, u32[]{:S(2)}) collective-permute-start(f32[32,1024]{1,0:T(8,128)S(1)} %get-tuple-element.22), channel_id=1, source_target_pairs={{0,4},{4,8},{8,12},{12,16},{16,20},{20,24},{24,28},{1,5},{5,9},{9,... | collective-permute-start | bytes 393224 | tf_op jit(solution)/shard_map/ppermute | solution.py:475
  31.4 9.3 %collective-permute-start.6 = (f32[32,1024]{1,0:T(8,128)S(1)}, f32[32,1024]{1,0:T(8,128)S(1)}, u32[]{:S(2)}, u32[]{:S(2)}) collective-permute-start(f32[32,1024]{1,0:T(8,128)S(1)} %get-tuple-element.23), channel_id=1, source_target_pairs={{4,0},{8,4},{12,8},{16,12},{20,16},{24,20},{28,24},{5,1},{9,5},{13... | collective-permute-start | bytes 393224 | tf_op jit(solution)/shard_map/ppermute | solution.py:475
  32.7 7.0 %collective-permute-start.4 = (s32[16,128]{1,0:T(8,128)S(1)}, s32[16,128]{1,0:T(8,128)S(1)}, u32[]{:S(2)}, u32[]{:S(2)}) collective-permute-start(s32[16,128]{1,0:T(8,128)S(1)} %pad_add_fusion), channel_id=1, source_target_pairs={{0,16},{8,24},{16,0},{24,8},{1,17},{9,25},{17,1},{25,9},{2,18},{10... | collective-permute-start | bytes 24584 | tf_op jit(solution)/shard_map/ppermute | solution.py:482
  45.0 21.3 %collective-permute-start.7 = (f32[64,1024]{1,0:T(8,128)S(1)}, f32[64,1024]{1,0:T(8,128)S(1)}, u32[]{:S(2)}, u32[]{:S(2)}) collective-permute-start(f32[64,1024]{1,0:T(8,128)S(1)} %get-tuple-element.25), channel_id=1, source_target_pairs={{0,4},{4,8},{8,12},{12,16},{16,20},{20,24},{24,28},{1,5},{5,9},{9,... | collective-permute-start | bytes 786440 | tf_op jit(solution)/shard_map/ppermute | solution.py:475
  47.2 19.0 %collective-permute-start.8 = (f32[64,1024]{1,0:T(8,128)S(1)}, f32[64,1024]{1,0:T(8,128)S(1)}, u32[]{:S(2)}, u32[]{:S(2)}) collective-permute-start(f32[64,1024]{1,0:T(8,128)S(1)} %get-tuple-element.26), channel_id=1, source_target_pairs={{4,0},{8,4},{12,8},{16,12},{20,16},{24,20},{28,24},{5,1},{9,5},{13... | collective-permute-start | bytes 786440 | tf_op jit(solution)/shard_map/ppermute | solution.py:475
  48.5 4.5 %collective-permute-start.9 = (f32[112,128]{1,0:T(8,128)S(1)}, f32[112,128]{1,0:T(8,128)S(1)}, u32[]{:S(2)}, u32[]{:S(2)}) collective-permute-start(f32[112,128]{1,0:T(8,128)S(1)} %get-tuple-element.27), channel_id=1, source_target_pairs={{0,1},{1,2},{2,3},{4,5},{5,6},{6,7},{8,9},{9,10},{10,11},{12,13},{... | collective-permute-start | bytes 172040 | tf_op jit(solution)/shard_map/ppermute | solution.py:475
  51.2 6.1 %collective-permute-start.10 = (f32[112,128]{1,0:T(8,128)S(1)}, f32[112,128]{1,0:T(8,128)S(1)}, u32[]{:S(2)}, u32[]{:S(2)}) collective-permute-start(f32[112,128]{1,0:T(8,128)S(1)} %get-tuple-element.28), channel_id=1, source_target_pairs={{1,0},{2,1},{3,2},{5,4},{6,5},{7,6},{9,8},{10,9},{11,10},{13,12},{... | collective-permute-start | bytes 172040 | tf_op jit(solution)/shard_map/ppermute | solution.py:475
  57.4 4.5 %collective-permute-start.11 = (f32[64,128]{1,0:T(8,128)S(1)}, f32[64,128]{1,0:T(8,128)S(1)}, u32[]{:S(2)}, u32[]{:S(2)}) collective-permute-start(f32[64,128]{1,0:T(8,128)S(1)} %get-tuple-element.29), channel_id=1, source_target_pairs={{0,4},{4,8},{8,12},{12,16},{16,20},{20,24},{24,28},{1,5},{5,9},{9,... | collective-permute-start | bytes 98312 | tf_op jit(solution)/shard_map/ppermute | solution.py:475
  60.5 5.8 %collective-permute-start.12 = (f32[64,128]{1,0:T(8,128)S(1)}, f32[64,128]{1,0:T(8,128)S(1)}, u32[]{:S(2)}, u32[]{:S(2)}) collective-permute-start(f32[64,128]{1,0:T(8,128)S(1)} %get-tuple-element.30), channel_id=1, source_target_pairs={{4,0},{8,4},{12,8},{16,12},{20,16},{24,20},{28,24},{5,1},{9,5},{13... | collective-permute-start | bytes 98312 | tf_op jit(solution)/shard_map/ppermute | solution.py:475
  66.3 0.7 copy-start.4
  86.1 31.3 %copy-start.2 = (f32[32,1024]{1,0:T(8,128)S(1)}, f32[32,1024]{1,0:T(8,128)}, u32[]{:S(2)}) copy-start(f32[32,1024]{1,0:T(8,128)} %param.6) | copy-start | bytes 393220

commit v2 on v1

--- a/solution.py
+++ b/solution.py
@@ -171,8 +171,9 @@
         strip(row, ref, slice(start, start + 16), row // quarter, row % quarter)
 
 
-def assemble_kernel(index_ref, tiles_ref, target_ref, ttop_ref, tbottom_ref, *rest):
-    mask_ref, first_ref, last_ref, left_ref, right_ref, turned_ref, pack_ref = rest[-7:]
+def assemble_kernel(index_ref, spot_ref, tiles_ref, target_ref, ttop_ref, tbottom_ref, *rest):
+    mask_ref, rowa_ref, rowb_ref, cola_ref, colb_ref, turned_ref, pack_ref = rest[-7:]
+    odd_row, odd_col = spot_ref[6] > 0, spot_ref[7] > 0
     tile_rows, tile_cols = index_ref.shape
     height, breadth = target_ref.shape
     wide = 2 * HALF
@@ -195,13 +196,15 @@
         lanes = slice(LANES * g, LANES * (g + 1))
         piece = turned_ref[g * height : (g + 1) * height, :]
         mask_ref[:, lanes] = piece
-        first_ref[:, lanes] = piece[:wide]
-        last_ref[:, lanes] = piece[height - wide :]
+        rowa_ref[:, lanes] = jnp.where(odd_row, piece[:wide], piece[height - wide :])
+        rowb_ref[:, lanes] = jnp.where(odd_row, piece[height - wide :], piece[:wide])
         upper, lower = piece[:half], piece[half:]
         if g == 0:
-            left_ref[:half, :] = jnp.where(lane < wide, upper, pltpu.roll(lower, wide, 1))
+            left = jnp.where(lane < wide, upper, pltpu.roll(lower, wide, 1))
         if g == groups - 1:
-            right_ref[:half, :] = jnp.where(lane < wide, pltpu.roll(upper, wide, 1), lower)
+            right = jnp.where(lane < wide, pltpu.roll(upper, wide, 1), lower)
+    cola_ref[:half, :] = jnp.where(odd_col, left, right)
+    colb_ref[:half, :] = jnp.where(odd_col, right, left)
 
     quarter = (height + 2 * HALF) // 4
 
@@ -215,32 +218,39 @@
 
     target_strips(target_ref, ttop_ref, tbottom_ref, strip)
     part_of = lax.broadcasted_iota(jnp.int32, (quarter, LANES), 1) // HALF
-    for side, ref in enumerate((left_ref, right_ref)):
+    sides = []
+    for side in range(2):
         piece = pack_ref[side, 0]
         for part in range(1, 4):
             piece = jnp.where(part_of == part, pack_ref[side, part], piece)
-        ref[half:, :] = piece
-
-
-def corners_kernel(before_ref, after_ref, first_ref, last_ref):
+        sides.append(piece)
+    cola_ref[half:, :] = jnp.where(odd_col, sides[0], sides[1])
+    colb_ref[half:, :] = jnp.where(odd_col, sides[1], sides[0])
+
+
+def corners_kernel(spot_ref, cola_ref, colb_ref, rowa_ref, rowb_ref):
+    odd_row, odd_col = spot_ref[6] > 0, spot_ref[7] > 0
     wide = 2 * HALF
     lane = lax.broadcasted_iota(jnp.int32, (wide, LANES), 1)
-    before, after = before_ref[:wide, :], after_ref[:wide, :]
-    first_ref[...] = jnp.where(lane < wide, before, pltpu.roll(after, wide, 1))
-    last_ref[...] = jnp.where(lane < wide, pltpu.roll(before, wide, 1), after)
+    one, other = cola_ref[:wide, :], colb_ref[:wide, :]
+    before, after = jnp.where(odd_col, one, other), jnp.where(odd_col, other, one)
+    first = jnp.where(lane < wide, before, pltpu.roll(after, wide, 1))
+    last = jnp.where(lane < wide, pltpu.roll(before, wide, 1), after)
+    rowa_ref[...] = jnp.where(odd_row, first, last)
+    rowb_ref[...] = jnp.where(odd_row, last, first)
 
 
 def image_kernel(
     index_ref,
-    where_ref,
+    spot_ref,
     weight_ref,
     mask_ref,
-    top_ref,
-    bottom_ref,
-    before_ref,
-    after_ref,
-    ctop_ref,
-    cbottom_ref,
+    rowa_ref,
+    rowb_ref,
+    cola_ref,
+    colb_ref,
+    cornera_ref,
+    cornerb_ref,
     own_ref,
     ttop_ref,
     tbottom_ref,
@@ -267,21 +277,18 @@
     groups = tile_cols // 4
     wide = 2 * HALF
     block = lax.broadcasted_iota(jnp.int32, (8, LANES), 1) // 32
+    odd_row, odd_col = spot_ref[6] > 0, spot_ref[7] > 0
     build_bands(wave_ref, fcol_ref, frow_ref, brow_ref, bcol_ref)
 
     lane = lax.broadcasted_iota(jnp.int32, (wide, LANES), 1)
     for rows in range(0, high_rows, wide):
-        if rows == 0:
-            ref, start = top_ref, 0
-        elif rows == high_rows - wide:
-            ref, start = bottom_ref, 0
+        outer = rows == 0 or rows == high_rows - wide
+        from_a = odd_row if rows == 0 else jnp.logical_not(odd_row)
+        if outer:
+            turned = final = jnp.where(from_a, cornera_ref[...], cornerb_ref[...])
         else:
-            ref, start = mask_ref, rows - wide
-        if rows == 0 or rows == high_rows - wide:
-            corner = ctop_ref if rows == 0 else cbottom_ref
-            turned = final = corner[...]
-        else:
-            turned, final = before_ref[:wide, :], after_ref[:wide, :]
+            one, other = cola_ref[:wide, :], colb_ref[:wide, :]
+            turned, final = jnp.where(odd_col, one, other), jnp.where(odd_col, other, one)
             if rows == wide:
                 final = pltpu.roll(final, wide, 1)
             else:
@@ -289,7 +296,11 @@
         for g in range(groups + 1):
             fresh = final
             if g < groups:
-                piece = ref[start : start + wide, LANES * g : LANES * (g + 1)]
+                lanes = slice(LANES * g, LANES * (g + 1))
+                if outer:
+                    piece = jnp.where(from_a, rowa_ref[:, lanes], rowb_ref[:, lanes])
+                else:
+                    piece = mask_ref[rows - wide : rows, lanes]
                 high, low = split(piece)
                 nhigh_ref[rows : rows + wide, LANES * g : LANES * (g + 1)] = high
                 nlow_ref[rows : rows + wide, LANES * g : LANES * (g + 1)] = low
@@ -304,8 +315,10 @@
     def strip(row, ref, rows, part, inner):
         edge = slice(packed + inner, packed + inner + 16)
         back, ahead = (-HALF * part) % LANES, (HALF - HALF * part) % LANES
-        turned = pltpu.roll(before_ref[edge, :], back, 1) if back else before_ref[edge, :]
-        final = pltpu.roll(after_ref[edge, :], ahead, 1) if ahead else after_ref[edge, :]
+        one, other = cola_ref[edge, :], colb_ref[edge, :]
+        turned, final = jnp.where(odd_col, one, other), jnp.where(odd_col, other, one)
+        turned = pltpu.roll(turned, back, 1) if back else turned
+        final = pltpu.roll(final, ahead, 1) if ahead else final
         for g in range(groups + 1):
             fresh = final
             if g < groups:
@@ -375,9 +388,9 @@
         place = pl.ds(pl.multiple_of(offset, LANES), width)
         target = target_ref[:, place]
         sensitivity = 2.0 * (resist - target) * STEEPNESS * resist * (1.0 - resist)
-        row = where_ref[0] + lax.broadcasted_iota(jnp.int32, (field_rows, width), 0)
-        col = where_ref[1] + offset + lax.broadcasted_iota(jnp.int32, (field_rows, width), 1)
-        inside = (row >= 0) & (row < where_ref[2]) & (col >= 0) & (col < where_ref[3])
+        row = spot_ref[2] + lax.broadcasted_iota(jnp.int32, (field_rows, width), 0)
+        col = spot_ref[3] + offset + lax.broadcasted_iota(jnp.int32, (field_rows, width), 1)
+        inside = (row >= 0) & (row < spot_ref[4]) & (col >= 0) & (col < spot_ref[5])
         sensitivity = jnp.where(inside, sensitivity, 0.0)
         ordered = (sensitivity, swapped(sensitivity))
         for k in range(KERNELS):
@@ -468,11 +481,13 @@
     return result[0] if single else result
 
 
-def neighbours(first, last, axis):
+def pairs(one, other, axis):
     count = lax.axis_size(axis)
-    up = [(i, i + 1) for i in range(count - 1)]
-    down = [(j, i) for i, j in up]
-    return lax.ppermute(last, axis, up), lax.ppermute(first, axis, down)
+    out = []
+    for x, start in ((one, 0), (other, 1)):
+        swap = [(i, i + 1) for i in range(start, count - 1, 2)]
+        out.append(lax.ppermute(x, axis, swap + [(j, i) for i, j in swap]))
+    return out
 
 
 def doubled(table, axis):
@@ -520,7 +535,20 @@
     stack = lax.all_to_all(copies, "deep", split_axis=0, concat_axis=0, tiled=True)
 
     near = doubled(doubled(named, "col"), "core")
-    me = jnp.stack([lax.axis_index(plane), lax.axis_index(everyone)]).astype(jnp.int32)
+    row_axes = ("deep", "core")
+    my_row, my_col = lax.axis_index(row_axes), lax.axis_index("col")
+    me = jnp.stack(
+        [
+            lax.axis_index(plane),
+            lax.axis_index(everyone),
+            my_row * height - HALF,
+            my_col * breadth - HALF,
+            jnp.int32(deep * cores * height),
+            jnp.int32(cols * breadth),
+            my_row % 2,
+            my_col % 2,
+        ]
+    ).astype(jnp.int32)
     owner = near // slots
     asked = requests(
         owner % peers == me[0], (owner // peers) * slots + near % slots, wide_capacity
@@ -539,11 +567,13 @@
         [waves],
         out_space=pl.ANY,
     )
-    packed, near, above, below = lax.optimization_barrier(
-        (packed, near, target[:HALF], target[height - HALF :])
-    )
-    row_axes = ("deep", "core")
-    above, below = neighbours(above, below, row_axes)
+    odd = me[6] > 0
+    head, foot = target[:HALF], target[height - HALF :]
+    packed, near, one, other = lax.optimization_barrier(
+        (packed, near, jnp.where(odd, head, foot), jnp.where(odd, foot, head))
+    )
+    one, other = pairs(one, other, row_axes)
+    above, below = jnp.where(odd, one, other), jnp.where(odd, other, one)
     arrived = lax.all_to_all(packed, plane, split_axis=0, concat_axis=0, tiled=True)
 
     everything = doubled(near, "deep")
@@ -559,7 +589,7 @@
     wide = 2 * HALF
     quarter = (height + wide) // 4
     edge = f32(height // 2 + quarter, LANES)
-    mask, first, last, left, right = kernel_call(
+    mask, rowa, rowb, cola, colb = kernel_call(
         assemble_kernel,
         "assemble",
         [f32(height, breadth), f32(wide, breadth), f32(wide, breadth), edge, edge],
@@ -567,25 +597,15 @@
             pltpu.VMEM((height * (breadth // LANES), LANES), F32),
             pltpu.VMEM((2, 4, quarter, LANES), F32),
         ],
-        [place(mine % peers, wide_capacity)],
+        [place(mine % peers, wide_capacity), me],
         [arrived, target, above, below],
         [wanted],
     )
-    before, after = neighbours(left, right, "col")
-    top, bottom = neighbours(first, last, row_axes)
+    cola, colb = pairs(cola, colb, "col")
+    rowa, rowb = pairs(rowa, rowb, row_axes)
     corner = f32(wide, LANES)
-    first, last = kernel_call(corners_kernel, "corners", [corner, corner], [], [], [before, after])
-    corner_top, corner_bottom = neighbours(first, last, row_axes)
-    my_row = lax.axis_index(("deep", "core"))
-    my_col = lax.axis_index("col")
-    where = jnp.stack(
-        [
-            my_row * height - HALF,
-            my_col * breadth - HALF,
-            jnp.int32(deep * cores * height),
-            jnp.int32(cols * breadth),
-        ]
-    ).astype(jnp.int32)
+    corners = kernel_call(corners_kernel, "corners", [corner, corner], [], [me], [cola, colb])
+    corners = pairs(*corners, row_axes)
     field_rows = height + 2 * HALF
     returned = kernel_call(
         image_kernel,
@@ -606,9 +626,8 @@
             pltpu.VMEM((KERNELS, height, breadth + 128), BF16),
             pltpu.VMEM((height * (breadth // LANES), LANES), F32),
         ],
-        [place(mine, capacity), where, kernel_weight],
-        [mask, top, bottom, before, after, corner_top, corner_bottom]
-        + [target, above, below, waves],
+        [place(mine, capacity), me, kernel_weight],
+        [mask, rowa, rowb, cola, colb, *corners, target, above, below, waves],
         megabytes=36,
     )
     back = lax.all_to_all(returned, everyone, split_axis=0, concat_axis=0, tiled=True)

time: 120 us -> 114 us (0.950)
  starting transfers between devices: 32.9 us -> 24.6 us
  blocking collectives: 31.2 us -> 37.3 us
  waiting for transfers between devices: 23.6 us -> 20.1 us
    ppermute x8, starting transfers between devices: 15.6 us -> 6.91 us  [pairs(): out.append(lax.ppermute(x, axis, swap + [(j, i) for i, j in swap]))]
    ppermute x8, waiting for transfers between devices: 9.16 us -> 2.93 us  [pairs(): out.append(lax.ppermute(x, axis, swap + [(j, i) for i, j in swap]))]
    all_to_all x1, blocking collectives: 31.2 us -> 37.3 us  [shards(): lax.all_to_all(returned, everyone, split_axis=0, concat_axis=0, tiled=True)]
    all_to_all x1, waiting for transfers between devices: 3.16 us -> 5.13 us  [shards(): lax.all_to_all(packed, plane, split_axis=0, concat_axis=0, tiled=True)]
  transfers between devices with their start and end apart: 15 -> 15, of which waited for: 8 -> 8; matrix products, arithmetic and copies ran while one was open for 3% -> 3% of each run, Pallas kernels for 0% -> 1%
where the time goes in v2:
time: 114 us
  blocking collectives  37.3 us (33%)
  Pallas kernels  26 us (23%)
  starting transfers between devices  24.6 us (22%)
  waiting for transfers between devices  20.1 us (18%)
  local copies, waits for them, and re-layouts  3.18 us (3%)
  other arithmetic  2.46 us (2%)
    all_to_all x1, blocking collectives, shards(): lax.all_to_all(returned, everyone, split_axis=0, concat_axis=0, tiled=True)  37.3 us
    pallas_call x6, Pallas kernels, kernel_call(): pl.pallas_call(body, out_shape=outs, in_specs=[pl.BlockSpec(memory_space=...  26 us
    ppermute x5, starting transfers between devices, doubled(): got = lax.ppermute(table, axis, [(i, i ^ bit) for i in range(count)])  7.51 us
    ppermute x8, starting transfers between devices, pairs(): out.append(lax.ppermute(x, axis, swap + [(j, i) for i, j in swap]))  6.91 us
    ppermute x5, waiting for transfers between devices, doubled(): got = lax.ppermute(table, axis, [(i, i ^ bit) for i in range(count)])  6.47 us
    all_to_all x1, starting transfers between devices, shards(): lax.all_to_all(copies, 'deep', split_axis=0, concat_axis=0, tiled=True)  6.45 us
    all_to_all x1, waiting for transfers between devices, shards(): lax.all_to_all(copies, 'deep', split_axis=0, concat_axis=0, tiled=True)  5.59 us
    all_to_all x1, waiting for transfers between devices, shards(): lax.all_to_all(packed, plane, split_axis=0, concat_axis=0, tiled=True)  5.13 us
  transfers between devices with their start and end apart: 15, of which 8 were waited for; matrix products, arithmetic and copies ran while one was open for 3% of the time, Pallas kernels for 1%

profile of v2, /device:TPU:0, one launch (start us, length us, event | category | flops | bytes accessed | tf_op | source)
XLA Modules:
  0.0 113.9 jit_solution(13273022186558185422)
XLA Ops:
  0.0 0.9 copy-done.1
  0.9 0.7 copy-done.3
  1.6 0.8 spread.1
  2.4 6.4 %all-to-all-start = ((f32[4,256,128]{2,1,0:T(8,128)}), f32[4,256,128]{2,1,0:T(8,128)S(1)}, u32[]{:S(2)}, u32[]{:S(2)}) async-start(f32[4,256,128]{2,1,0:T(8,128)} %bitcast.9), calls=%async_computation | async-start | bytes 1048576 | tf_op jit(solution)/shard_map/all_to_all | solution.py:535
  8.9 1.5 %collective-permute-start = (s32[1,128]{1,0:T(1,128)S(1)}, s32[1,128]{1,0:T(1,128)S(1)}, u32[]{:S(2)}, u32[]{:S(2)}) collective-permute-start(s32[1,128]{1,0:T(1,128)S(1)} %get-tuple-element.18), channel_id=1, source_target_pairs={{0,1},{1,0},{2,3},{3,2},{4,5},{5,4},{6,7},{7,6},{8,9},{9,8},{10,11... | collective-permute-start | bytes 1544 | tf_op jit(solution)/shard_map/ppermute | solution.py:497
  10.4 0.5 broadcast.474
  10.9 0.7 fusion.19
  12.4 1.5 %collective-permute-start.1 = (s32[2,128]{1,0:T(2,128)S(1)}, s32[2,128]{1,0:T(2,128)S(1)}, u32[]{:S(2)}, u32[]{:S(2)}) collective-permute-start(s32[2,128]{1,0:T(2,128)S(1)} %pad_add_fusion.3), channel_id=1, source_target_pairs={{0,2},{1,3},{2,0},{3,1},{4,6},{5,7},{6,4},{7,5},{8,10},{9,11},{10,... | collective-permute-start | bytes 3080 | tf_op jit(solution)/shard_map/ppermute | solution.py:497
  14.0 2.0 %collective-permute-done.1 = s32[2,128]{1,0:T(2,128)S(1)} collective-permute-done((s32[2,128]{1,0:T(2,128)S(1)}, s32[2,128]{1,0:T(2,128)S(1)}, u32[]{:S(2)}, u32[]{:S(2)}) %collective-permute-start.1) | collective-permute-done | bytes 1056 | tf_op jit(solution)/shard_map/ppermute | solution.py:497
  16.2 1.0 collective-permute-done.2
  17.8 5.6 %all-to-all-done = f32[4,256,128]{2,1,0:T(8,128)S(1)} async-done(((f32[4,256,128]{2,1,0:T(8,128)}), f32[4,256,128]{2,1,0:T(8,128)S(1)}, u32[]{:S(2)}, u32[]{:S(2)}) %all-to-all-start) | async-done | bytes 524320 | tf_op jit(solution)/shard_map/all_to_all | solution.py:535
  23.4 1.8 %pack.1 = f32[2048,128]{1,0:T(8,128)} custom-call(s32[8,32]{1,0:T(8,128)S(1)} %select_reduce_fusion.1.asked_ref, s32[8]{0:T(128)S(1)} %stack.27.me_ref.spot_ref, f32[1024,128]{1,0:T(8,128)S(1)} %bitcast.37, f32[32,128]{1,0:T(8,128)S(1)} %select_maximum_fusion.rest_0_.wave_ref), custom_call_target="tpu_custom_call" | custom-call | tf_op jit(solution)/shard_map/pack/pallas_call | solution.py:470
  25.2 3.7 %all-to-all-start.1 = ((f32[8,256,128]{2,1,0:T(8,128)}), f32[8,256,128]{2,1,0:T(8,128)S(1)}, u32[]{:S(2)}, u32[]{:S(2)}) async-start(f32[8,256,128]{2,1,0:T(8,128)} %bitcast.14), calls=%async_computation.1 | async-start | bytes 2097152 | tf_op jit(solution)/shard_map/all_to_all | solution.py:577
  29.0 0.5 collective-permute-start.5
  29.5 0.7 collective-permute-start.6
  30.2 4.4 %collective-permute-start.4 = (s32[16,128]{1,0:T(8,128)S(1)}, s32[16,128]{1,0:T(8,128)S(1)}, u32[]{:S(2)}, u32[]{:S(2)}) collective-permute-start(s32[16,128]{1,0:T(8,128)S(1)} %pad_add_fusion), channel_id=1, source_target_pairs={{0,16},{8,24},{16,0},{24,8},{1,17},{9,25},{17,1},{25,9},{2,18},{10... | collective-permute-start | bytes 24584 | tf_op jit(solution)/shard_map/ppermute | solution.py:497
  34.5 3.2 %collective-permute-done.4 = s32[16,128]{1,0:T(8,128)S(1)} collective-permute-done((s32[16,128]{1,0:T(8,128)S(1)}, s32[16,128]{1,0:T(8,128)S(1)}, u32[]{:S(2)}, u32[]{:S(2)}) %collective-permute-start.4) | collective-permute-done | bytes 8224 | tf_op jit(solution)/shard_map/ppermute | solution.py:497
  38.1 0.6 select_reduce_fusion.rest_0_.asked_ref
  38.7 5.1 %all-to-all-done.1 = f32[8,256,128]{2,1,0:T(8,128)S(1)} async-done(((f32[8,256,128]{2,1,0:T(8,128)}), f32[8,256,128]{2,1,0:T(8,128)S(1)}, u32[]{:S(2)}, u32[]{:S(2)}) %all-to-all-start.1) | async-done | bytes 1048608 | tf_op jit(solution)/shard_map/all_to_all | solution.py:577
  43.9 1.1 %assemble.1 = (f32[128,1024]{1,0:T(8,128)S(1)}, f32[64,1024]{1,0:T(8,128)S(1)}, f32[64,1024]{1,0:T(8,128)S(1)}, f32[112,128]{1,0:T(8,128)S(1)}, f32[112,128]{1,0:T(8,128)S(1)}) custom-call(s32[4,32]{1,0:T(4,128)S(1)} %get-tuple-element.47.index_ref, s32[8]{0:T(128)S(1)} %stack.27.me_ref.spot_ref, f32[2048,128]{1,0:T(8,128)S(1)} %bitcast.35, ...), custom_call_target="tpu_custom_call" | custom-call | tf_op jit(solution)/shard_map/assemble/pallas_call | solution.py:470
  45.0 0.4 collective-permute-start.7
  45.4 0.7 collective-permute-start.8
  46.0 0.9 collective-permute-start.9
  46.9 0.7 collective-permute-start.10
  47.6 2.7 %collective-permute-done.9.cola_ref = f32[112,128]{1,0:T(8,128)S(1)} collective-permute-done((f32[112,128]{1,0:T(8,128)S(1)}, f32[112,128]{1,0:T(8,128)S(1)}, u32[]{:S(2)}, u32[]{:S(2)}) %collective-permute-start.9) | collective-permute-done | bytes 57376 | tf_op jit(solution)/shard_map/ppermute | solution.py:489
  50.3 0.6 corners.1
  50.9 2.5 %collective-permute-start.11 = (f32[64,128]{1,0:T(8,128)S(1)}, f32[64,128]{1,0:T(8,128)S(1)}, u32[]{:S(2)}, u32[]{:S(2)}) collective-permute-start(f32[64,128]{1,0:T(8,128)S(1)} %get-tuple-element.29), channel_id=1, source_target_pairs={{0,4},{8,12},{16,20},{24,28},{4,0},{12,8},{20,16},{28,24},{1,5},{9... | collective-permute-start | bytes 98312 | tf_op jit(solution)/shard_map/ppermute | solution.py:489
  53.5 0.7 collective-permute-start.12
  54.4 0.6 copy-done.4
  55.0 19.2 %image.1 = f32[2048,128]{1,0:T(8,128)S(1)} custom-call(s32[4,32]{1,0:T(4,128)S(1)} %get-tuple-element.48.index_ref, s32[8]{0:T(128)S(1)} %stack.27.me_ref.spot_ref, f32[8]{0:T(128)S(1)} %copy-done.4, f32[128,1024]{1,0:T(8,128)S(1)} %get-tuple-element.24.mask_ref, f32[64,1024]{1,0:T(8,128)S(1)} %collective-permute-done.7.rowa_ref, ...), custom_call_target="tpu_custom_call" | custom-call | tf_op jit(solution)/shard_map/image/pallas_call | solution.py:470
  74.2 37.3 %all_to_all.33 = f32[32,64,128]{2,1,0:T(8,128)S(1)} all-to-all(f32[32,64,128]{2,1,0:T(8,128)S(1)} %bitcast.34), channel_id=1, replica_groups=mesh['deep'=4,'core'=2,'col'=4] {'deep','core','col'}, dimensions={0} | all-to-all | bytes 2097152 | tf_op jit(solution)/shard_map/all_to_all | solution.py:633
  111.5 2.4 %step.1 = f32[256,128]{1,0:T(8,128)} custom-call(s32[32,8]{1,0:T(8,128)S(1)} %select_reduce_fusion.rest_0_.asked_ref, s32[8]{0:T(128)S(1)} %stack.27.me_ref.spot_ref, f32[256,128]{1,0:T(8,128)S(1)} %bitcast.39, f32[2048,128]{1,0:T(8,128)S(1)} %bitcast.36), custom_call_target="tpu_custom_call" | custom-call | tf_op jit(solution)/shard_map/step/pallas_call | solution.py:470
  (49 shorter events, 2.3 us)
Async XLA Ops:
  0.0 0.9 copy-start.1
  0.9 0.7 copy-start.3
  2.4 9.6 %copy-start = (f32[128,1024]{1,0:T(8,128)S(1)}, f32[128,1024]{1,0:T(8,128)}, u32[]{:S(2)}) copy-start(f32[128,1024]{1,0:T(8,128)} %own_ref.1) | copy-start | bytes 1572868
  2.4 20.9 %all-to-all-start = ((f32[4,256,128]{2,1,0:T(8,128)}), f32[4,256,128]{2,1,0:T(8,128)S(1)}, u32[]{:S(2)}, u32[]{:S(2)}) async-start(f32[4,256,128]{2,1,0:T(8,128)} %bitcast.9), calls=%async_computation | async-start | bytes 1048576 | tf_op jit(solution)/shard_map/all_to_all | solution.py:535
  8.9 3.5 %collective-permute-start = (s32[1,128]{1,0:T(1,128)S(1)}, s32[1,128]{1,0:T(1,128)S(1)}, u32[]{:S(2)}, u32[]{:S(2)}) collective-permute-start(s32[1,128]{1,0:T(1,128)S(1)} %get-tuple-element.18), channel_id=1, source_target_pairs={{0,1},{1,0},{2,3},{3,2},{4,5},{5,4},{6,7},{7,6},{8,9},{9,8},{10,11... | collective-permute-start | bytes 1544 | tf_op jit(solution)/shard_map/ppermute | solution.py:497
  12.0 1.9 %copy-start.5 = (f32[8,65]{1,0:T(8,128)S(1)}, f32[8,65]{1,0:T(8,128)}, u32[]{:S(2)}) copy-start(f32[8,65]{1,0:T(8,128)} %param.10) | copy-start | bytes 6244
  12.1 1.9 %copy-start.6 = (f32[8,65]{1,0:T(8,128)S(1)}, f32[8,65]{1,0:T(8,128)}, u32[]{:S(2)}) copy-start(f32[8,65]{1,0:T(8,128)} %param.9) | copy-start | bytes 6244
  12.4 3.6 %collective-permute-start.1 = (s32[2,128]{1,0:T(2,128)S(1)}, s32[2,128]{1,0:T(2,128)S(1)}, u32[]{:S(2)}, u32[]{:S(2)}) collective-permute-start(s32[2,128]{1,0:T(2,128)S(1)} %pad_add_fusion.3), channel_id=1, source_target_pairs={{0,2},{1,3},{2,0},{3,1},{4,6},{5,7},{6,4},{7,5},{8,10},{9,11},{10,... | collective-permute-start | bytes 3080 | tf_op jit(solution)/shard_map/ppermute | solution.py:497
  16.0 1.2 %collective-permute-start.2 = (s32[4,128]{1,0:T(4,128)S(1)}, s32[4,128]{1,0:T(4,128)S(1)}, u32[]{:S(2)}, u32[]{:S(2)}) collective-permute-start(s32[4,128]{1,0:T(4,128)S(1)} %pad_add_fusion.2), channel_id=1, source_target_pairs={{0,4},{4,0},{1,5},{5,1},{2,6},{6,2},{3,7},{7,3},{8,12},{12,8},{9,1... | collective-permute-start | bytes 6152 | tf_op jit(solution)/shard_map/ppermute | solution.py:497
  25.2 5.0 %collective-permute-start.3 = (s32[8,128]{1,0:T(8,128)S(1)}, s32[8,128]{1,0:T(8,128)S(1)}, u32[]{:S(2)}, u32[]{:S(2)}) collective-permute-start(s32[8,128]{1,0:T(8,128)S(1)} %get-tuple-element.20), channel_id=1, source_target_pairs={{0,8},{8,0},{16,24},{24,16},{1,9},{9,1},{17,25},{25,17},{2,10},{10... | collective-permute-start | bytes 12296 | tf_op jit(solution)/shard_map/ppermute | solution.py:497
  25.2 18.6 %all-to-all-start.1 = ((f32[8,256,128]{2,1,0:T(8,128)}), f32[8,256,128]{2,1,0:T(8,128)S(1)}, u32[]{:S(2)}, u32[]{:S(2)}) async-start(f32[8,256,128]{2,1,0:T(8,128)} %bitcast.14), calls=%async_computation.1 | async-start | bytes 2097152 | tf_op jit(solution)/shard_map/all_to_all | solution.py:577
  29.0 9.7 %collective-permute-start.5 = (f32[32,1024]{1,0:T(8,128)S(1)}, f32[32,1024]{1,0:T(8,128)S(1)}, u32[]{:S(2)}, u32[]{:S(2)}) collective-permute-start(f32[32,1024]{1,0:T(8,128)S(1)} %get-tuple-element.22), channel_id=1, source_target_pairs={{0,4},{8,12},{16,20},{24,28},{4,0},{12,8},{20,16},{28,24},{1,5},{9... | collective-permute-start | bytes 393224 | tf_op jit(solution)/shard_map/ppermute | solution.py:489
  29.5 9.2 %collective-permute-start.6 = (f32[32,1024]{1,0:T(8,128)S(1)}, f32[32,1024]{1,0:T(8,128)S(1)}, u32[]{:S(2)}, u32[]{:S(2)}) collective-permute-start(f32[32,1024]{1,0:T(8,128)S(1)} %get-tuple-element.23), channel_id=1, source_target_pairs={{4,8},{12,16},{20,24},{8,4},{16,12},{24,20},{5,9},{13,17},{21,25},... | collective-permute-start | bytes 393224 | tf_op jit(solution)/shard_map/ppermute | solution.py:489
  30.2 7.5 %collective-permute-start.4 = (s32[16,128]{1,0:T(8,128)S(1)}, s32[16,128]{1,0:T(8,128)S(1)}, u32[]{:S(2)}, u32[]{:S(2)}) collective-permute-start(s32[16,128]{1,0:T(8,128)S(1)} %pad_add_fusion), channel_id=1, source_target_pairs={{0,16},{8,24},{16,0},{24,8},{1,17},{9,25},{17,1},{25,9},{2,18},{10... | collective-permute-start | bytes 24584 | tf_op jit(solution)/shard_map/ppermute | solution.py:497
  45.0 9.3 %collective-permute-start.7 = (f32[64,1024]{1,0:T(8,128)S(1)}, f32[64,1024]{1,0:T(8,128)S(1)}, u32[]{:S(2)}, u32[]{:S(2)}) collective-permute-start(f32[64,1024]{1,0:T(8,128)S(1)} %get-tuple-element.25), channel_id=1, source_target_pairs={{0,4},{8,12},{16,20},{24,28},{4,0},{12,8},{20,16},{28,24},{1,5},{9... | collective-permute-start | bytes 786440 | tf_op jit(solution)/shard_map/ppermute | solution.py:489
  45.4 9.0 %collective-permute-start.8 = (f32[64,1024]{1,0:T(8,128)S(1)}, f32[64,1024]{1,0:T(8,128)S(1)}, u32[]{:S(2)}, u32[]{:S(2)}) collective-permute-start(f32[64,1024]{1,0:T(8,128)S(1)} %get-tuple-element.26), channel_id=1, source_target_pairs={{4,8},{12,16},{20,24},{8,4},{16,12},{24,20},{5,9},{13,17},{21,25},... | collective-permute-start | bytes 786440 | tf_op jit(solution)/shard_map/ppermute | solution.py:489
  46.0 4.2 %collective-permute-start.9 = (f32[112,128]{1,0:T(8,128)S(1)}, f32[112,128]{1,0:T(8,128)S(1)}, u32[]{:S(2)}, u32[]{:S(2)}) collective-permute-start(f32[112,128]{1,0:T(8,128)S(1)} %get-tuple-element.27), channel_id=1, source_target_pairs={{0,1},{2,3},{1,0},{3,2},{4,5},{6,7},{5,4},{7,6},{8,9},{10,11},{9,8... | collective-permute-start | bytes 172040 | tf_op jit(solution)/shard_map/ppermute | solution.py:489
  46.9 3.4 %collective-permute-start.10 = (f32[112,128]{1,0:T(8,128)S(1)}, f32[112,128]{1,0:T(8,128)S(1)}, u32[]{:S(2)}, u32[]{:S(2)}) collective-permute-start(f32[112,128]{1,0:T(8,128)S(1)} %get-tuple-element.28), channel_id=1, source_target_pairs={{1,2},{2,1},{5,6},{6,5},{9,10},{10,9},{13,14},{14,13},{17,18},{18,... | collective-permute-start | bytes 172040 | tf_op jit(solution)/shard_map/ppermute | solution.py:489
  50.9 3.4 %collective-permute-start.11 = (f32[64,128]{1,0:T(8,128)S(1)}, f32[64,128]{1,0:T(8,128)S(1)}, u32[]{:S(2)}, u32[]{:S(2)}) collective-permute-start(f32[64,128]{1,0:T(8,128)S(1)} %get-tuple-element.29), channel_id=1, source_target_pairs={{0,4},{8,12},{16,20},{24,28},{4,0},{12,8},{20,16},{28,24},{1,5},{9... | collective-permute-start | bytes 98312 | tf_op jit(solution)/shard_map/ppermute | solution.py:489
  53.5 0.9 collective-permute-start.12
  54.3 0.7 copy-start.4
  74.2 37.3 %copy-start.2 = (f32[32,1024]{1,0:T(8,128)S(1)}, f32[32,1024]{1,0:T(8,128)}, u32[]{:S(2)}) copy-start(f32[32,1024]{1,0:T(8,128)} %param.6) | copy-start | bytes 393220

commit v3 on v2

--- a/solution.py
+++ b/solution.py
@@ -171,13 +171,11 @@
         strip(row, ref, slice(start, start + 16), row // quarter, row % quarter)
 
 
-def assemble_kernel(index_ref, spot_ref, tiles_ref, target_ref, ttop_ref, tbottom_ref, *rest):
-    mask_ref, rowa_ref, rowb_ref, cola_ref, colb_ref, turned_ref, pack_ref = rest[-7:]
-    odd_row, odd_col = spot_ref[6] > 0, spot_ref[7] > 0
+def assemble_kernel(index_ref, spot_ref, tiles_ref, mask_ref, rowa_ref, rowb_ref, turned_ref):
+    odd_row = spot_ref[6] > 0
     tile_rows, tile_cols = index_ref.shape
-    height, breadth = target_ref.shape
+    height = tile_rows * TILE
     wide = 2 * HALF
-    half = height // 2
     groups = tile_cols // 4
     block = lax.broadcasted_iota(jnp.int32, (8, LANES), 1) // 32
 
@@ -191,25 +189,41 @@
             for s, piece in enumerate(transpose_blocks(parts, block)):
                 turned_ref[pl.ds(g * height + a * TILE + s, 8, stride=4), :] = piece
 
-    lane = lax.broadcasted_iota(jnp.int32, (half, LANES), 1)
     for g in range(groups):
         lanes = slice(LANES * g, LANES * (g + 1))
         piece = turned_ref[g * height : (g + 1) * height, :]
         mask_ref[:, lanes] = piece
         rowa_ref[:, lanes] = jnp.where(odd_row, piece[:wide], piece[height - wide :])
         rowb_ref[:, lanes] = jnp.where(odd_row, piece[height - wide :], piece[:wide])
-        upper, lower = piece[:half], piece[half:]
-        if g == 0:
-            left = jnp.where(lane < wide, upper, pltpu.roll(lower, wide, 1))
-        if g == groups - 1:
-            right = jnp.where(lane < wide, pltpu.roll(upper, wide, 1), lower)
-    cola_ref[:half, :] = jnp.where(odd_col, left, right)
-    colb_ref[:half, :] = jnp.where(odd_col, right, left)
+
+
+def edges_kernel(spot_ref, mask_ref, rowa_ref, rowb_ref, target_ref, ttop_ref, tbottom_ref, *rest):
+    cola_ref, colb_ref, pack_ref = rest[-3:]
+    odd_row, odd_col = spot_ref[6] > 0, spot_ref[7] > 0
+    height, breadth = mask_ref.shape
+    wide = 2 * HALF
+    half = height // 2
+    packed = half + wide
+    lane = lax.broadcasted_iota(jnp.int32, (packed, LANES), 1)
+    head, tail = slice(0, LANES), slice(breadth - LANES, breadth)
+
+    def halves(lanes):
+        one, other = rowa_ref[:, lanes], rowb_ref[:, lanes]
+        top, bottom = jnp.where(odd_row, one, other), jnp.where(odd_row, other, one)
+        upper = jnp.concatenate([top, mask_ref[:half, lanes]], axis=0)
+        return upper, jnp.concatenate([mask_ref[half:, lanes], bottom], axis=0)
+
+    upper, lower = halves(head)
+    left = jnp.where(lane < wide, upper, pltpu.roll(lower, wide, 1))
+    upper, lower = halves(tail)
+    right = jnp.where(lane < wide, pltpu.roll(upper, wide, 1), lower)
+    cola_ref[:packed, :] = jnp.where(odd_col, left, right)
+    colb_ref[:packed, :] = jnp.where(odd_col, right, left)
 
     quarter = (height + 2 * HALF) // 4
 
     def strip(row, ref, rows, part, inner):
-        for side, lanes in enumerate((slice(0, LANES), slice(breadth - LANES, breadth))):
+        for side, lanes in enumerate((head, tail)):
             shift = (HALF * (part + side)) % LANES
             piece = ref[rows, lanes]
             pack_ref[side, part, inner : inner + 16, :] = (
@@ -224,20 +238,8 @@
         for part in range(1, 4):
             piece = jnp.where(part_of == part, pack_ref[side, part], piece)
         sides.append(piece)
-    cola_ref[half:, :] = jnp.where(odd_col, sides[0], sides[1])
-    colb_ref[half:, :] = jnp.where(odd_col, sides[1], sides[0])
-
-
-def corners_kernel(spot_ref, cola_ref, colb_ref, rowa_ref, rowb_ref):
-    odd_row, odd_col = spot_ref[6] > 0, spot_ref[7] > 0
-    wide = 2 * HALF
-    lane = lax.broadcasted_iota(jnp.int32, (wide, LANES), 1)
-    one, other = cola_ref[:wide, :], colb_ref[:wide, :]
-    before, after = jnp.where(odd_col, one, other), jnp.where(odd_col, other, one)
-    first = jnp.where(lane < wide, before, pltpu.roll(after, wide, 1))
-    last = jnp.where(lane < wide, pltpu.roll(before, wide, 1), after)
-    rowa_ref[...] = jnp.where(odd_row, first, last)
-    rowb_ref[...] = jnp.where(odd_row, last, first)
+    cola_ref[packed:, :] = jnp.where(odd_col, sides[0], sides[1])
+    colb_ref[packed:, :] = jnp.where(odd_col, sides[1], sides[0])
 
 
 def image_kernel(
@@ -249,8 +251,6 @@
     rowb_ref,
     cola_ref,
     colb_ref,
-    cornera_ref,
-    cornerb_ref,
     own_ref,
     ttop_ref,
     tbottom_ref,
@@ -284,15 +284,14 @@
     for rows in range(0, high_rows, wide):
         outer = rows == 0 or rows == high_rows - wide
         from_a = odd_row if rows == 0 else jnp.logical_not(odd_row)
-        if outer:
-            turned = final = jnp.where(from_a, cornera_ref[...], cornerb_ref[...])
+        half = high_rows // 2
+        edge = slice(rows % half, rows % half + wide)
+        one, other = cola_ref[edge, :], colb_ref[edge, :]
+        turned, final = jnp.where(odd_col, one, other), jnp.where(odd_col, other, one)
+        if rows < half:
+            final = pltpu.roll(final, wide, 1)
         else:
-            one, other = cola_ref[:wide, :], colb_ref[:wide, :]
-            turned, final = jnp.where(odd_col, one, other), jnp.where(odd_col, other, one)
-            if rows == wide:
-                final = pltpu.roll(final, wide, 1)
-            else:
-                turned = pltpu.roll(turned, wide, 1)
+            turned = pltpu.roll(turned, wide, 1)
         for g in range(groups + 1):
             fresh = final
             if g < groups:
@@ -309,7 +308,7 @@
             mhigh_ref[rows : rows + wide, LANES * g : LANES * (g + 1)] = high
             mlow_ref[rows : rows + wide, LANES * g : LANES * (g + 1)] = low
             turned = fresh
-    packed = rows_here // 2
+    packed = high_rows // 2
     near_lane = lax.broadcasted_iota(jnp.int32, (16, LANES), 1)
 
     def strip(row, ref, rows, part, inner):
@@ -365,21 +364,28 @@
         for quad in range(KERNELS // 4):
             even = mm(even_rows, band(quad, 0))
             odd = even if last else mm(odd_rows, band(quad, 1))
-            for h in range(4):
-                k = 4 * quad + h
-                pieces = []
-                for j in range(blocks):
-                    rows = slice(j * high_rows, (j + 1) * high_rows)
-                    lanes = slice((h // 2) * LANES, (h // 2 + 1) * LANES)
-                    if last:
-                        pieces.append(even[rows, lanes])
-                    elif h % 2 == 0:
-                        pieces.append(jnp.where(left, even[rows, lanes], odd[rows, lanes]))
-                    else:
-                        pieces.append(jnp.where(left, odd[rows, lanes], even[rows, lanes]))
-                high, low = split(pieces[0] if last else jnp.concatenate(pieces, axis=1))
-                both = mm(jnp.concatenate([frow_ref[k, 0], frow_ref[k, 1]], axis=0), high)
-                field = both[:field_rows] + both[field_rows:] + mm(frow_ref[k, 0], low)
+            four = range(4 * quad, 4 * quad + 4)
+            if last:
+                high, low = split(even)
+                both = mm(jnp.concatenate([frow_ref[k, v] for k in four for v in range(2)], 0), high)
+                more = mm(jnp.concatenate([frow_ref[k, 0] for k in four], axis=0), low)
+            for h, k in enumerate(four):
+                lanes = slice((h // 2) * LANES, (h // 2 + 1) * LANES)
+                if last:
+                    start = 2 * h * field_rows
+                    field = both[start : start + field_rows, lanes]
+                    field = field + both[start + field_rows : start + 2 * field_rows, lanes]
+                    field = field + more[h * field_rows : (h + 1) * field_rows, lanes]
+                else:
+                    pieces = []
+                    for j in range(blocks):
+                        rows = slice(j * high_rows, (j + 1) * high_rows)
+                        one, other = even[rows, lanes], odd[rows, lanes]
+                        one, other = (other, one) if h % 2 else (one, other)
+                        pieces.append(jnp.where(left, one, other))
+                    high, low = split(jnp.concatenate(pieces, axis=1))
+                    both = mm(jnp.concatenate([frow_ref[k, 0], frow_ref[k, 1]], axis=0), high)
+                    field = both[:field_rows] + both[field_rows:] + mm(frow_ref[k, 0], low)
                 field_ref[k, :, :width] = field
                 term = weight_ref[k] * field * field
                 sums[h % 2] = term if sums[h % 2] is None else sums[h % 2] + term
@@ -393,15 +399,41 @@
         inside = (row >= 0) & (row < spot_ref[4]) & (col >= 0) & (col < spot_ref[5])
         sensitivity = jnp.where(inside, sensitivity, 0.0)
         ordered = (sensitivity, swapped(sensitivity))
-        for k in range(KERNELS):
-            product = (2.0 * weight_ref[k]) * ordered[k % 2] * field_ref[k, :, :width]
-            high, low = split(product)
-            near = brow_ref[k, 0, :, :field_rows]
-            both = mm(jnp.concatenate([near, brow_ref[k, 1, :, :field_rows]], axis=0), high)
-            part = both[:rows_here] + both[rows_here:] + mm(near, low)
+
+        def product(k):
+            return (2.0 * weight_ref[k]) * ordered[k % 2] * field_ref[k, :, :width]
+
+        def keep(k, part):
             straight, turned = (part, swapped(part))[:: 1 - 2 * (k % 2)]
             ghigh_ref[k, :, place] = straight.astype(BF16)
             gturn_ref[k, :, place] = split(turned)[1]
+
+        if last:
+            half = left[:field_rows]
+            for quad in range(KERNELS // 4):
+                four = range(4 * quad, 4 * quad + 4)
+                each = [product(k) for k in four]
+                high, low = split(
+                    jnp.concatenate(
+                        [jnp.where(half, each[0], each[1]), jnp.where(half, each[2], each[3])],
+                        axis=1,
+                    )
+                )
+                near = [brow_ref[k, v, :, :field_rows] for k in four for v in range(2)]
+                both = mm(jnp.concatenate(near, axis=0), high)
+                more = mm(jnp.concatenate(near[::2], axis=0), low)
+                for h, k in enumerate(four):
+                    lanes = slice((h // 2) * LANES, (h // 2 + 1) * LANES)
+                    start = 2 * h * rows_here
+                    part = both[start : start + rows_here, lanes]
+                    part = part + both[start + rows_here : start + 2 * rows_here, lanes]
+                    keep(k, part + more[h * rows_here : (h + 1) * rows_here, lanes])
+            return
+        for k in range(KERNELS):
+            high, low = split(product(k))
+            near = brow_ref[k, 0, :, :field_rows]
+            both = mm(jnp.concatenate([near, brow_ref[k, 1, :, :field_rows]], axis=0), high)
+            keep(k, both[:rows_here] + both[rows_here:] + mm(near, low))
 
     supers = tile_cols * TILE // WIDE
 
@@ -588,24 +620,26 @@
 
     wide = 2 * HALF
     quarter = (height + wide) // 4
-    edge = f32(height // 2 + quarter, LANES)
-    mask, rowa, rowb, cola, colb = kernel_call(
+    edge = f32(height // 2 + wide + quarter, LANES)
+    mask, rowa, rowb = kernel_call(
         assemble_kernel,
         "assemble",
-        [f32(height, breadth), f32(wide, breadth), f32(wide, breadth), edge, edge],
-        [
-            pltpu.VMEM((height * (breadth // LANES), LANES), F32),
-            pltpu.VMEM((2, 4, quarter, LANES), F32),
-        ],
+        [f32(height, breadth), f32(wide, breadth), f32(wide, breadth)],
+        [pltpu.VMEM((height * (breadth // LANES), LANES), F32)],
         [place(mine % peers, wide_capacity), me],
-        [arrived, target, above, below],
+        [arrived],
+    )
+    rowa, rowb = pairs(rowa, rowb, row_axes)
+    cola, colb = kernel_call(
+        edges_kernel,
+        "edges",
+        [edge, edge],
+        [pltpu.VMEM((2, 4, quarter, LANES), F32)],
+        [me],
+        [mask, rowa, rowb, target, above, below],
         [wanted],
     )
     cola, colb = pairs(cola, colb, "col")
-    rowa, rowb = pairs(rowa, rowb, row_axes)
-    corner = f32(wide, LANES)
-    corners = kernel_call(corners_kernel, "corners", [corner, corner], [], [me], [cola, colb])
-    corners = pairs(*corners, row_axes)
     field_rows = height + 2 * HALF
     returned = kernel_call(
         image_kernel,
@@ -627,7 +661,7 @@
             pltpu.VMEM((height * (breadth // LANES), LANES), F32),
         ],
         [place(mine, capacity), me, kernel_weight],
-        [mask, rowa, rowb, cola, colb, *corners, target, above, below, waves],
+        [mask, rowa, rowb, cola, colb, target, above, below, waves],
         megabytes=36,
     )
     back = lax.all_to_all(returned, everyone, split_axis=0, concat_axis=0, tiled=True)

time: 114 us -> 114 us (level)
  starting transfers between devices: 24.6 us -> 21.6 us
  blocking collectives: 37.3 us -> 39.3 us
    ppermute x8 -> x6, starting transfers between devices: 6.91 us -> 3.91 us  [pairs(): out.append(lax.ppermute(x, axis, swap + [(j, i) for i, j in swap]))]
    all_to_all x1, blocking collectives: 37.3 us -> 39.3 us  [shards(): lax.all_to_all(returned, everyone, split_axis=0, concat_axis=0, tiled=True)]
    ppermute x8 -> x6, waiting for transfers between devices: 2.93 us -> 2.88 us  [pairs(): out.append(lax.ppermute(x, axis, swap + [(j, i) for i, j in swap]))]
  transfers between devices with their start and end apart: 15 -> 13, of which waited for: 8 -> 7; matrix products, arithmetic and copies ran while one was open for 3% -> 3% of each run, Pallas kernels for 1% -> 1%
where the time goes in v3:
time: 114 us; the launch traced here: 113 us
  blocking collectives  39.3 us (34%)
  Pallas kernels  26.3 us (23%)
  starting transfers between devices  21.6 us (19%)
  waiting for transfers between devices  20.7 us (18%)
  local copies, waits for them, and re-layouts  2.54 us (2%)
  other arithmetic  2.46 us (2%)
    all_to_all x1, blocking collectives, shards(): lax.all_to_all(returned, everyone, split_axis=0, concat_axis=0, tiled=True)  39.3 us
    pallas_call x6, Pallas kernels, kernel_call(): pl.pallas_call(body, out_shape=outs, in_specs=[pl.BlockSpec(memory_space=...  26.3 us
    ppermute x5, starting transfers between devices, doubled(): got = lax.ppermute(table, axis, [(i, i ^ bit) for i in range(count)])  7.51 us
    ppermute x5, waiting for transfers between devices, doubled(): got = lax.ppermute(table, axis, [(i, i ^ bit) for i in range(count)])  6.47 us
    all_to_all x1, starting transfers between devices, shards(): lax.all_to_all(copies, 'deep', split_axis=0, concat_axis=0, tiled=True)  6.45 us
    all_to_all x1, waiting for transfers between devices, shards(): lax.all_to_all(packed, plane, split_axis=0, concat_axis=0, tiled=True)  5.8 us
    all_to_all x1, waiting for transfers between devices, shards(): lax.all_to_all(copies, 'deep', split_axis=0, concat_axis=0, tiled=True)  5.59 us
    ppermute x6, starting transfers between devices, pairs(): out.append(lax.ppermute(x, axis, swap + [(j, i) for i, j in swap]))  3.91 us
  transfers between devices with their start and end apart: 13, of which 7 were waited for; matrix products, arithmetic and copies ran while one was open for 3% of the time, Pallas kernels for 1%

profile of v3, /device:TPU:0, one launch (start us, length us, event | category | flops | bytes accessed | tf_op | source)
XLA Modules:
  0.0 113.2 jit_solution(2251643348002663751)
XLA Ops:
  0.0 0.9 copy-done.1
  0.9 0.7 copy-done.3
  1.6 0.8 spread.1
  2.4 6.4 %all-to-all-start = ((f32[4,256,128]{2,1,0:T(8,128)}), f32[4,256,128]{2,1,0:T(8,128)S(1)}, u32[]{:S(2)}, u32[]{:S(2)}) async-start(f32[4,256,128]{2,1,0:T(8,128)} %bitcast.9), calls=%async_computation | async-start | bytes 1048576 | tf_op jit(solution)/shard_map/all_to_all | solution.py:567
  8.9 1.5 %collective-permute-start = (s32[1,128]{1,0:T(1,128)S(1)}, s32[1,128]{1,0:T(1,128)S(1)}, u32[]{:S(2)}, u32[]{:S(2)}) collective-permute-start(s32[1,128]{1,0:T(1,128)S(1)} %get-tuple-element.16), channel_id=1, source_target_pairs={{0,1},{1,0},{2,3},{3,2},{4,5},{5,4},{6,7},{7,6},{8,9},{9,8},{10,11... | collective-permute-start | bytes 1544 | tf_op jit(solution)/shard_map/ppermute | solution.py:529
  10.4 0.5 broadcast.474
  10.9 0.7 fusion.19
  12.1 0.3 collective-permute-done
  12.4 1.5 %collective-permute-start.1 = (s32[2,128]{1,0:T(2,128)S(1)}, s32[2,128]{1,0:T(2,128)S(1)}, u32[]{:S(2)}, u32[]{:S(2)}) collective-permute-start(s32[2,128]{1,0:T(2,128)S(1)} %pad_add_fusion.3), channel_id=1, source_target_pairs={{0,2},{1,3},{2,0},{3,1},{4,6},{5,7},{6,4},{7,5},{8,10},{9,11},{10,... | collective-permute-start | bytes 3080 | tf_op jit(solution)/shard_map/ppermute | solution.py:529
  14.0 2.0 %collective-permute-done.1 = s32[2,128]{1,0:T(2,128)S(1)} collective-permute-done((s32[2,128]{1,0:T(2,128)S(1)}, s32[2,128]{1,0:T(2,128)S(1)}, u32[]{:S(2)}, u32[]{:S(2)}) %collective-permute-start.1) | collective-permute-done | bytes 1056 | tf_op jit(solution)/shard_map/ppermute | solution.py:529
  16.2 1.0 collective-permute-done.2
  17.2 0.3 reduce_window_sum.22
  17.8 5.6 %all-to-all-done = f32[4,256,128]{2,1,0:T(8,128)S(1)} async-done(((f32[4,256,128]{2,1,0:T(8,128)}), f32[4,256,128]{2,1,0:T(8,128)S(1)}, u32[]{:S(2)}, u32[]{:S(2)}) %all-to-all-start) | async-done | bytes 524320 | tf_op jit(solution)/shard_map/all_to_all | solution.py:567
  23.4 1.8 %pack.1 = f32[2048,128]{1,0:T(8,128)} custom-call(s32[8,32]{1,0:T(8,128)S(1)} %select_reduce_fusion.1.asked_ref, s32[8]{0:T(128)S(1)} %stack.27.me_ref.spot_ref, f32[1024,128]{1,0:T(8,128)S(1)} %bitcast.37, f32[32,128]{1,0:T(8,128)S(1)} %select_maximum_fusion.rest_0_.wave_ref), custom_call_target="tpu_custom_call" | custom-call | tf_op jit(solution)/shard_map/pack/pallas_call | solution.py:502
  25.2 3.7 %all-to-all-start.1 = ((f32[8,256,128]{2,1,0:T(8,128)}), f32[8,256,128]{2,1,0:T(8,128)S(1)}, u32[]{:S(2)}, u32[]{:S(2)}) async-start(f32[8,256,128]{2,1,0:T(8,128)} %bitcast.14), calls=%async_computation.1 | async-start | bytes 2097152 | tf_op jit(solution)/shard_map/all_to_all | solution.py:609
  29.0 0.5 collective-permute-start.7
  29.5 0.7 collective-permute-start.8
  30.2 4.4 %collective-permute-start.4 = (s32[16,128]{1,0:T(8,128)S(1)}, s32[16,128]{1,0:T(8,128)S(1)}, u32[]{:S(2)}, u32[]{:S(2)}) collective-permute-start(s32[16,128]{1,0:T(8,128)S(1)} %pad_add_fusion), channel_id=1, source_target_pairs={{0,16},{8,24},{16,0},{24,8},{1,17},{9,25},{17,1},{25,9},{2,18},{10... | collective-permute-start | bytes 24584 | tf_op jit(solution)/shard_map/ppermute | solution.py:529
  34.5 3.2 %collective-permute-done.4 = s32[16,128]{1,0:T(8,128)S(1)} collective-permute-done((s32[16,128]{1,0:T(8,128)S(1)}, s32[16,128]{1,0:T(8,128)S(1)}, u32[]{:S(2)}, u32[]{:S(2)}) %collective-permute-start.4) | collective-permute-done | bytes 8224 | tf_op jit(solution)/shard_map/ppermute | solution.py:529
  37.7 0.3 reduce_window_sum.23
  38.1 5.8 %all-to-all-done.1 = f32[8,256,128]{2,1,0:T(8,128)S(1)} async-done(((f32[8,256,128]{2,1,0:T(8,128)}), f32[8,256,128]{2,1,0:T(8,128)S(1)}, u32[]{:S(2)}, u32[]{:S(2)}) %all-to-all-start.1) | async-done | bytes 1048608 | tf_op jit(solution)/shard_map/all_to_all | solution.py:609
  43.9 1.1 assemble.1
  45.0 0.4 collective-permute-start.5
  45.3 0.7 collective-permute-start.6
  46.0 0.6 select_reduce_fusion.rest_0_.asked_ref
  46.7 0.7 edges.1
  47.4 0.9 collective-permute-start.9
  48.3 0.8 collective-permute-start.10
  49.1 2.9 %collective-permute-done.9.cola_ref = f32[176,128]{1,0:T(8,128)S(1)} collective-permute-done((f32[176,128]{1,0:T(8,128)S(1)}, f32[176,128]{1,0:T(8,128)S(1)}, u32[]{:S(2)}, u32[]{:S(2)}) %collective-permute-start.9) | collective-permute-done | bytes 90144 | tf_op jit(solution)/shard_map/ppermute | solution.py:521
  52.0 19.5 %image.1 = f32[2048,128]{1,0:T(8,128)S(1)} custom-call(s32[4,32]{1,0:T(4,128)S(1)} %get-tuple-element.44.index_ref, s32[8]{0:T(128)S(1)} %stack.27.me_ref.spot_ref, f32[8]{0:T(128)S(1)} %copy-done.4, f32[128,1024]{1,0:T(8,128)S(1)} %get-tuple-element.20.mask_ref, f32[64,1024]{1,0:T(8,128)S(1)} %collective-permute-done.5.rowa_ref, ...), custom_call_target="tpu_custom_call" | custom-call | tf_op jit(solution)/shard_map/image/pallas_call | solution.py:502
  71.5 39.3 %all_to_all.33 = f32[32,64,128]{2,1,0:T(8,128)S(1)} all-to-all(f32[32,64,128]{2,1,0:T(8,128)S(1)} %bitcast.34), channel_id=1, replica_groups=mesh['deep'=4,'core'=2,'col'=4] {'deep','core','col'}, dimensions={0} | all-to-all | bytes 2097152 | tf_op jit(solution)/shard_map/all_to_all | solution.py:667
  110.8 2.4 %step.1 = f32[256,128]{1,0:T(8,128)} custom-call(s32[32,8]{1,0:T(8,128)S(1)} %select_reduce_fusion.rest_0_.asked_ref, s32[8]{0:T(128)S(1)} %stack.27.me_ref.spot_ref, f32[256,128]{1,0:T(8,128)S(1)} %bitcast.39, f32[2048,128]{1,0:T(8,128)S(1)} %bitcast.36), custom_call_target="tpu_custom_call" | custom-call | tf_op jit(solution)/shard_map/step/pallas_call | solution.py:502
  (45 shorter events, 1.2 us)
Async XLA Ops:
  0.0 0.9 copy-start.1
  0.9 0.7 copy-start.3
  2.4 9.6 %copy-start = (f32[128,1024]{1,0:T(8,128)S(1)}, f32[128,1024]{1,0:T(8,128)}, u32[]{:S(2)}) copy-start(f32[128,1024]{1,0:T(8,128)} %own_ref.1) | copy-start | bytes 1572868
  2.4 20.9 %all-to-all-start = ((f32[4,256,128]{2,1,0:T(8,128)}), f32[4,256,128]{2,1,0:T(8,128)S(1)}, u32[]{:S(2)}, u32[]{:S(2)}) async-start(f32[4,256,128]{2,1,0:T(8,128)} %bitcast.9), calls=%async_computation | async-start | bytes 1048576 | tf_op jit(solution)/shard_map/all_to_all | solution.py:567
  8.9 3.5 %collective-permute-start = (s32[1,128]{1,0:T(1,128)S(1)}, s32[1,128]{1,0:T(1,128)S(1)}, u32[]{:S(2)}, u32[]{:S(2)}) collective-permute-start(s32[1,128]{1,0:T(1,128)S(1)} %get-tuple-element.16), channel_id=1, source_target_pairs={{0,1},{1,0},{2,3},{3,2},{4,5},{5,4},{6,7},{7,6},{8,9},{9,8},{10,11... | collective-permute-start | bytes 1544 | tf_op jit(solution)/shard_map/ppermute | solution.py:529
  12.1 1.9 %copy-start.5 = (f32[8,65]{1,0:T(8,128)S(1)}, f32[8,65]{1,0:T(8,128)}, u32[]{:S(2)}) copy-start(f32[8,65]{1,0:T(8,128)} %param.10) | copy-start | bytes 6244
  12.1 1.9 %copy-start.6 = (f32[8,65]{1,0:T(8,128)S(1)}, f32[8,65]{1,0:T(8,128)}, u32[]{:S(2)}) copy-start(f32[8,65]{1,0:T(8,128)} %param.9) | copy-start | bytes 6244
  12.4 3.6 %collective-permute-start.1 = (s32[2,128]{1,0:T(2,128)S(1)}, s32[2,128]{1,0:T(2,128)S(1)}, u32[]{:S(2)}, u32[]{:S(2)}) collective-permute-start(s32[2,128]{1,0:T(2,128)S(1)} %pad_add_fusion.3), channel_id=1, source_target_pairs={{0,2},{1,3},{2,0},{3,1},{4,6},{5,7},{6,4},{7,5},{8,10},{9,11},{10,... | collective-permute-start | bytes 3080 | tf_op jit(solution)/shard_map/ppermute | solution.py:529
  16.0 1.2 %collective-permute-start.2 = (s32[4,128]{1,0:T(4,128)S(1)}, s32[4,128]{1,0:T(4,128)S(1)}, u32[]{:S(2)}, u32[]{:S(2)}) collective-permute-start(s32[4,128]{1,0:T(4,128)S(1)} %pad_add_fusion.2), channel_id=1, source_target_pairs={{0,4},{4,0},{1,5},{5,1},{2,6},{6,2},{3,7},{7,3},{8,12},{12,8},{9,1... | collective-permute-start | bytes 6152 | tf_op jit(solution)/shard_map/ppermute | solution.py:529
  25.2 5.0 %collective-permute-start.3 = (s32[8,128]{1,0:T(8,128)S(1)}, s32[8,128]{1,0:T(8,128)S(1)}, u32[]{:S(2)}, u32[]{:S(2)}) collective-permute-start(s32[8,128]{1,0:T(8,128)S(1)} %get-tuple-element.18), channel_id=1, source_target_pairs={{0,8},{8,0},{16,24},{24,16},{1,9},{9,1},{17,25},{25,17},{2,10},{10... | collective-permute-start | bytes 12296 | tf_op jit(solution)/shard_map/ppermute | solution.py:529
  25.2 18.6 %all-to-all-start.1 = ((f32[8,256,128]{2,1,0:T(8,128)}), f32[8,256,128]{2,1,0:T(8,128)S(1)}, u32[]{:S(2)}, u32[]{:S(2)}) async-start(f32[8,256,128]{2,1,0:T(8,128)} %bitcast.14), calls=%async_computation.1 | async-start | bytes 2097152 | tf_op jit(solution)/shard_map/all_to_all | solution.py:609
  29.0 17.7 %collective-permute-start.7 = (f32[32,1024]{1,0:T(8,128)S(1)}, f32[32,1024]{1,0:T(8,128)S(1)}, u32[]{:S(2)}, u32[]{:S(2)}) collective-permute-start(f32[32,1024]{1,0:T(8,128)S(1)} %get-tuple-element.23), channel_id=1, source_target_pairs={{0,4},{8,12},{16,20},{24,28},{4,0},{12,8},{20,16},{28,24},{1,5},{9... | collective-permute-start | bytes 393224 | tf_op jit(solution)/shard_map/ppermute | solution.py:521
  29.5 17.2 %collective-permute-start.8 = (f32[32,1024]{1,0:T(8,128)S(1)}, f32[32,1024]{1,0:T(8,128)S(1)}, u32[]{:S(2)}, u32[]{:S(2)}) collective-permute-start(f32[32,1024]{1,0:T(8,128)S(1)} %get-tuple-element.24), channel_id=1, source_target_pairs={{4,8},{12,16},{20,24},{8,4},{16,12},{24,20},{5,9},{13,17},{21,25},... | collective-permute-start | bytes 393224 | tf_op jit(solution)/shard_map/ppermute | solution.py:521
  30.2 7.5 %collective-permute-start.4 = (s32[16,128]{1,0:T(8,128)S(1)}, s32[16,128]{1,0:T(8,128)S(1)}, u32[]{:S(2)}, u32[]{:S(2)}) collective-permute-start(s32[16,128]{1,0:T(8,128)S(1)} %pad_add_fusion), channel_id=1, source_target_pairs={{0,16},{8,24},{16,0},{24,8},{1,17},{9,25},{17,1},{25,9},{2,18},{10... | collective-permute-start | bytes 24584 | tf_op jit(solution)/shard_map/ppermute | solution.py:529
  45.0 1.7 %collective-permute-start.5 = (f32[64,1024]{1,0:T(8,128)S(1)}, f32[64,1024]{1,0:T(8,128)S(1)}, u32[]{:S(2)}, u32[]{:S(2)}) collective-permute-start(f32[64,1024]{1,0:T(8,128)S(1)} %get-tuple-element.21), channel_id=1, source_target_pairs={{0,4},{8,12},{16,20},{24,28},{4,0},{12,8},{20,16},{28,24},{1,5},{9... | collective-permute-start | bytes 786440 | tf_op jit(solution)/shard_map/ppermute | solution.py:521
  45.3 1.4 %collective-permute-start.6 = (f32[64,1024]{1,0:T(8,128)S(1)}, f32[64,1024]{1,0:T(8,128)S(1)}, u32[]{:S(2)}, u32[]{:S(2)}) collective-permute-start(f32[64,1024]{1,0:T(8,128)S(1)} %get-tuple-element.22), channel_id=1, source_target_pairs={{4,8},{12,16},{20,24},{8,4},{16,12},{24,20},{5,9},{13,17},{21,25},... | collective-permute-start | bytes 786440 | tf_op jit(solution)/shard_map/ppermute | solution.py:521
  47.4 4.6 %collective-permute-start.9 = (f32[176,128]{1,0:T(8,128)S(1)}, f32[176,128]{1,0:T(8,128)S(1)}, u32[]{:S(2)}, u32[]{:S(2)}) collective-permute-start(f32[176,128]{1,0:T(8,128)S(1)} %get-tuple-element.25), channel_id=1, source_target_pairs={{0,1},{2,3},{1,0},{3,2},{4,5},{6,7},{5,4},{7,6},{8,9},{10,11},{9,8... | collective-permute-start | bytes 270344 | tf_op jit(solution)/shard_map/ppermute | solution.py:521
  48.3 3.7 %copy-start.4 = (f32[8]{0:T(128)S(1)}, f32[8]{0:T(128)}, u32[]{:S(2)}) copy-start(f32[8]{0:T(128)} %weight_ref.1) | copy-start | bytes 100
  48.3 3.7 %collective-permute-start.10 = (f32[176,128]{1,0:T(8,128)S(1)}, f32[176,128]{1,0:T(8,128)S(1)}, u32[]{:S(2)}, u32[]{:S(2)}) collective-permute-start(f32[176,128]{1,0:T(8,128)S(1)} %get-tuple-element.26), channel_id=1, source_target_pairs={{1,2},{2,1},{5,6},{6,5},{9,10},{10,9},{13,14},{14,13},{17,18},{18,... | collective-permute-start | bytes 270344 | tf_op jit(solution)/shard_map/ppermute | solution.py:521
  71.5 39.3 %copy-start.2 = (f32[32,1024]{1,0:T(8,128)S(1)}, f32[32,1024]{1,0:T(8,128)}, u32[]{:S(2)}) copy-start(f32[32,1024]{1,0:T(8,128)} %param.6) | copy-start | bytes 393220

commit v4 on v3

--- a/solution.py
+++ b/solution.py
@@ -101,19 +101,16 @@
 
 
 def spread_kernel(cells_ref, instance_ref, out_ref, named_ref):
-    own = cells_ref.shape[0]
-    for c in range(own // 8):
-        tile = cells_ref[pl.ds((c // 8) * 64 + c % 8, 8, stride=8), :]
-        for d in range(out_ref.shape[0] // own):
-            out_ref[d * own + c * 8 : d * own + c * 8 + 8, :] = tile
+    for c in range(out_ref.shape[0] // 8):
+        out_ref[c * 8 : c * 8 + 8, :] = cells_ref[pl.ds((c // 8) * 64 + c % 8, 8, stride=8), :]
     rows = [instance_ref[a : a + 1, :] for a in range(instance_ref.shape[0])]
     named_ref[...] = jnp.concatenate(rows, axis=1)
 
 
-def pack_kernel(asked_ref, me_ref, cells_ref, *rest):
+def pack_kernel(asked_ref, me_ref, *rest):
     out_ref, stage_ref, sems = rest[-3:]
-    peers, capacity = asked_ref.shape
-    chunk = capacity * 8
+    peers, planes, capacity = asked_ref.shape
+    chunk = planes * capacity * 8
 
     def send(i):
         rows = pl.ds(pl.multiple_of((me_ref[0] ^ i) * chunk, chunk), chunk)
@@ -121,11 +118,13 @@
 
     @pl.loop(0, peers)
     def _(i):
-        base = (me_ref[0] ^ i) * capacity
-        for j in range(capacity):
-            asked = jnp.maximum(asked_ref[i, j], 0)
-            tile = cells_ref[pl.ds(pl.multiple_of(asked * 8, 8), 8), :]
-            stage_ref[pl.ds(pl.multiple_of((base + j) * 8, 8), 8), :] = tile
+        base = (me_ref[0] ^ i) * planes * capacity
+        for e in range(planes):
+            for j in range(capacity):
+                asked = jnp.maximum(asked_ref[i, e, j], 0)
+                tile = rest[e][pl.ds(pl.multiple_of(asked * 8, 8), 8), :]
+                there = (base + e * capacity + j) * 8
+                stage_ref[pl.ds(pl.multiple_of(there, 8), 8), :] = tile
         send(i).start()
 
     @pl.loop(0, peers)
@@ -171,8 +170,10 @@
         strip(row, ref, slice(start, start + 16), row // quarter, row % quarter)
 
 
-def assemble_kernel(index_ref, spot_ref, tiles_ref, mask_ref, rowa_ref, rowb_ref, turned_ref):
+def assemble_kernel(index_ref, spot_ref, near_ref, far_ref, mask_ref, *rest):
+    rowa_ref, rowb_ref, turned_ref = rest
     odd_row = spot_ref[6] > 0
+    tiles = near_ref.shape[0] // 8
     tile_rows, tile_cols = index_ref.shape
     height = tile_rows * TILE
     wide = 2 * HALF
@@ -182,10 +183,12 @@
     @pl.loop(0, tile_rows)
     def _(a):
         for g in range(groups):
-            parts = [
-                tiles_ref[pl.ds(pl.multiple_of(index_ref[a, 4 * g + b] * 8, 8), 8), :]
-                for b in range(4)
-            ]
+            parts = []
+            for b in range(4):
+                index = index_ref[a, 4 * g + b]
+                far = index >= tiles
+                there = pl.ds(pl.multiple_of(jnp.where(far, index - tiles, index) * 8, 8), 8)
+                parts.append(jnp.where(far, far_ref[there, :], near_ref[there, :]))
             for s, piece in enumerate(transpose_blocks(parts, block)):
                 turned_ref[pl.ds(g * height + a * TILE + s, 8, stride=4), :] = piece
 
@@ -549,24 +552,21 @@
     height, breadth = target.shape
     owners = deep * peers
     capacity = 2 * ((tiles_here + owners - 1) // owners)
-    wide_capacity = min(tiles_here, deep * capacity)
     f32 = lambda *shape: jax.ShapeDtypeStruct(shape, F32)
 
     flat = to_rows(cells)
-    copies, named = kernel_call(
+    ordered, named = kernel_call(
         spread_kernel,
         "spread",
-        [
-            f32(deep * slots * 8, LANES),
-            jax.ShapeDtypeStruct((1, tiles_here), jnp.int32),
-        ],
+        [f32(slots * 8, LANES), jax.ShapeDtypeStruct((1, tiles_here), jnp.int32)],
         [],
         [],
         [flat, instance_cell],
     )
-    stack = lax.all_to_all(copies, "deep", split_axis=0, concat_axis=0, tiled=True)
-
     near = doubled(doubled(named, "col"), "core")
+    levels = [ordered]
+    for e in range(1, deep):
+        levels.append(lax.ppermute(ordered, "deep", [(i, i ^ e) for i in range(deep)]))
     row_axes = ("deep", "core")
     my_row, my_col = lax.axis_index(row_axes), lax.axis_index("col")
     me = jnp.stack(
@@ -581,32 +581,41 @@
             my_col % 2,
         ]
     ).astype(jnp.int32)
-    owner = near // slots
+    my_deep = lax.axis_index("deep")
+    planes = deep // 2
+    here = ((my_deep ^ jnp.arange(deep)) * peers + me[0])[None, :, None]
+    match = (near // slots)[:, None, :] == here
+    slot = jnp.broadcast_to((near % slots)[:, None, :], match.shape)
     asked = requests(
-        owner % peers == me[0], (owner // peers) * slots + near % slots, wide_capacity
-    )
+        match.reshape(peers * deep, tiles_here), slot.reshape(peers * deep, tiles_here), capacity
+    ).reshape(peers, deep, capacity)
     waves = make_waves(row_taps, col_taps)
-    packed = kernel_call(
-        pack_kernel,
-        "pack",
-        f32(peers * wide_capacity * 8, LANES),
-        [
-            pltpu.VMEM((peers * wide_capacity * 8, LANES), F32),
-            pltpu.SemaphoreType.DMA((peers,)),
-        ],
-        [asked, me],
-        [stack],
-        [waves],
-        out_space=pl.ANY,
-    )
+    size = peers * planes * capacity * 8
+    packed = []
+    for half in range(2):
+        which = slice(half * planes, (half + 1) * planes)
+        packed.append(
+            kernel_call(
+                pack_kernel,
+                "pack",
+                f32(size, LANES),
+                [pltpu.VMEM((size, LANES), F32), pltpu.SemaphoreType.DMA((peers,))],
+                [asked[:, which], me],
+                levels[which],
+                [waves] if half else [],
+                out_space=pl.ANY,
+            )
+        )
     odd = me[6] > 0
     head, foot = target[:HALF], target[height - HALF :]
-    packed, near, one, other = lax.optimization_barrier(
-        (packed, near, jnp.where(odd, head, foot), jnp.where(odd, foot, head))
+    packed[1], near, one, other = lax.optimization_barrier(
+        (packed[1], near, jnp.where(odd, head, foot), jnp.where(odd, foot, head))
     )
     one, other = pairs(one, other, row_axes)
     above, below = jnp.where(odd, one, other), jnp.where(odd, other, one)
-    arrived = lax.all_to_all(packed, plane, split_axis=0, concat_axis=0, tiled=True)
+    arrived = [
+        lax.all_to_all(x, plane, split_axis=0, concat_axis=0, tiled=True) for x in packed
+    ]
 
     everything = doubled(near, "deep")
     wanted = requests(everything // slots == me[1], everything % slots, capacity)
@@ -618,6 +627,11 @@
         where = group * size + jnp.sum(same.astype(jnp.int32), axis=1)
         return where.reshape(tile_rows, tile_cols)
 
+    home = place(mine, capacity)
+    theirs = home // capacity
+    level = my_deep ^ (theirs // peers)
+    index = (level // planes * peers + theirs % peers) * planes + level % planes
+    index = index * capacity + home % capacity
     wide = 2 * HALF
     quarter = (height + wide) // 4
     edge = f32(height // 2 + wide + quarter, LANES)
@@ -626,8 +640,8 @@
         "assemble",
         [f32(height, breadth), f32(wide, breadth), f32(wide, breadth)],
         [pltpu.VMEM((height * (breadth // LANES), LANES), F32)],
-        [place(mine % peers, wide_capacity), me],
-        [arrived],
+        [index, me],
+        arrived,
     )
     rowa, rowb = pairs(rowa, rowb, row_axes)
     cola, colb = kernel_call(
@@ -660,7 +674,7 @@
             pltpu.VMEM((KERNELS, height, breadth + 128), BF16),
             pltpu.VMEM((height * (breadth // LANES), LANES), F32),
         ],
-        [place(mine, capacity), me, kernel_weight],
+        [home, me, kernel_weight],
         [mask, rowa, rowb, cola, colb, target, above, below, waves],
         megabytes=36,
     )

time: 114 us -> 115 us (level)
  waiting for transfers between devices: 20.7 us -> 16.6 us
  starting transfers between devices: 21.6 us -> 24 us
  other arithmetic: 2.46 us -> 3.88 us
    ppermute x0 -> x3, starting transfers between devices: none -> 5.64 us  [shards(): lax.ppermute(ordered, 'deep', [(i, i ^ e) for i in range(deep)])]
    all_to_all x2, starting transfers between devices: 10.2 us -> 7 us  [shards(): lax.all_to_all(x, plane, split_axis=0, concat_axis=0, tiled=True)]
    ppermute x5, waiting for transfers between devices: 6.47 us -> 3.93 us  [doubled(): got = lax.ppermute(table, axis, [(i, i ^ bit) for i in range(count)])]
    all_to_all x2, waiting for transfers between devices: 11.4 us -> 9.79 us  [shards(): lax.all_to_all(x, plane, split_axis=0, concat_axis=0, tiled=True)]
    pallas_call x6 -> x7, Pallas kernels: 26.3 us -> 27.2 us  [kernel_call(): pl.pallas_call(body, out_shape=outs, in_specs=[pl.BlockSpec(memory_space=...]
  transfers between devices with their start and end apart: 13 -> 16, of which waited for: 7 -> 6; matrix products, arithmetic and copies ran while one was open for 3% -> 4% of each run, Pallas kernels for 1% -> 4%
where the time goes in v4:
time: 115 us
  blocking collectives  40.2 us (35%)
  Pallas kernels  27.2 us (24%)
  starting transfers between devices  24 us (21%)
  waiting for transfers between devices  16.6 us (14%)
  other arithmetic  3.88 us (3%)
  local copies, waits for them, and re-layouts  2.55 us (2%)
    all_to_all x1, blocking collectives, shards(): lax.all_to_all(returned, everyone, split_axis=0, concat_axis=0, tiled=True)  40.2 us
    pallas_call x7, Pallas kernels, kernel_call(): pl.pallas_call(body, out_shape=outs, in_specs=[pl.BlockSpec(memory_space=...  27.2 us
    all_to_all x2, waiting for transfers between devices, shards(): lax.all_to_all(x, plane, split_axis=0, concat_axis=0, tiled=True)  9.79 us
    ppermute x5, starting transfers between devices, doubled(): got = lax.ppermute(table, axis, [(i, i ^ bit) for i in range(count)])  7.81 us
    all_to_all x2, starting transfers between devices, shards(): lax.all_to_all(x, plane, split_axis=0, concat_axis=0, tiled=True)  7 us
    ppermute x3, starting transfers between devices, shards(): lax.ppermute(ordered, 'deep', [(i, i ^ e) for i in range(deep)])  5.64 us
    ppermute x5, waiting for transfers between devices, doubled(): got = lax.ppermute(table, axis, [(i, i ^ bit) for i in range(count)])  3.93 us
    ppermute x6, starting transfers between devices, pairs(): out.append(lax.ppermute(x, axis, swap + [(j, i) for i, j in swap]))  3.53 us
  transfers between devices with their start and end apart: 16, of which 6 were waited for; matrix products, arithmetic and copies ran while one was open for 4% of the time, Pallas kernels for 4%

profile of v4, /device:TPU:0, one launch (start us, length us, event | category | flops | bytes accessed | tf_op | source)
XLA Modules:
  0.0 114.8 jit_solution(14879483895328993728)
XLA Ops:
  0.0 0.9 copy-done.1
  0.9 0.7 copy-done.3
  1.7 3.0 %collective-permute-start.7 = (f32[256,128]{1,0:T(8,128)S(1)}, f32[256,128]{1,0:T(8,128)S(1)}, u32[]{:S(2)}, u32[]{:S(2)}) collective-permute-start(f32[256,128]{1,0:T(8,128)S(1)} %get-tuple-element.17.rest_0_), channel_id=1, source_target_pairs={{0,8},{8,0},{16,24},{24,16},{1,9},{9,1},{17,25},{25,17},{2,10},{10... | collective-permute-start | bytes 393224 | tf_op jit(solution)/shard_map/ppermute | solution.py:569
  4.7 2.5 %collective-permute-start.4 = (f32[256,128]{1,0:T(8,128)S(1)}, f32[256,128]{1,0:T(8,128)S(1)}, u32[]{:S(2)}, u32[]{:S(2)}) collective-permute-start(f32[256,128]{1,0:T(8,128)S(1)} %get-tuple-element.17.rest_0_), channel_id=1, source_target_pairs={{0,24},{8,16},{16,8},{24,0},{1,25},{9,17},{17,9},{25,1},{2,26},{10... | collective-permute-start | bytes 393224 | tf_op jit(solution)/shard_map/ppermute | solution.py:569
  7.3 1.5 %collective-permute-start = (s32[1,128]{1,0:T(1,128)S(1)}, s32[1,128]{1,0:T(1,128)S(1)}, u32[]{:S(2)}, u32[]{:S(2)}) collective-permute-start(s32[1,128]{1,0:T(1,128)S(1)} %get-tuple-element.16), channel_id=1, source_target_pairs={{0,1},{1,0},{2,3},{3,2},{4,5},{5,4},{6,7},{7,6},{8,9},{9,8},{10,11... | collective-permute-start | bytes 1544 | tf_op jit(solution)/shard_map/ppermute | solution.py:532
  8.8 0.5 broadcast.317
  9.3 0.7 fusion.30
  10.0 1.0 slice_select_fusion
  11.4 1.6 %collective-permute-start.1 = (s32[2,128]{1,0:T(2,128)S(1)}, s32[2,128]{1,0:T(2,128)S(1)}, u32[]{:S(2)}, u32[]{:S(2)}) collective-permute-start(s32[2,128]{1,0:T(2,128)S(1)} %pad_add_fusion.3), channel_id=1, source_target_pairs={{0,2},{1,3},{2,0},{3,1},{4,6},{5,7},{6,4},{7,5},{8,10},{9,11},{10,... | collective-permute-start | bytes 3080 | tf_op jit(solution)/shard_map/ppermute | solution.py:532
  13.0 2.0 %collective-permute-done.1 = s32[2,128]{1,0:T(2,128)S(1)} collective-permute-done((s32[2,128]{1,0:T(2,128)S(1)}, s32[2,128]{1,0:T(2,128)S(1)}, u32[]{:S(2)}, u32[]{:S(2)}) %collective-permute-start.1) | collective-permute-done | bytes 1056 | tf_op jit(solution)/shard_map/ppermute | solution.py:532
  15.3 0.9 collective-permute-done.2
  16.6 0.6 select_reduce_fusion.1
  17.3 1.6 %pack.3 = f32[1024,128]{1,0:T(8,128)} custom-call(s32[8,2,8]{2,1,0:T(2,128)S(1)} %get-tuple-element.37.asked_ref, s32[8]{0:T(128)S(1)} %stack.27.me_ref.spot_ref, f32[256,128]{1,0:T(8,128)S(1)} %get-tuple-element.17.rest_0_, f32[256,128]{1,0:T(8,128)S(1)} %collective-permute-done.7.rest_1_), custom_call_target="tpu_custom_call" | custom-call | tf_op jit(solution)/shard_map/pack/pallas_call | solution.py:505
  18.9 3.5 %all-to-all-start = ((f32[8,128,128]{2,1,0:T(8,128)}), f32[8,128,128]{2,1,0:T(8,128)S(1)}, u32[]{:S(2)}, u32[]{:S(2)}) async-start(f32[8,128,128]{2,1,0:T(8,128)} %bitcast.14), calls=%async_computation | async-start | bytes 1048576 | tf_op jit(solution)/shard_map/all_to_all | solution.py:617
  22.6 1.6 %pack.2 = f32[1024,128]{1,0:T(8,128)} custom-call(s32[8,2,8]{2,1,0:T(2,128)S(1)} %get-tuple-element.38.asked_ref, s32[8]{0:T(128)S(1)} %stack.27.me_ref.spot_ref, f32[256,128]{1,0:T(8,128)S(1)} %collective-permute-done.3.rest_0_, f32[256,128]{1,0:T(8,128)S(1)} %collective-permute-done.4.rest_1_, f32[32,128]{1,0:T(8,128)S(1)} %select_maximum_fusion.rest_2_.wave_ref), custom_call_target="tpu_custom_call" | custom-call | tf_op jit(solution)/shard_map/pack/pallas_call | solution.py:505
  24.2 1.9 %collective-permute-start.5 = (s32[8,128]{1,0:T(8,128)S(1)}, s32[8,128]{1,0:T(8,128)S(1)}, u32[]{:S(2)}, u32[]{:S(2)}) collective-permute-start(s32[8,128]{1,0:T(8,128)S(1)} %get-tuple-element.18), channel_id=1, source_target_pairs={{0,8},{8,0},{16,24},{24,16},{1,9},{9,1},{17,25},{25,17},{2,10},{10... | collective-permute-start | bytes 12296 | tf_op jit(solution)/shard_map/ppermute | solution.py:532
  26.2 0.7 collective-permute-start.11
  26.9 1.0 collective-permute-done.5
  27.9 2.8 %collective-permute-start.6 = (s32[16,128]{1,0:T(8,128)S(1)}, s32[16,128]{1,0:T(8,128)S(1)}, u32[]{:S(2)}, u32[]{:S(2)}) collective-permute-start(s32[16,128]{1,0:T(8,128)S(1)} %pad_add_fusion), channel_id=1, source_target_pairs={{0,16},{8,24},{16,0},{24,8},{1,17},{9,25},{17,1},{25,9},{2,18},{10... | collective-permute-start | bytes 24584 | tf_op jit(solution)/shard_map/ppermute | solution.py:532
  30.7 0.9 all-to-all-done
  31.6 3.5 %all-to-all-start.1 = ((f32[8,128,128]{2,1,0:T(8,128)}), f32[8,128,128]{2,1,0:T(8,128)S(1)}, u32[]{:S(2)}, u32[]{:S(2)}) async-start(f32[8,128,128]{2,1,0:T(8,128)} %bitcast.16), calls=%async_computation.1 | async-start | bytes 1048576 | tf_op jit(solution)/shard_map/all_to_all | solution.py:617
  35.5 8.8 %all-to-all-done.1 = f32[8,128,128]{2,1,0:T(8,128)S(1)} async-done(((f32[8,128,128]{2,1,0:T(8,128)}), f32[8,128,128]{2,1,0:T(8,128)S(1)}, u32[]{:S(2)}, u32[]{:S(2)}) %all-to-all-start.1) | async-done | bytes 524320 | tf_op jit(solution)/shard_map/all_to_all | solution.py:617
  44.3 1.3 %assemble.1 = (f32[128,1024]{1,0:T(8,128)S(1)}, f32[64,1024]{1,0:T(8,128)S(1)}, f32[64,1024]{1,0:T(8,128)S(1)}) custom-call(s32[4,32]{1,0:T(4,128)S(1)} %get-tuple-element.27.index_ref, s32[8]{0:T(128)S(1)} %stack.27.me_ref.spot_ref, f32[1024,128]{1,0:T(8,128)S(1)} %bitcast.37, f32[1024,128]{1,0:T(8,128)S(1)} %bitcast.38), custom_call_target="tpu_custom_call" | custom-call | tf_op jit(solution)/shard_map/assemble/pallas_call | solution.py:505
  46.0 0.7 collective-permute-start.9
  46.7 0.6 select_reduce_fusion.rest_0_.asked_ref
  47.4 0.7 edges.1
  48.1 0.9 collective-permute-start.12
  49.0 0.8 collective-permute-start.13
  49.8 2.9 %collective-permute-done.12.cola_ref = f32[176,128]{1,0:T(8,128)S(1)} collective-permute-done((f32[176,128]{1,0:T(8,128)S(1)}, f32[176,128]{1,0:T(8,128)S(1)}, u32[]{:S(2)}, u32[]{:S(2)}) %collective-permute-start.12) | collective-permute-done | bytes 90144 | tf_op jit(solution)/shard_map/ppermute | solution.py:524
  52.7 19.5 %image.1 = f32[2048,128]{1,0:T(8,128)S(1)} custom-call(s32[4,32]{1,0:T(4,128)S(1)} %get-tuple-element.28.index_ref, s32[8]{0:T(128)S(1)} %stack.27.me_ref.spot_ref, f32[8]{0:T(128)S(1)} %copy-done.4, f32[128,1024]{1,0:T(8,128)S(1)} %get-tuple-element.20.mask_ref, f32[64,1024]{1,0:T(8,128)S(1)} %collective-permute-done.8.rowa_ref, ...), custom_call_target="tpu_custom_call" | custom-call | tf_op jit(solution)/shard_map/image/pallas_call | solution.py:505
  72.2 40.2 %all_to_all.33 = f32[32,64,128]{2,1,0:T(8,128)S(1)} all-to-all(f32[32,64,128]{2,1,0:T(8,128)S(1)} %bitcast.35), channel_id=1, replica_groups=mesh['deep'=4,'core'=2,'col'=4] {'deep','core','col'}, dimensions={0} | all-to-all | bytes 2097152 | tf_op jit(solution)/shard_map/all_to_all | solution.py:681
  112.4 2.4 %step.1 = f32[256,128]{1,0:T(8,128)} custom-call(s32[32,8]{1,0:T(8,128)S(1)} %select_reduce_fusion.rest_0_.asked_ref, s32[8]{0:T(128)S(1)} %stack.27.me_ref.spot_ref, f32[256,128]{1,0:T(8,128)S(1)} %bitcast.40, f32[2048,128]{1,0:T(8,128)S(1)} %bitcast.36), custom_call_target="tpu_custom_call" | custom-call | tf_op jit(solution)/shard_map/step/pallas_call | solution.py:505
  (57 shorter events, 2.2 us)
Async XLA Ops:
  0.0 0.9 copy-start.1
  0.9 0.7 copy-start.3
  1.7 15.6 %collective-permute-start.7 = (f32[256,128]{1,0:T(8,128)S(1)}, f32[256,128]{1,0:T(8,128)S(1)}, u32[]{:S(2)}, u32[]{:S(2)}) collective-permute-start(f32[256,128]{1,0:T(8,128)S(1)} %get-tuple-element.17.rest_0_), channel_id=1, source_target_pairs={{0,8},{8,0},{16,24},{24,16},{1,9},{9,1},{17,25},{25,17},{2,10},{10... | collective-permute-start | bytes 393224 | tf_op jit(solution)/shard_map/ppermute | solution.py:569
  4.7 17.8 %collective-permute-start.4 = (f32[256,128]{1,0:T(8,128)S(1)}, f32[256,128]{1,0:T(8,128)S(1)}, u32[]{:S(2)}, u32[]{:S(2)}) collective-permute-start(f32[256,128]{1,0:T(8,128)S(1)} %get-tuple-element.17.rest_0_), channel_id=1, source_target_pairs={{0,24},{8,16},{16,8},{24,0},{1,25},{9,17},{17,9},{25,1},{2,26},{10... | collective-permute-start | bytes 393224 | tf_op jit(solution)/shard_map/ppermute | solution.py:569
  7.2 15.4 %collective-permute-start.3 = (f32[256,128]{1,0:T(8,128)S(1)}, f32[256,128]{1,0:T(8,128)S(1)}, u32[]{:S(2)}, u32[]{:S(2)}) collective-permute-start(f32[256,128]{1,0:T(8,128)S(1)} %get-tuple-element.17.rest_0_), channel_id=1, source_target_pairs={{0,16},{8,24},{16,0},{24,8},{1,17},{9,25},{17,1},{25,9},{2,18},{10... | collective-permute-start | bytes 393224 | tf_op jit(solution)/shard_map/ppermute | solution.py:569
  7.3 4.0 %collective-permute-start = (s32[1,128]{1,0:T(1,128)S(1)}, s32[1,128]{1,0:T(1,128)S(1)}, u32[]{:S(2)}, u32[]{:S(2)}) collective-permute-start(s32[1,128]{1,0:T(1,128)S(1)} %get-tuple-element.16), channel_id=1, source_target_pairs={{0,1},{1,0},{2,3},{3,2},{4,5},{5,4},{6,7},{7,6},{8,9},{9,8},{10,11... | collective-permute-start | bytes 1544 | tf_op jit(solution)/shard_map/ppermute | solution.py:532
  11.4 3.6 %collective-permute-start.1 = (s32[2,128]{1,0:T(2,128)S(1)}, s32[2,128]{1,0:T(2,128)S(1)}, u32[]{:S(2)}, u32[]{:S(2)}) collective-permute-start(s32[2,128]{1,0:T(2,128)S(1)} %pad_add_fusion.3), channel_id=1, source_target_pairs={{0,2},{1,3},{2,0},{3,1},{4,6},{5,7},{6,4},{7,5},{8,10},{9,11},{10,... | collective-permute-start | bytes 3080 | tf_op jit(solution)/shard_map/ppermute | solution.py:532
  15.0 1.2 %collective-permute-start.2 = (s32[4,128]{1,0:T(4,128)S(1)}, s32[4,128]{1,0:T(4,128)S(1)}, u32[]{:S(2)}, u32[]{:S(2)}) collective-permute-start(s32[4,128]{1,0:T(4,128)S(1)} %pad_add_fusion.2), channel_id=1, source_target_pairs={{0,4},{4,0},{1,5},{5,1},{2,6},{6,2},{3,7},{7,3},{8,12},{12,8},{9,1... | collective-permute-start | bytes 6152 | tf_op jit(solution)/shard_map/ppermute | solution.py:532
  18.9 3.5 %copy-start.5 = (f32[8,65]{1,0:T(8,128)S(1)}, f32[8,65]{1,0:T(8,128)}, u32[]{:S(2)}) copy-start(f32[8,65]{1,0:T(8,128)} %param.10) | copy-start | bytes 6244
  18.9 3.5 %copy-start.6 = (f32[8,65]{1,0:T(8,128)S(1)}, f32[8,65]{1,0:T(8,128)}, u32[]{:S(2)}) copy-start(f32[8,65]{1,0:T(8,128)} %param.9) | copy-start | bytes 6244
  18.9 12.7 %all-to-all-start = ((f32[8,128,128]{2,1,0:T(8,128)}), f32[8,128,128]{2,1,0:T(8,128)S(1)}, u32[]{:S(2)}, u32[]{:S(2)}) async-start(f32[8,128,128]{2,1,0:T(8,128)} %bitcast.14), calls=%async_computation | async-start | bytes 1048576 | tf_op jit(solution)/shard_map/all_to_all | solution.py:617
  24.2 3.7 %collective-permute-start.5 = (s32[8,128]{1,0:T(8,128)S(1)}, s32[8,128]{1,0:T(8,128)S(1)}, u32[]{:S(2)}, u32[]{:S(2)}) collective-permute-start(s32[8,128]{1,0:T(8,128)S(1)} %get-tuple-element.18), channel_id=1, source_target_pairs={{0,8},{8,0},{16,24},{24,16},{1,9},{9,1},{17,25},{25,17},{2,10},{10... | collective-permute-start | bytes 12296 | tf_op jit(solution)/shard_map/ppermute | solution.py:532
  26.0 21.3 %collective-permute-start.10 = (f32[32,1024]{1,0:T(8,128)S(1)}, f32[32,1024]{1,0:T(8,128)S(1)}, u32[]{:S(2)}, u32[]{:S(2)}) collective-permute-start(f32[32,1024]{1,0:T(8,128)S(1)} %get-tuple-element.23), channel_id=1, source_target_pairs={{0,4},{8,12},{16,20},{24,28},{4,0},{12,8},{20,16},{28,24},{1,5},{9... | collective-permute-start | bytes 393224 | tf_op jit(solution)/shard_map/ppermute | solution.py:524
  26.2 21.1 %collective-permute-start.11 = (f32[32,1024]{1,0:T(8,128)S(1)}, f32[32,1024]{1,0:T(8,128)S(1)}, u32[]{:S(2)}, u32[]{:S(2)}) collective-permute-start(f32[32,1024]{1,0:T(8,128)S(1)} %get-tuple-element.24), channel_id=1, source_target_pairs={{4,8},{12,16},{20,24},{8,4},{16,12},{24,20},{5,9},{13,17},{21,25},... | collective-permute-start | bytes 393224 | tf_op jit(solution)/shard_map/ppermute | solution.py:524
  27.9 7.3 %collective-permute-start.6 = (s32[16,128]{1,0:T(8,128)S(1)}, s32[16,128]{1,0:T(8,128)S(1)}, u32[]{:S(2)}, u32[]{:S(2)}) collective-permute-start(s32[16,128]{1,0:T(8,128)S(1)} %pad_add_fusion), channel_id=1, source_target_pairs={{0,16},{8,24},{16,0},{24,8},{1,17},{9,25},{17,1},{25,9},{2,18},{10... | collective-permute-start | bytes 24584 | tf_op jit(solution)/shard_map/ppermute | solution.py:532
  31.6 12.7 %all-to-all-start.1 = ((f32[8,128,128]{2,1,0:T(8,128)}), f32[8,128,128]{2,1,0:T(8,128)S(1)}, u32[]{:S(2)}, u32[]{:S(2)}) async-start(f32[8,128,128]{2,1,0:T(8,128)} %bitcast.16), calls=%async_computation.1 | async-start | bytes 1048576 | tf_op jit(solution)/shard_map/all_to_all | solution.py:617
  45.6 1.7 %copy-start = (f32[128,1024]{1,0:T(8,128)S(1)}, f32[128,1024]{1,0:T(8,128)}, u32[]{:S(2)}) copy-start(f32[128,1024]{1,0:T(8,128)} %own_ref.1) | copy-start | bytes 1572868
  45.6 1.7 %collective-permute-start.8 = (f32[64,1024]{1,0:T(8,128)S(1)}, f32[64,1024]{1,0:T(8,128)S(1)}, u32[]{:S(2)}, u32[]{:S(2)}) collective-permute-start(f32[64,1024]{1,0:T(8,128)S(1)} %get-tuple-element.21), channel_id=1, source_target_pairs={{0,4},{8,12},{16,20},{24,28},{4,0},{12,8},{20,16},{28,24},{1,5},{9... | collective-permute-start | bytes 786440 | tf_op jit(solution)/shard_map/ppermute | solution.py:524
  46.0 1.4 %collective-permute-start.9 = (f32[64,1024]{1,0:T(8,128)S(1)}, f32[64,1024]{1,0:T(8,128)S(1)}, u32[]{:S(2)}, u32[]{:S(2)}) collective-permute-start(f32[64,1024]{1,0:T(8,128)S(1)} %get-tuple-element.22), channel_id=1, source_target_pairs={{4,8},{12,16},{20,24},{8,4},{16,12},{24,20},{5,9},{13,17},{21,25},... | collective-permute-start | bytes 786440 | tf_op jit(solution)/shard_map/ppermute | solution.py:524
  48.1 4.6 %collective-permute-start.12 = (f32[176,128]{1,0:T(8,128)S(1)}, f32[176,128]{1,0:T(8,128)S(1)}, u32[]{:S(2)}, u32[]{:S(2)}) collective-permute-start(f32[176,128]{1,0:T(8,128)S(1)} %get-tuple-element.25), channel_id=1, source_target_pairs={{0,1},{2,3},{1,0},{3,2},{4,5},{6,7},{5,4},{7,6},{8,9},{10,11},{9,8... | collective-permute-start | bytes 270344 | tf_op jit(solution)/shard_map/ppermute | solution.py:524
  49.0 3.7 %copy-start.4 = (f32[8]{0:T(128)S(1)}, f32[8]{0:T(128)}, u32[]{:S(2)}) copy-start(f32[8]{0:T(128)} %weight_ref.1) | copy-start | bytes 100
  49.0 3.7 %collective-permute-start.13 = (f32[176,128]{1,0:T(8,128)S(1)}, f32[176,128]{1,0:T(8,128)S(1)}, u32[]{:S(2)}, u32[]{:S(2)}) collective-permute-start(f32[176,128]{1,0:T(8,128)S(1)} %get-tuple-element.26), channel_id=1, source_target_pairs={{1,2},{2,1},{5,6},{6,5},{9,10},{10,9},{13,14},{14,13},{17,18},{18,... | collective-permute-start | bytes 270344 | tf_op jit(solution)/shard_map/ppermute | solution.py:524
  72.2 40.2 %copy-start.2 = (f32[32,1024]{1,0:T(8,128)S(1)}, f32[32,1024]{1,0:T(8,128)}, u32[]{:S(2)}) copy-start(f32[32,1024]{1,0:T(8,128)} %param.6) | copy-start | bytes 393220

commit v5 on v4

--- a/solution.py
+++ b/solution.py
@@ -170,10 +170,8 @@
         strip(row, ref, slice(start, start + 16), row // quarter, row % quarter)
 
 
-def assemble_kernel(index_ref, spot_ref, near_ref, far_ref, mask_ref, *rest):
-    rowa_ref, rowb_ref, turned_ref = rest
+def assemble_kernel(index_ref, spot_ref, tiles_ref, mask_ref, rowa_ref, rowb_ref, turned_ref):
     odd_row = spot_ref[6] > 0
-    tiles = near_ref.shape[0] // 8
     tile_rows, tile_cols = index_ref.shape
     height = tile_rows * TILE
     wide = 2 * HALF
@@ -183,12 +181,10 @@
     @pl.loop(0, tile_rows)
     def _(a):
         for g in range(groups):
-            parts = []
-            for b in range(4):
-                index = index_ref[a, 4 * g + b]
-                far = index >= tiles
-                there = pl.ds(pl.multiple_of(jnp.where(far, index - tiles, index) * 8, 8), 8)
-                parts.append(jnp.where(far, far_ref[there, :], near_ref[there, :]))
+            parts = [
+                tiles_ref[pl.ds(pl.multiple_of(index_ref[a, 4 * g + b] * 8, 8), 8), :]
+                for b in range(4)
+            ]
             for s, piece in enumerate(transpose_blocks(parts, block)):
                 turned_ref[pl.ds(g * height + a * TILE + s, 8, stride=4), :] = piece
 
@@ -582,7 +578,6 @@
         ]
     ).astype(jnp.int32)
     my_deep = lax.axis_index("deep")
-    planes = deep // 2
     here = ((my_deep ^ jnp.arange(deep)) * peers + me[0])[None, :, None]
     match = (near // slots)[:, None, :] == here
     slot = jnp.broadcast_to((near % slots)[:, None, :], match.shape)
@@ -590,32 +585,25 @@
         match.reshape(peers * deep, tiles_here), slot.reshape(peers * deep, tiles_here), capacity
     ).reshape(peers, deep, capacity)
     waves = make_waves(row_taps, col_taps)
-    size = peers * planes * capacity * 8
-    packed = []
-    for half in range(2):
-        which = slice(half * planes, (half + 1) * planes)
-        packed.append(
-            kernel_call(
-                pack_kernel,
-                "pack",
-                f32(size, LANES),
-                [pltpu.VMEM((size, LANES), F32), pltpu.SemaphoreType.DMA((peers,))],
-                [asked[:, which], me],
-                levels[which],
-                [waves] if half else [],
-                out_space=pl.ANY,
-            )
-        )
+    size = peers * deep * capacity * 8
+    packed = kernel_call(
+        pack_kernel,
+        "pack",
+        f32(size, LANES),
+        [pltpu.VMEM((size, LANES), F32), pltpu.SemaphoreType.DMA((peers,))],
+        [asked, me],
+        levels,
+        [waves],
+        out_space=pl.ANY,
+    )
     odd = me[6] > 0
     head, foot = target[:HALF], target[height - HALF :]
-    packed[1], near, one, other = lax.optimization_barrier(
-        (packed[1], near, jnp.where(odd, head, foot), jnp.where(odd, foot, head))
+    packed, near, one, other = lax.optimization_barrier(
+        (packed, near, jnp.where(odd, head, foot), jnp.where(odd, foot, head))
     )
     one, other = pairs(one, other, row_axes)
     above, below = jnp.where(odd, one, other), jnp.where(odd, other, one)
-    arrived = [
-        lax.all_to_all(x, plane, split_axis=0, concat_axis=0, tiled=True) for x in packed
-    ]
+    arrived = lax.all_to_all(packed, plane, split_axis=0, concat_axis=0, tiled=True)
 
     everything = doubled(near, "deep")
     wanted = requests(everything // slots == me[1], everything % slots, capacity)
@@ -630,8 +618,7 @@
     home = place(mine, capacity)
     theirs = home // capacity
     level = my_deep ^ (theirs // peers)
-    index = (level // planes * peers + theirs % peers) * planes + level % planes
-    index = index * capacity + home % capacity
+    index = (theirs % peers * deep + level) * capacity + home % capacity
     wide = 2 * HALF
     quarter = (height + wide) // 4
     edge = f32(height // 2 + wide + quarter, LANES)
@@ -641,7 +628,7 @@
         [f32(height, breadth), f32(wide, breadth), f32(wide, breadth)],
         [pltpu.VMEM((height * (breadth // LANES), LANES), F32)],
         [index, me],
-        arrived,
+        [arrived],
     )
     rowa, rowb = pairs(rowa, rowb, row_axes)
     cola, colb = kernel_call(

time: 115 us -> 109 us (0.948)
  starting transfers between devices: 24 us -> 19.3 us
  Pallas kernels: 27.2 us -> 25.8 us
    all_to_all x2 -> x1, waiting for transfers between devices: 9.79 us -> 5.65 us  [shards(): lax.all_to_all(packed, plane, split_axis=0, concat_axis=0, tiled=True)]
    ppermute x5, waiting for transfers between devices: 3.93 us -> 7.88 us  [doubled(): got = lax.ppermute(table, axis, [(i, i ^ bit) for i in range(count)])]
    all_to_all x2 -> x1, starting transfers between devices: 7 us -> 3.74 us  [shards(): lax.all_to_all(packed, plane, split_axis=0, concat_axis=0, tiled=True)]
    ppermute x5, starting transfers between devices: 7.81 us -> 6.27 us  [doubled(): got = lax.ppermute(table, axis, [(i, i ^ bit) for i in range(count)])]
    pallas_call x7 -> x6, Pallas kernels: 27.2 us -> 25.8 us  [kernel_call(): pl.pallas_call(body, out_shape=outs, in_specs=[pl.BlockSpec(memory_space=...]
  transfers between devices with their start and end apart: 16 -> 15, of which waited for: 6 -> 7; matrix products, arithmetic and copies ran while one was open for 4% -> 4% of each run, Pallas kernels for 4% -> 1%
where the time goes in v5:
time: 109 us
  blocking collectives  40.3 us (37%)
  Pallas kernels  25.8 us (24%)
  starting transfers between devices  19.3 us (18%)
  waiting for transfers between devices  16.8 us (15%)
  other arithmetic  3.87 us (4%)
  local copies, waits for them, and re-layouts  2.54 us (2%)
    all_to_all x1, blocking collectives, shards(): lax.all_to_all(returned, everyone, split_axis=0, concat_axis=0, tiled=True)  40.3 us
    pallas_call x6, Pallas kernels, kernel_call(): pl.pallas_call(body, out_shape=outs, in_specs=[pl.BlockSpec(memory_space=...  25.8 us
    ppermute x5, waiting for transfers between devices, doubled(): got = lax.ppermute(table, axis, [(i, i ^ bit) for i in range(count)])  7.88 us
    ppermute x5, starting transfers between devices, doubled(): got = lax.ppermute(table, axis, [(i, i ^ bit) for i in range(count)])  6.27 us
    ppermute x3, starting transfers between devices, shards(): lax.ppermute(ordered, 'deep', [(i, i ^ e) for i in range(deep)])  5.72 us
    all_to_all x1, waiting for transfers between devices, shards(): lax.all_to_all(packed, plane, split_axis=0, concat_axis=0, tiled=True)  5.65 us
    all_to_all x1, starting transfers between devices, shards(): lax.all_to_all(packed, plane, split_axis=0, concat_axis=0, tiled=True)  3.74 us
    ppermute x6, starting transfers between devices, pairs(): out.append(lax.ppermute(x, axis, swap + [(j, i) for i, j in swap]))  3.55 us
  transfers between devices with their start and end apart: 15, of which 7 were waited for; matrix products, arithmetic and copies ran while one was open for 4% of the time, Pallas kernels for 1%

profile of v5, /device:TPU:0, one launch (start us, length us, event | category | flops | bytes accessed | tf_op | source)
XLA Modules:
  0.0 108.8 jit_solution(6499690155096716532)
XLA Ops:
  0.0 0.9 copy-done.1
  0.9 0.7 copy-done.3
  1.7 5.1 %collective-permute-start.5 = (f32[256,128]{1,0:T(8,128)S(1)}, f32[256,128]{1,0:T(8,128)S(1)}, u32[]{:S(2)}, u32[]{:S(2)}) collective-permute-start(f32[256,128]{1,0:T(8,128)S(1)} %get-tuple-element.17.rest_0_), channel_id=1, source_target_pairs={{0,24},{8,16},{16,8},{24,0},{1,25},{9,17},{17,9},{25,1},{2,26},{10... | collective-permute-start | bytes 393224 | tf_op jit(solution)/shard_map/ppermute | solution.py:565
  6.7 0.6 collective-permute-start.3
  7.4 1.6 %collective-permute-start = (s32[1,128]{1,0:T(1,128)S(1)}, s32[1,128]{1,0:T(1,128)S(1)}, u32[]{:S(2)}, u32[]{:S(2)}) collective-permute-start(s32[1,128]{1,0:T(1,128)S(1)} %get-tuple-element.16), channel_id=1, source_target_pairs={{0,1},{1,0},{2,3},{3,2},{4,5},{5,4},{6,7},{7,6},{8,9},{9,8},{10,11... | collective-permute-start | bytes 1544 | tf_op jit(solution)/shard_map/ppermute | solution.py:528
  9.0 0.5 broadcast.308
  9.6 0.7 fusion.25
  10.2 1.0 slice_select_fusion
  11.5 1.6 %collective-permute-start.1 = (s32[2,128]{1,0:T(2,128)S(1)}, s32[2,128]{1,0:T(2,128)S(1)}, u32[]{:S(2)}, u32[]{:S(2)}) collective-permute-start(s32[2,128]{1,0:T(2,128)S(1)} %pad_add_fusion.3), channel_id=1, source_target_pairs={{0,2},{1,3},{2,0},{3,1},{4,6},{5,7},{6,4},{7,5},{8,10},{9,11},{10,... | collective-permute-start | bytes 3080 | tf_op jit(solution)/shard_map/ppermute | solution.py:528
  13.1 2.0 %collective-permute-done.1 = s32[2,128]{1,0:T(2,128)S(1)} collective-permute-done((s32[2,128]{1,0:T(2,128)S(1)}, s32[2,128]{1,0:T(2,128)S(1)}, u32[]{:S(2)}, u32[]{:S(2)}) %collective-permute-start.1) | collective-permute-done | bytes 1056 | tf_op jit(solution)/shard_map/ppermute | solution.py:528
  15.6 0.8 collective-permute-done.2
  16.8 0.6 select_reduce_fusion.1
  17.4 0.4 collective-permute-done.4.rest_2_
  17.8 2.0 %pack.1 = f32[2048,128]{1,0:T(8,128)} custom-call(s32[8,4,8]{2,1,0:T(4,128)S(1)} %bitcast.38, s32[8]{0:T(128)S(1)} %stack.27.me_ref.spot_ref, f32[256,128]{1,0:T(8,128)S(1)} %get-tuple-element.17.rest_0_, f32[256,128]{1,0:T(8,128)S(1)} %collective-permute-done.3.rest_1_, f32[256,128]{1,0:T(8,128)S(1)} %collective-permute-done.4.rest_2_, ...), custom_call_target="tpu_custom_call" | custom-call | tf_op jit(solution)/shard_map/pack/pallas_call | solution.py:501
  19.8 3.7 %all-to-all-start = ((f32[8,256,128]{2,1,0:T(8,128)}), f32[8,256,128]{2,1,0:T(8,128)S(1)}, u32[]{:S(2)}, u32[]{:S(2)}) async-start(f32[8,256,128]{2,1,0:T(8,128)} %bitcast.14), calls=%async_computation | async-start | bytes 2097152 | tf_op jit(solution)/shard_map/all_to_all | solution.py:606
  23.6 0.8 collective-permute-start.6
  24.5 0.7 collective-permute-start.11
  25.2 2.1 %collective-permute-done.6 = s32[8,128]{1,0:T(8,128)S(1)} collective-permute-done((s32[8,128]{1,0:T(8,128)S(1)}, s32[8,128]{1,0:T(8,128)S(1)}, u32[]{:S(2)}, u32[]{:S(2)}) %collective-permute-start.6) | collective-permute-done | bytes 4128 | tf_op jit(solution)/shard_map/ppermute | solution.py:528
  27.3 2.2 %collective-permute-start.7 = (s32[16,128]{1,0:T(8,128)S(1)}, s32[16,128]{1,0:T(8,128)S(1)}, u32[]{:S(2)}, u32[]{:S(2)}) collective-permute-start(s32[16,128]{1,0:T(8,128)S(1)} %pad_add_fusion), channel_id=1, source_target_pairs={{0,16},{8,24},{16,0},{24,8},{1,17},{9,25},{17,1},{25,9},{2,18},{10... | collective-permute-start | bytes 24584 | tf_op jit(solution)/shard_map/ppermute | solution.py:528
  29.5 3.0 %collective-permute-done.7 = s32[16,128]{1,0:T(8,128)S(1)} collective-permute-done((s32[16,128]{1,0:T(8,128)S(1)}, s32[16,128]{1,0:T(8,128)S(1)}, u32[]{:S(2)}, u32[]{:S(2)}) %collective-permute-start.7) | collective-permute-done | bytes 8224 | tf_op jit(solution)/shard_map/ppermute | solution.py:528
  32.8 5.6 %all-to-all-done = f32[8,256,128]{2,1,0:T(8,128)S(1)} async-done(((f32[8,256,128]{2,1,0:T(8,128)}), f32[8,256,128]{2,1,0:T(8,128)S(1)}, u32[]{:S(2)}, u32[]{:S(2)}) %all-to-all-start) | async-done | bytes 1048608 | tf_op jit(solution)/shard_map/all_to_all | solution.py:606
  38.4 1.1 %assemble.1 = (f32[128,1024]{1,0:T(8,128)S(1)}, f32[64,1024]{1,0:T(8,128)S(1)}, f32[64,1024]{1,0:T(8,128)S(1)}) custom-call(s32[4,32]{1,0:T(4,128)S(1)} %get-tuple-element.27.index_ref, s32[8]{0:T(128)S(1)} %stack.27.me_ref.spot_ref, f32[2048,128]{1,0:T(8,128)S(1)} %bitcast.34), custom_call_target="tpu_custom_call" | custom-call | tf_op jit(solution)/shard_map/assemble/pallas_call | solution.py:501
  39.6 0.4 collective-permute-start.8
  39.9 0.7 collective-permute-start.9
  40.6 0.6 select_reduce_fusion.rest_0_.asked_ref
  41.3 0.7 edges.1
  42.0 0.9 collective-permute-start.12
  42.9 0.8 collective-permute-start.13
  43.7 2.9 %collective-permute-done.12.cola_ref = f32[176,128]{1,0:T(8,128)S(1)} collective-permute-done((f32[176,128]{1,0:T(8,128)S(1)}, f32[176,128]{1,0:T(8,128)S(1)}, u32[]{:S(2)}, u32[]{:S(2)}) %collective-permute-start.12) | collective-permute-done | bytes 90144 | tf_op jit(solution)/shard_map/ppermute | solution.py:520
  46.6 19.5 %image.1 = f32[2048,128]{1,0:T(8,128)S(1)} custom-call(s32[4,32]{1,0:T(4,128)S(1)} %get-tuple-element.28.index_ref, s32[8]{0:T(128)S(1)} %stack.27.me_ref.spot_ref, f32[8]{0:T(128)S(1)} %copy-done.4, f32[128,1024]{1,0:T(8,128)S(1)} %get-tuple-element.20.mask_ref, f32[64,1024]{1,0:T(8,128)S(1)} %collective-permute-done.8.rowa_ref, ...), custom_call_target="tpu_custom_call" | custom-call | tf_op jit(solution)/shard_map/image/pallas_call | solution.py:501
  66.1 40.3 %all_to_all.22 = f32[32,64,128]{2,1,0:T(8,128)S(1)} all-to-all(f32[32,64,128]{2,1,0:T(8,128)S(1)} %bitcast.33), channel_id=1, replica_groups=mesh['deep'=4,'core'=2,'col'=4] {'deep','core','col'}, dimensions={0} | all-to-all | bytes 2097152 | tf_op jit(solution)/shard_map/all_to_all | solution.py:668
  106.4 2.4 %step.1 = f32[256,128]{1,0:T(8,128)} custom-call(s32[32,8]{1,0:T(8,128)S(1)} %select_reduce_fusion.rest_0_.asked_ref, s32[8]{0:T(128)S(1)} %stack.27.me_ref.spot_ref, f32[256,128]{1,0:T(8,128)S(1)} %bitcast.37, f32[2048,128]{1,0:T(8,128)S(1)} %bitcast.35), custom_call_target="tpu_custom_call" | custom-call | tf_op jit(solution)/shard_map/step/pallas_call | solution.py:501
  (53 shorter events, 1.7 us)
Async XLA Ops:
  0.0 0.9 copy-start.1
  0.9 0.7 copy-start.3
  1.7 15.8 %collective-permute-start.5 = (f32[256,128]{1,0:T(8,128)S(1)}, f32[256,128]{1,0:T(8,128)S(1)}, u32[]{:S(2)}, u32[]{:S(2)}) collective-permute-start(f32[256,128]{1,0:T(8,128)S(1)} %get-tuple-element.17.rest_0_), channel_id=1, source_target_pairs={{0,24},{8,16},{16,8},{24,0},{1,25},{9,17},{17,9},{25,1},{2,26},{10... | collective-permute-start | bytes 393224 | tf_op jit(solution)/shard_map/ppermute | solution.py:565
  6.7 11.1 %collective-permute-start.4 = (f32[256,128]{1,0:T(8,128)S(1)}, f32[256,128]{1,0:T(8,128)S(1)}, u32[]{:S(2)}, u32[]{:S(2)}) collective-permute-start(f32[256,128]{1,0:T(8,128)S(1)} %get-tuple-element.17.rest_0_), channel_id=1, source_target_pairs={{0,16},{8,24},{16,0},{24,8},{1,17},{9,25},{17,1},{25,9},{2,18},{10... | collective-permute-start | bytes 393224 | tf_op jit(solution)/shard_map/ppermute | solution.py:565
  6.7 11.1 %collective-permute-start.3 = (f32[256,128]{1,0:T(8,128)S(1)}, f32[256,128]{1,0:T(8,128)S(1)}, u32[]{:S(2)}, u32[]{:S(2)}) collective-permute-start(f32[256,128]{1,0:T(8,128)S(1)} %get-tuple-element.17.rest_0_), channel_id=1, source_target_pairs={{0,8},{8,0},{16,24},{24,16},{1,9},{9,1},{17,25},{25,17},{2,10},{10... | collective-permute-start | bytes 393224 | tf_op jit(solution)/shard_map/ppermute | solution.py:565
  7.4 4.1 %collective-permute-start = (s32[1,128]{1,0:T(1,128)S(1)}, s32[1,128]{1,0:T(1,128)S(1)}, u32[]{:S(2)}, u32[]{:S(2)}) collective-permute-start(s32[1,128]{1,0:T(1,128)S(1)} %get-tuple-element.16), channel_id=1, source_target_pairs={{0,1},{1,0},{2,3},{3,2},{4,5},{5,4},{6,7},{7,6},{8,9},{9,8},{10,11... | collective-permute-start | bytes 1544 | tf_op jit(solution)/shard_map/ppermute | solution.py:528
  10.2 1.2 %copy-start.5 = (f32[8,65]{1,0:T(8,128)S(1)}, f32[8,65]{1,0:T(8,128)}, u32[]{:S(2)}) copy-start(f32[8,65]{1,0:T(8,128)} %param.10) | copy-start | bytes 6244
  10.2 1.2 %copy-start.6 = (f32[8,65]{1,0:T(8,128)S(1)}, f32[8,65]{1,0:T(8,128)}, u32[]{:S(2)}) copy-start(f32[8,65]{1,0:T(8,128)} %param.9) | copy-start | bytes 6244
  11.5 3.6 %collective-permute-start.1 = (s32[2,128]{1,0:T(2,128)S(1)}, s32[2,128]{1,0:T(2,128)S(1)}, u32[]{:S(2)}, u32[]{:S(2)}) collective-permute-start(s32[2,128]{1,0:T(2,128)S(1)} %pad_add_fusion.3), channel_id=1, source_target_pairs={{0,2},{1,3},{2,0},{3,1},{4,6},{5,7},{6,4},{7,5},{8,10},{9,11},{10,... | collective-permute-start | bytes 3080 | tf_op jit(solution)/shard_map/ppermute | solution.py:528
  15.2 1.2 %collective-permute-start.2 = (s32[4,128]{1,0:T(4,128)S(1)}, s32[4,128]{1,0:T(4,128)S(1)}, u32[]{:S(2)}, u32[]{:S(2)}) collective-permute-start(s32[4,128]{1,0:T(4,128)S(1)} %pad_add_fusion.2), channel_id=1, source_target_pairs={{0,4},{4,0},{1,5},{5,1},{2,6},{6,2},{3,7},{7,3},{8,12},{12,8},{9,1... | collective-permute-start | bytes 6152 | tf_op jit(solution)/shard_map/ppermute | solution.py:528
  19.8 18.6 %all-to-all-start = ((f32[8,256,128]{2,1,0:T(8,128)}), f32[8,256,128]{2,1,0:T(8,128)S(1)}, u32[]{:S(2)}, u32[]{:S(2)}) async-start(f32[8,256,128]{2,1,0:T(8,128)} %bitcast.14), calls=%async_computation | async-start | bytes 2097152 | tf_op jit(solution)/shard_map/all_to_all | solution.py:606
  23.6 3.7 %collective-permute-start.6 = (s32[8,128]{1,0:T(8,128)S(1)}, s32[8,128]{1,0:T(8,128)S(1)}, u32[]{:S(2)}, u32[]{:S(2)}) collective-permute-start(s32[8,128]{1,0:T(8,128)S(1)} %get-tuple-element.18), channel_id=1, source_target_pairs={{0,8},{8,0},{16,24},{24,16},{1,9},{9,1},{17,25},{25,17},{2,10},{10... | collective-permute-start | bytes 12296 | tf_op jit(solution)/shard_map/ppermute | solution.py:528
  24.4 16.8 %collective-permute-start.10 = (f32[32,1024]{1,0:T(8,128)S(1)}, f32[32,1024]{1,0:T(8,128)S(1)}, u32[]{:S(2)}, u32[]{:S(2)}) collective-permute-start(f32[32,1024]{1,0:T(8,128)S(1)} %get-tuple-element.23), channel_id=1, source_target_pairs={{0,4},{8,12},{16,20},{24,28},{4,0},{12,8},{20,16},{28,24},{1,5},{9... | collective-permute-start | bytes 393224 | tf_op jit(solution)/shard_map/ppermute | solution.py:520
  24.5 16.7 %collective-permute-start.11 = (f32[32,1024]{1,0:T(8,128)S(1)}, f32[32,1024]{1,0:T(8,128)S(1)}, u32[]{:S(2)}, u32[]{:S(2)}) collective-permute-start(f32[32,1024]{1,0:T(8,128)S(1)} %get-tuple-element.24), channel_id=1, source_target_pairs={{4,8},{12,16},{20,24},{8,4},{16,12},{24,20},{5,9},{13,17},{21,25},... | collective-permute-start | bytes 393224 | tf_op jit(solution)/shard_map/ppermute | solution.py:520
  27.3 5.2 %collective-permute-start.7 = (s32[16,128]{1,0:T(8,128)S(1)}, s32[16,128]{1,0:T(8,128)S(1)}, u32[]{:S(2)}, u32[]{:S(2)}) collective-permute-start(s32[16,128]{1,0:T(8,128)S(1)} %pad_add_fusion), channel_id=1, source_target_pairs={{0,16},{8,24},{16,0},{24,8},{1,17},{9,25},{17,1},{25,9},{2,18},{10... | collective-permute-start | bytes 24584 | tf_op jit(solution)/shard_map/ppermute | solution.py:528
  39.6 1.7 %copy-start = (f32[128,1024]{1,0:T(8,128)S(1)}, f32[128,1024]{1,0:T(8,128)}, u32[]{:S(2)}) copy-start(f32[128,1024]{1,0:T(8,128)} %own_ref.1) | copy-start | bytes 1572868
  39.6 1.7 %collective-permute-start.8 = (f32[64,1024]{1,0:T(8,128)S(1)}, f32[64,1024]{1,0:T(8,128)S(1)}, u32[]{:S(2)}, u32[]{:S(2)}) collective-permute-start(f32[64,1024]{1,0:T(8,128)S(1)} %get-tuple-element.21), channel_id=1, source_target_pairs={{0,4},{8,12},{16,20},{24,28},{4,0},{12,8},{20,16},{28,24},{1,5},{9... | collective-permute-start | bytes 786440 | tf_op jit(solution)/shard_map/ppermute | solution.py:520
  39.9 1.4 %collective-permute-start.9 = (f32[64,1024]{1,0:T(8,128)S(1)}, f32[64,1024]{1,0:T(8,128)S(1)}, u32[]{:S(2)}, u32[]{:S(2)}) collective-permute-start(f32[64,1024]{1,0:T(8,128)S(1)} %get-tuple-element.22), channel_id=1, source_target_pairs={{4,8},{12,16},{20,24},{8,4},{16,12},{24,20},{5,9},{13,17},{21,25},... | collective-permute-start | bytes 786440 | tf_op jit(solution)/shard_map/ppermute | solution.py:520
  42.0 4.6 %collective-permute-start.12 = (f32[176,128]{1,0:T(8,128)S(1)}, f32[176,128]{1,0:T(8,128)S(1)}, u32[]{:S(2)}, u32[]{:S(2)}) collective-permute-start(f32[176,128]{1,0:T(8,128)S(1)} %get-tuple-element.25), channel_id=1, source_target_pairs={{0,1},{2,3},{1,0},{3,2},{4,5},{6,7},{5,4},{7,6},{8,9},{10,11},{9,8... | collective-permute-start | bytes 270344 | tf_op jit(solution)/shard_map/ppermute | solution.py:520
  42.9 3.7 %copy-start.4 = (f32[8]{0:T(128)S(1)}, f32[8]{0:T(128)}, u32[]{:S(2)}) copy-start(f32[8]{0:T(128)} %weight_ref.1) | copy-start | bytes 100
  42.9 3.7 %collective-permute-start.13 = (f32[176,128]{1,0:T(8,128)S(1)}, f32[176,128]{1,0:T(8,128)S(1)}, u32[]{:S(2)}, u32[]{:S(2)}) collective-permute-start(f32[176,128]{1,0:T(8,128)S(1)} %get-tuple-element.26), channel_id=1, source_target_pairs={{1,2},{2,1},{5,6},{6,5},{9,10},{10,9},{13,14},{14,13},{17,18},{18,... | collective-permute-start | bytes 270344 | tf_op jit(solution)/shard_map/ppermute | solution.py:520
  66.1 40.3 %copy-start.2 = (f32[32,1024]{1,0:T(8,128)S(1)}, f32[32,1024]{1,0:T(8,128)}, u32[]{:S(2)}) copy-start(f32[32,1024]{1,0:T(8,128)} %param.6) | copy-start | bytes 393220

commit v6 on v5

--- a/solution.py
+++ b/solution.py
@@ -138,14 +138,15 @@
     for total in totals:
         total[...] = jnp.zeros_like(total)
 
-    @pl.loop(0, owners)
-    def _(i):
-        base = (me_ref[1] ^ i) * capacity
-        for j in range(capacity):
+    @pl.loop(0, owners // 2)
+    def _(pair):
+        for n in range(2 * capacity):
+            i, j = pair * 2 + n // capacity, n % capacity
             asked = asked_ref[i, j]
-            tile = tiles_ref[pl.ds(pl.multiple_of((base + j) * 8, 8), 8), :]
+            place = ((me_ref[1] ^ i) * capacity + j) * 8
+            tile = tiles_ref[pl.ds(pl.multiple_of(place, 8), 8), :]
             there = pl.ds(pl.multiple_of(jnp.maximum(asked, 0) * 8, 8), 8)
-            total = totals[j % len(totals)]
+            total = totals[n % len(totals)]
             total[there, :] += jnp.where(asked >= 0, tile, nothing)
 
     for c in range(out_ref.shape[0] // 8):
@@ -444,35 +445,36 @@
 
     lower = lax.broadcasted_iota(jnp.int32, (rows_here, LANES), 1) < LANES // 2
 
-    def spread_back(k):
-        stacked = []
-        for jj in range(supers):
-            c0 = WIDE * jj
-            high = [ghigh_ref[k, :, c0 + LANES * n : c0 + LANES * (n + 1)] for n in range(3)]
-            turn = [gturn_ref[k, :, c0 + LANES * n : c0 + LANES * (n + 1)] for n in range(3)]
-            row = [
-                high[0],
-                high[1],
-                jnp.where(lower, high[2], turn[0]),
-                jnp.where(lower, turn[0], turn[1]),
-                jnp.where(lower, turn[1], turn[2]),
-                *high,
-            ]
-            stacked.append(jnp.concatenate(row, axis=1))
-        return mm(jnp.concatenate(stacked, axis=0), bcol_ref[k])
-
-    def add(part, fresh):
+    def windows_of(k, c0):
+        high = [ghigh_ref[k, :, c0 + LANES * n : c0 + LANES * (n + 1)] for n in range(3)]
+        turn = [gturn_ref[k, :, c0 + LANES * n : c0 + LANES * (n + 1)] for n in range(3)]
+        return [
+            high[0],
+            high[1],
+            jnp.where(lower, high[2], turn[0]),
+            jnp.where(lower, turn[0], turn[1]),
+            jnp.where(lower, turn[1], turn[2]),
+            *high,
+        ]
+
+    together = 4
+    grad_ref[...] = jnp.zeros_like(grad_ref)
+
+    @pl.loop(0, KERNELS // together)
+    def _(part_of):
+        ks = [part_of * together + n for n in range(together)]
+        stacked = [
+            jnp.concatenate([x for k in ks for x in windows_of(k, WIDE * jj)], axis=1)
+            for jj in range(supers)
+        ]
+        band = jnp.concatenate([bcol_ref[k] for k in ks], axis=0)
+        part = mm(jnp.concatenate(stacked, axis=0), band)
         for g in range(groups):
             rows = slice(g * rows_here, (g + 1) * rows_here)
             top = (g // 2) * rows_here
-            piece = part[top : top + rows_here, LANES * (g % 2) : LANES * (g % 2 + 1)]
-            grad_ref[rows, :] = piece if fresh else grad_ref[rows, :] + piece
-
-    add(spread_back(0), True)
-
-    @pl.loop(1, KERNELS)
-    def _(k):
-        add(spread_back(k), False)
+            grad_ref[rows, :] += part[
+                top : top + rows_here, LANES * (g % 2) : LANES * (g % 2 + 1)
+            ]
 
     @pl.loop(0, tile_rows)
     def _(a):
@@ -514,11 +516,13 @@
 
 def pairs(one, other, axis):
     count = lax.axis_size(axis)
-    out = []
-    for x, start in ((one, 0), (other, 1)):
+
+    def exchange(x, start):
         swap = [(i, i + 1) for i in range(start, count - 1, 2)]
-        out.append(lax.ppermute(x, axis, swap + [(j, i) for i, j in swap]))
-    return out
+        return lax.ppermute(x, axis, swap + [(j, i) for i, j in swap])
+
+    got = exchange(other, 1)
+    return exchange(one, 0), got
 
 
 def doubled(table, axis):
@@ -670,7 +674,7 @@
         step_kernel,
         "step",
         f32(slots * 8, LANES),
-        [pltpu.VMEM((slots * 8, LANES), F32)] * 4,
+        [pltpu.VMEM((slots * 8, LANES), F32)] * 8,
         [wanted, me],
         [flat, back],
     )

time: 109 us -> 108 us (level)
  Pallas kernels: 25.8 us -> 24.4 us
    pallas_call x6, Pallas kernels: 25.8 us -> 24.4 us  [kernel_call(): pl.pallas_call(body, out_shape=outs, in_specs=[pl.BlockSpec(memory_space=...]
where the time goes in v6:
time: 108 us; the launch traced here: 107 us
  blocking collectives  40.3 us (37%)
  Pallas kernels  24.4 us (23%)
  starting transfers between devices  19.3 us (18%)
  waiting for transfers between devices  16.8 us (16%)
  other arithmetic  3.87 us (4%)
  local copies, waits for them, and re-layouts  2.54 us (2%)
    all_to_all x1, blocking collectives, shards(): lax.all_to_all(returned, everyone, split_axis=0, concat_axis=0, tiled=True)  40.3 us
    pallas_call x6, Pallas kernels, kernel_call(): pl.pallas_call(body, out_shape=outs, in_specs=[pl.BlockSpec(memory_space=...  24.4 us
    ppermute x5, waiting for transfers between devices, doubled(): got = lax.ppermute(table, axis, [(i, i ^ bit) for i in range(count)])  7.88 us
    ppermute x5, starting transfers between devices, doubled(): got = lax.ppermute(table, axis, [(i, i ^ bit) for i in range(count)])  6.27 us
    ppermute x3, starting transfers between devices, shards(): lax.ppermute(ordered, 'deep', [(i, i ^ e) for i in range(deep)])  5.72 us
    all_to_all x1, waiting for transfers between devices, shards(): lax.all_to_all(packed, plane, split_axis=0, concat_axis=0, tiled=True)  5.65 us
    all_to_all x1, starting transfers between devices, shards(): lax.all_to_all(packed, plane, split_axis=0, concat_axis=0, tiled=True)  3.74 us
    ppermute x6, starting transfers between devices, exchange(): return lax.ppermute(x, axis, swap + [(j, i) for i, j in swap])  3.55 us
  transfers between devices with their start and end apart: 15, of which 7 were waited for; matrix products, arithmetic and copies ran while one was open for 4% of the time, Pallas kernels for 1%

profile of v6, /device:TPU:0, one launch (start us, length us, event | category | flops | bytes accessed | tf_op | source)
XLA Modules:
  0.0 107.5 jit_solution(12411228275089255722)
XLA Ops:
  0.0 0.9 copy-done.1
  0.9 0.7 copy-done.3
  1.7 5.1 %collective-permute-start.5 = (f32[256,128]{1,0:T(8,128)S(1)}, f32[256,128]{1,0:T(8,128)S(1)}, u32[]{:S(2)}, u32[]{:S(2)}) collective-permute-start(f32[256,128]{1,0:T(8,128)S(1)} %get-tuple-element.17.rest_0_), channel_id=1, source_target_pairs={{0,24},{8,16},{16,8},{24,0},{1,25},{9,17},{17,9},{25,1},{2,26},{10... | collective-permute-start | bytes 393224 | tf_op jit(solution)/shard_map/ppermute | solution.py:569
  6.7 0.6 collective-permute-start.3
  7.4 1.6 %collective-permute-start = (s32[1,128]{1,0:T(1,128)S(1)}, s32[1,128]{1,0:T(1,128)S(1)}, u32[]{:S(2)}, u32[]{:S(2)}) collective-permute-start(s32[1,128]{1,0:T(1,128)S(1)} %get-tuple-element.16), channel_id=1, source_target_pairs={{0,1},{1,0},{2,3},{3,2},{4,5},{5,4},{6,7},{7,6},{8,9},{9,8},{10,11... | collective-permute-start | bytes 1544 | tf_op jit(solution)/shard_map/ppermute | solution.py:532
  9.0 0.5 broadcast.308
  9.6 0.7 fusion.25
  10.2 1.0 slice_select_fusion
  11.5 1.6 %collective-permute-start.1 = (s32[2,128]{1,0:T(2,128)S(1)}, s32[2,128]{1,0:T(2,128)S(1)}, u32[]{:S(2)}, u32[]{:S(2)}) collective-permute-start(s32[2,128]{1,0:T(2,128)S(1)} %pad_add_fusion.3), channel_id=1, source_target_pairs={{0,2},{1,3},{2,0},{3,1},{4,6},{5,7},{6,4},{7,5},{8,10},{9,11},{10,... | collective-permute-start | bytes 3080 | tf_op jit(solution)/shard_map/ppermute | solution.py:532
  13.1 2.0 %collective-permute-done.1 = s32[2,128]{1,0:T(2,128)S(1)} collective-permute-done((s32[2,128]{1,0:T(2,128)S(1)}, s32[2,128]{1,0:T(2,128)S(1)}, u32[]{:S(2)}, u32[]{:S(2)}) %collective-permute-start.1) | collective-permute-done | bytes 1056 | tf_op jit(solution)/shard_map/ppermute | solution.py:532
  15.6 0.8 collective-permute-done.2
  16.8 0.6 select_reduce_fusion.1
  17.4 0.4 collective-permute-done.4.rest_2_
  17.8 2.0 %pack.1 = f32[2048,128]{1,0:T(8,128)} custom-call(s32[8,4,8]{2,1,0:T(4,128)S(1)} %bitcast.38, s32[8]{0:T(128)S(1)} %stack.27.me_ref.spot_ref, f32[256,128]{1,0:T(8,128)S(1)} %get-tuple-element.17.rest_0_, f32[256,128]{1,0:T(8,128)S(1)} %collective-permute-done.3.rest_1_, f32[256,128]{1,0:T(8,128)S(1)} %collective-permute-done.4.rest_2_, ...), custom_call_target="tpu_custom_call" | custom-call | tf_op jit(solution)/shard_map/pack/pallas_call | solution.py:503
  19.8 3.7 %all-to-all-start = ((f32[8,256,128]{2,1,0:T(8,128)}), f32[8,256,128]{2,1,0:T(8,128)S(1)}, u32[]{:S(2)}, u32[]{:S(2)}) async-start(f32[8,256,128]{2,1,0:T(8,128)} %bitcast.14), calls=%async_computation | async-start | bytes 2097152 | tf_op jit(solution)/shard_map/all_to_all | solution.py:610
  23.6 0.8 collective-permute-start.6
  24.5 0.7 collective-permute-start.11
  25.2 2.1 %collective-permute-done.6 = s32[8,128]{1,0:T(8,128)S(1)} collective-permute-done((s32[8,128]{1,0:T(8,128)S(1)}, s32[8,128]{1,0:T(8,128)S(1)}, u32[]{:S(2)}, u32[]{:S(2)}) %collective-permute-start.6) | collective-permute-done | bytes 4128 | tf_op jit(solution)/shard_map/ppermute | solution.py:532
  27.3 2.2 %collective-permute-start.7 = (s32[16,128]{1,0:T(8,128)S(1)}, s32[16,128]{1,0:T(8,128)S(1)}, u32[]{:S(2)}, u32[]{:S(2)}) collective-permute-start(s32[16,128]{1,0:T(8,128)S(1)} %pad_add_fusion), channel_id=1, source_target_pairs={{0,16},{8,24},{16,0},{24,8},{1,17},{9,25},{17,1},{25,9},{2,18},{10... | collective-permute-start | bytes 24584 | tf_op jit(solution)/shard_map/ppermute | solution.py:532
  29.5 3.0 %collective-permute-done.7 = s32[16,128]{1,0:T(8,128)S(1)} collective-permute-done((s32[16,128]{1,0:T(8,128)S(1)}, s32[16,128]{1,0:T(8,128)S(1)}, u32[]{:S(2)}, u32[]{:S(2)}) %collective-permute-start.7) | collective-permute-done | bytes 8224 | tf_op jit(solution)/shard_map/ppermute | solution.py:532
  32.8 5.6 %all-to-all-done = f32[8,256,128]{2,1,0:T(8,128)S(1)} async-done(((f32[8,256,128]{2,1,0:T(8,128)}), f32[8,256,128]{2,1,0:T(8,128)S(1)}, u32[]{:S(2)}, u32[]{:S(2)}) %all-to-all-start) | async-done | bytes 1048608 | tf_op jit(solution)/shard_map/all_to_all | solution.py:610
  38.4 1.1 %assemble.1 = (f32[128,1024]{1,0:T(8,128)S(1)}, f32[64,1024]{1,0:T(8,128)S(1)}, f32[64,1024]{1,0:T(8,128)S(1)}) custom-call(s32[4,32]{1,0:T(4,128)S(1)} %get-tuple-element.27.index_ref, s32[8]{0:T(128)S(1)} %stack.27.me_ref.spot_ref, f32[2048,128]{1,0:T(8,128)S(1)} %bitcast.34), custom_call_target="tpu_custom_call" | custom-call | tf_op jit(solution)/shard_map/assemble/pallas_call | solution.py:503
  39.6 0.4 collective-permute-start.8
  39.9 0.7 collective-permute-start.9
  40.6 0.6 select_reduce_fusion.rest_0_.asked_ref
  41.3 0.7 edges.1
  42.0 0.9 collective-permute-start.12
  42.9 0.8 collective-permute-start.13
  43.7 2.9 %collective-permute-done.12.cola_ref = f32[176,128]{1,0:T(8,128)S(1)} collective-permute-done((f32[176,128]{1,0:T(8,128)S(1)}, f32[176,128]{1,0:T(8,128)S(1)}, u32[]{:S(2)}, u32[]{:S(2)}) %collective-permute-start.12) | collective-permute-done | bytes 90144 | tf_op jit(solution)/shard_map/ppermute | solution.py:522
  46.6 18.2 %image.1 = f32[2048,128]{1,0:T(8,128)S(1)} custom-call(s32[4,32]{1,0:T(4,128)S(1)} %get-tuple-element.28.index_ref, s32[8]{0:T(128)S(1)} %stack.27.me_ref.spot_ref, f32[8]{0:T(128)S(1)} %copy-done.4, f32[128,1024]{1,0:T(8,128)S(1)} %get-tuple-element.20.mask_ref, f32[64,1024]{1,0:T(8,128)S(1)} %collective-permute-done.8.rowa_ref, ...), custom_call_target="tpu_custom_call" | custom-call | tf_op jit(solution)/shard_map/image/pallas_call | solution.py:503
  64.8 40.3 %all_to_all.22 = f32[32,64,128]{2,1,0:T(8,128)S(1)} all-to-all(f32[32,64,128]{2,1,0:T(8,128)S(1)} %bitcast.33), channel_id=1, replica_groups=mesh['deep'=4,'core'=2,'col'=4] {'deep','core','col'}, dimensions={0} | all-to-all | bytes 2097152 | tf_op jit(solution)/shard_map/all_to_all | solution.py:672
  105.1 2.4 %step.1 = f32[256,128]{1,0:T(8,128)} custom-call(s32[32,8]{1,0:T(8,128)S(1)} %select_reduce_fusion.rest_0_.asked_ref, s32[8]{0:T(128)S(1)} %stack.27.me_ref.spot_ref, f32[256,128]{1,0:T(8,128)S(1)} %bitcast.37, f32[2048,128]{1,0:T(8,128)S(1)} %bitcast.35), custom_call_target="tpu_custom_call" | custom-call | tf_op jit(solution)/shard_map/step/pallas_call | solution.py:503
  (53 shorter events, 1.7 us)
Async XLA Ops:
  0.0 0.9 copy-start.1
  0.9 0.7 copy-start.3
  1.7 15.8 %collective-permute-start.5 = (f32[256,128]{1,0:T(8,128)S(1)}, f32[256,128]{1,0:T(8,128)S(1)}, u32[]{:S(2)}, u32[]{:S(2)}) collective-permute-start(f32[256,128]{1,0:T(8,128)S(1)} %get-tuple-element.17.rest_0_), channel_id=1, source_target_pairs={{0,24},{8,16},{16,8},{24,0},{1,25},{9,17},{17,9},{25,1},{2,26},{10... | collective-permute-start | bytes 393224 | tf_op jit(solution)/shard_map/ppermute | solution.py:569
  6.7 11.1 %collective-permute-start.4 = (f32[256,128]{1,0:T(8,128)S(1)}, f32[256,128]{1,0:T(8,128)S(1)}, u32[]{:S(2)}, u32[]{:S(2)}) collective-permute-start(f32[256,128]{1,0:T(8,128)S(1)} %get-tuple-element.17.rest_0_), channel_id=1, source_target_pairs={{0,16},{8,24},{16,0},{24,8},{1,17},{9,25},{17,1},{25,9},{2,18},{10... | collective-permute-start | bytes 393224 | tf_op jit(solution)/shard_map/ppermute | solution.py:569
  6.7 11.1 %collective-permute-start.3 = (f32[256,128]{1,0:T(8,128)S(1)}, f32[256,128]{1,0:T(8,128)S(1)}, u32[]{:S(2)}, u32[]{:S(2)}) collective-permute-start(f32[256,128]{1,0:T(8,128)S(1)} %get-tuple-element.17.rest_0_), channel_id=1, source_target_pairs={{0,8},{8,0},{16,24},{24,16},{1,9},{9,1},{17,25},{25,17},{2,10},{10... | collective-permute-start | bytes 393224 | tf_op jit(solution)/shard_map/ppermute | solution.py:569
  7.4 4.1 %collective-permute-start = (s32[1,128]{1,0:T(1,128)S(1)}, s32[1,128]{1,0:T(1,128)S(1)}, u32[]{:S(2)}, u32[]{:S(2)}) collective-permute-start(s32[1,128]{1,0:T(1,128)S(1)} %get-tuple-element.16), channel_id=1, source_target_pairs={{0,1},{1,0},{2,3},{3,2},{4,5},{5,4},{6,7},{7,6},{8,9},{9,8},{10,11... | collective-permute-start | bytes 1544 | tf_op jit(solution)/shard_map/ppermute | solution.py:532
  10.2 1.2 %copy-start.5 = (f32[8,65]{1,0:T(8,128)S(1)}, f32[8,65]{1,0:T(8,128)}, u32[]{:S(2)}) copy-start(f32[8,65]{1,0:T(8,128)} %param.10) | copy-start | bytes 6244
  10.2 1.2 %copy-start.6 = (f32[8,65]{1,0:T(8,128)S(1)}, f32[8,65]{1,0:T(8,128)}, u32[]{:S(2)}) copy-start(f32[8,65]{1,0:T(8,128)} %param.9) | copy-start | bytes 6244
  11.5 3.6 %collective-permute-start.1 = (s32[2,128]{1,0:T(2,128)S(1)}, s32[2,128]{1,0:T(2,128)S(1)}, u32[]{:S(2)}, u32[]{:S(2)}) collective-permute-start(s32[2,128]{1,0:T(2,128)S(1)} %pad_add_fusion.3), channel_id=1, source_target_pairs={{0,2},{1,3},{2,0},{3,1},{4,6},{5,7},{6,4},{7,5},{8,10},{9,11},{10,... | collective-permute-start | bytes 3080 | tf_op jit(solution)/shard_map/ppermute | solution.py:532
  15.2 1.2 %collective-permute-start.2 = (s32[4,128]{1,0:T(4,128)S(1)}, s32[4,128]{1,0:T(4,128)S(1)}, u32[]{:S(2)}, u32[]{:S(2)}) collective-permute-start(s32[4,128]{1,0:T(4,128)S(1)} %pad_add_fusion.2), channel_id=1, source_target_pairs={{0,4},{4,0},{1,5},{5,1},{2,6},{6,2},{3,7},{7,3},{8,12},{12,8},{9,1... | collective-permute-start | bytes 6152 | tf_op jit(solution)/shard_map/ppermute | solution.py:532
  19.8 18.6 %all-to-all-start = ((f32[8,256,128]{2,1,0:T(8,128)}), f32[8,256,128]{2,1,0:T(8,128)S(1)}, u32[]{:S(2)}, u32[]{:S(2)}) async-start(f32[8,256,128]{2,1,0:T(8,128)} %bitcast.14), calls=%async_computation | async-start | bytes 2097152 | tf_op jit(solution)/shard_map/all_to_all | solution.py:610
  23.6 3.7 %collective-permute-start.6 = (s32[8,128]{1,0:T(8,128)S(1)}, s32[8,128]{1,0:T(8,128)S(1)}, u32[]{:S(2)}, u32[]{:S(2)}) collective-permute-start(s32[8,128]{1,0:T(8,128)S(1)} %get-tuple-element.18), channel_id=1, source_target_pairs={{0,8},{8,0},{16,24},{24,16},{1,9},{9,1},{17,25},{25,17},{2,10},{10... | collective-permute-start | bytes 12296 | tf_op jit(solution)/shard_map/ppermute | solution.py:532
  24.4 16.8 %collective-permute-start.10 = (f32[32,1024]{1,0:T(8,128)S(1)}, f32[32,1024]{1,0:T(8,128)S(1)}, u32[]{:S(2)}, u32[]{:S(2)}) collective-permute-start(f32[32,1024]{1,0:T(8,128)S(1)} %get-tuple-element.23), channel_id=1, source_target_pairs={{0,4},{8,12},{16,20},{24,28},{4,0},{12,8},{20,16},{28,24},{1,5},{9... | collective-permute-start | bytes 393224 | tf_op jit(solution)/shard_map/ppermute | solution.py:522
  24.5 16.7 %collective-permute-start.11 = (f32[32,1024]{1,0:T(8,128)S(1)}, f32[32,1024]{1,0:T(8,128)S(1)}, u32[]{:S(2)}, u32[]{:S(2)}) collective-permute-start(f32[32,1024]{1,0:T(8,128)S(1)} %get-tuple-element.24), channel_id=1, source_target_pairs={{4,8},{12,16},{20,24},{8,4},{16,12},{24,20},{5,9},{13,17},{21,25},... | collective-permute-start | bytes 393224 | tf_op jit(solution)/shard_map/ppermute | solution.py:522
  27.3 5.2 %collective-permute-start.7 = (s32[16,128]{1,0:T(8,128)S(1)}, s32[16,128]{1,0:T(8,128)S(1)}, u32[]{:S(2)}, u32[]{:S(2)}) collective-permute-start(s32[16,128]{1,0:T(8,128)S(1)} %pad_add_fusion), channel_id=1, source_target_pairs={{0,16},{8,24},{16,0},{24,8},{1,17},{9,25},{17,1},{25,9},{2,18},{10... | collective-permute-start | bytes 24584 | tf_op jit(solution)/shard_map/ppermute | solution.py:532
  39.6 1.7 %copy-start = (f32[128,1024]{1,0:T(8,128)S(1)}, f32[128,1024]{1,0:T(8,128)}, u32[]{:S(2)}) copy-start(f32[128,1024]{1,0:T(8,128)} %own_ref.1) | copy-start | bytes 1572868
  39.6 1.7 %collective-permute-start.8 = (f32[64,1024]{1,0:T(8,128)S(1)}, f32[64,1024]{1,0:T(8,128)S(1)}, u32[]{:S(2)}, u32[]{:S(2)}) collective-permute-start(f32[64,1024]{1,0:T(8,128)S(1)} %get-tuple-element.21), channel_id=1, source_target_pairs={{0,4},{8,12},{16,20},{24,28},{4,0},{12,8},{20,16},{28,24},{1,5},{9... | collective-permute-start | bytes 786440 | tf_op jit(solution)/shard_map/ppermute | solution.py:522
  39.9 1.4 %collective-permute-start.9 = (f32[64,1024]{1,0:T(8,128)S(1)}, f32[64,1024]{1,0:T(8,128)S(1)}, u32[]{:S(2)}, u32[]{:S(2)}) collective-permute-start(f32[64,1024]{1,0:T(8,128)S(1)} %get-tuple-element.22), channel_id=1, source_target_pairs={{4,8},{12,16},{20,24},{8,4},{16,12},{24,20},{5,9},{13,17},{21,25},... | collective-permute-start | bytes 786440 | tf_op jit(solution)/shard_map/ppermute | solution.py:522
  42.0 4.6 %collective-permute-start.12 = (f32[176,128]{1,0:T(8,128)S(1)}, f32[176,128]{1,0:T(8,128)S(1)}, u32[]{:S(2)}, u32[]{:S(2)}) collective-permute-start(f32[176,128]{1,0:T(8,128)S(1)} %get-tuple-element.25), channel_id=1, source_target_pairs={{0,1},{2,3},{1,0},{3,2},{4,5},{6,7},{5,4},{7,6},{8,9},{10,11},{9,8... | collective-permute-start | bytes 270344 | tf_op jit(solution)/shard_map/ppermute | solution.py:522
  42.9 3.7 %copy-start.4 = (f32[8]{0:T(128)S(1)}, f32[8]{0:T(128)}, u32[]{:S(2)}) copy-start(f32[8]{0:T(128)} %weight_ref.1) | copy-start | bytes 100
  42.9 3.7 %collective-permute-start.13 = (f32[176,128]{1,0:T(8,128)S(1)}, f32[176,128]{1,0:T(8,128)S(1)}, u32[]{:S(2)}, u32[]{:S(2)}) collective-permute-start(f32[176,128]{1,0:T(8,128)S(1)} %get-tuple-element.26), channel_id=1, source_target_pairs={{1,2},{2,1},{5,6},{6,5},{9,10},{10,9},{13,14},{14,13},{17,18},{18,... | collective-permute-start | bytes 270344 | tf_op jit(solution)/shard_map/ppermute | solution.py:522
  64.8 40.3 %copy-start.2 = (f32[32,1024]{1,0:T(8,128)S(1)}, f32[32,1024]{1,0:T(8,128)}, u32[]{:S(2)}) copy-start(f32[32,1024]{1,0:T(8,128)} %param.6) | copy-start | bytes 393220

commit v7 on v6

--- a/solution.py
+++ b/solution.py
@@ -269,6 +269,8 @@
     ghigh_ref,
     gturn_ref,
     grad_ref,
+    tiles_ref,
+    sent,
 ):
     tile_rows, tile_cols = index_ref.shape
     rows_here = tile_rows * TILE
@@ -457,24 +459,16 @@
             *high,
         ]
 
-    together = 4
-    grad_ref[...] = jnp.zeros_like(grad_ref)
-
-    @pl.loop(0, KERNELS // together)
-    def _(part_of):
-        ks = [part_of * together + n for n in range(together)]
-        stacked = [
-            jnp.concatenate([x for k in ks for x in windows_of(k, WIDE * jj)], axis=1)
-            for jj in range(supers)
-        ]
-        band = jnp.concatenate([bcol_ref[k] for k in ks], axis=0)
-        part = mm(jnp.concatenate(stacked, axis=0), band)
-        for g in range(groups):
-            rows = slice(g * rows_here, (g + 1) * rows_here)
-            top = (g // 2) * rows_here
-            grad_ref[rows, :] += part[
-                top : top + rows_here, LANES * (g % 2) : LANES * (g % 2 + 1)
-            ]
+    stacked = [
+        jnp.concatenate([x for k in range(KERNELS) for x in windows_of(k, WIDE * jj)], axis=1)
+        for jj in range(supers)
+    ]
+    band = jnp.concatenate([bcol_ref[k] for k in range(KERNELS)], axis=0)
+    part = mm(jnp.concatenate(stacked, axis=0), band)
+    for g in range(groups):
+        rows = slice(g * rows_here, (g + 1) * rows_here)
+        top = (g // 2) * rows_here
+        grad_ref[rows, :] = part[top : top + rows_here, LANES * (g % 2) : LANES * (g % 2 + 1)]
 
     @pl.loop(0, tile_rows)
     def _(a):
@@ -482,8 +476,15 @@
             base = g * rows_here + a * TILE
             parts = [grad_ref[pl.ds(base + s, 8, stride=4), :] for s in range(4)]
             for b, tile in enumerate(transpose_blocks(parts, block)):
-                place = pl.multiple_of(index_ref[a, 4 * g + b] * 8, 8)
-                out_ref[pl.ds(place, 8), :] = tile
+                home = pl.multiple_of(index_ref[a, 4 * g + b] * 8, 8)
+                here = pl.ds(pl.multiple_of((a * tile_cols + 4 * g + b) * 8, 8), 8)
+                tiles_ref[here, :] = tile
+                pltpu.make_async_copy(
+                    tiles_ref.at[here, :], out_ref.at[pl.ds(home, 8), :], sent
+                ).start()
+
+    every = tiles_ref.shape[0]
+    pltpu.make_async_copy(tiles_ref, out_ref.at[pl.ds(0, every), :], sent).wait()
 
 
 def to_rows(x):
@@ -664,10 +665,13 @@
             pltpu.VMEM((KERNELS, height, breadth + 128), BF16),
             pltpu.VMEM((KERNELS, height, breadth + 128), BF16),
             pltpu.VMEM((height * (breadth // LANES), LANES), F32),
+            pltpu.VMEM((tiles_here * 8, LANES), F32),
+            pltpu.SemaphoreType.DMA,
         ],
         [home, me, kernel_weight],
         [mask, rowa, rowb, cola, colb, target, above, below, waves],
         megabytes=36,
+        out_space=pl.ANY,
     )
     back = lax.all_to_all(returned, everyone, split_axis=0, concat_axis=0, tiled=True)
     stepped = kernel_call(

time: 108 us -> 112 us (1.037)
  Pallas kernels: 24.4 us -> 28.3 us
    pallas_call x6, Pallas kernels: 24.4 us -> 28.3 us  [kernel_call(): pl.pallas_call(body, out_shape=outs, in_specs=[pl.BlockSpec(memory_space=...]
where the time goes in v7:
time: 112 us; the launch traced here: 111 us
  blocking collectives  40.3 us (36%)
  Pallas kernels  28.3 us (25%)
  starting transfers between devices  19.3 us (17%)
  waiting for transfers between devices  16.8 us (15%)
  other arithmetic  3.87 us (3%)
  local copies, waits for them, and re-layouts  2.54 us (2%)
    all_to_all x1, blocking collectives, shards(): lax.all_to_all(returned, everyone, split_axis=0, concat_axis=0, tiled=True)  40.3 us
    pallas_call x6, Pallas kernels, kernel_call(): pl.pallas_call(body, out_shape=outs, in_specs=[pl.BlockSpec(memory_space=...  28.3 us
    ppermute x5, waiting for transfers between devices, doubled(): got = lax.ppermute(table, axis, [(i, i ^ bit) for i in range(count)])  7.88 us
    ppermute x5, starting transfers between devices, doubled(): got = lax.ppermute(table, axis, [(i, i ^ bit) for i in range(count)])  6.27 us
    ppermute x3, starting transfers between devices, shards(): lax.ppermute(ordered, 'deep', [(i, i ^ e) for i in range(deep)])  5.72 us
    all_to_all x1, waiting for transfers between devices, shards(): lax.all_to_all(packed, plane, split_axis=0, concat_axis=0, tiled=True)  5.65 us
    all_to_all x1, starting transfers between devices, shards(): lax.all_to_all(packed, plane, split_axis=0, concat_axis=0, tiled=True)  3.74 us
    ppermute x6, starting transfers between devices, exchange(): return lax.ppermute(x, axis, swap + [(j, i) for i, j in swap])  3.55 us
  transfers between devices with their start and end apart: 15, of which 7 were waited for; matrix products, arithmetic and copies ran while one was open for 4% of the time, Pallas kernels for 1%

profile of v7, /device:TPU:0, one launch (start us, length us, event | category | flops | bytes accessed | tf_op | source)
XLA Modules:
  0.0 111.3 jit_solution(3443986222378747287)
XLA Ops:
  0.0 0.9 copy-done.1
  0.9 0.7 copy-done.3
  1.7 5.1 %collective-permute-start.5 = (f32[256,128]{1,0:T(8,128)S(1)}, f32[256,128]{1,0:T(8,128)S(1)}, u32[]{:S(2)}, u32[]{:S(2)}) collective-permute-start(f32[256,128]{1,0:T(8,128)S(1)} %get-tuple-element.17.rest_0_), channel_id=1, source_target_pairs={{0,24},{8,16},{16,8},{24,0},{1,25},{9,17},{17,9},{25,1},{2,26},{10... | collective-permute-start | bytes 393224 | tf_op jit(solution)/shard_map/ppermute | solution.py:570
  6.7 0.6 collective-permute-start.3
  7.4 1.6 %collective-permute-start = (s32[1,128]{1,0:T(1,128)S(1)}, s32[1,128]{1,0:T(1,128)S(1)}, u32[]{:S(2)}, u32[]{:S(2)}) collective-permute-start(s32[1,128]{1,0:T(1,128)S(1)} %get-tuple-element.16), channel_id=1, source_target_pairs={{0,1},{1,0},{2,3},{3,2},{4,5},{5,4},{6,7},{7,6},{8,9},{9,8},{10,11... | collective-permute-start | bytes 1544 | tf_op jit(solution)/shard_map/ppermute | solution.py:533
  9.0 0.5 broadcast.308
  9.6 0.7 fusion.25
  10.2 1.0 slice_select_fusion
  11.5 1.6 %collective-permute-start.1 = (s32[2,128]{1,0:T(2,128)S(1)}, s32[2,128]{1,0:T(2,128)S(1)}, u32[]{:S(2)}, u32[]{:S(2)}) collective-permute-start(s32[2,128]{1,0:T(2,128)S(1)} %pad_add_fusion.3), channel_id=1, source_target_pairs={{0,2},{1,3},{2,0},{3,1},{4,6},{5,7},{6,4},{7,5},{8,10},{9,11},{10,... | collective-permute-start | bytes 3080 | tf_op jit(solution)/shard_map/ppermute | solution.py:533
  13.1 2.0 %collective-permute-done.1 = s32[2,128]{1,0:T(2,128)S(1)} collective-permute-done((s32[2,128]{1,0:T(2,128)S(1)}, s32[2,128]{1,0:T(2,128)S(1)}, u32[]{:S(2)}, u32[]{:S(2)}) %collective-permute-start.1) | collective-permute-done | bytes 1056 | tf_op jit(solution)/shard_map/ppermute | solution.py:533
  15.6 0.8 collective-permute-done.2
  16.8 0.6 select_reduce_fusion.1
  17.4 0.4 collective-permute-done.4.rest_2_
  17.8 2.0 %pack.1 = f32[2048,128]{1,0:T(8,128)} custom-call(s32[8,4,8]{2,1,0:T(4,128)S(1)} %bitcast.38, s32[8]{0:T(128)S(1)} %stack.27.me_ref.spot_ref, f32[256,128]{1,0:T(8,128)S(1)} %get-tuple-element.17.rest_0_, f32[256,128]{1,0:T(8,128)S(1)} %collective-permute-done.3.rest_1_, f32[256,128]{1,0:T(8,128)S(1)} %collective-permute-done.4.rest_2_, ...), custom_call_target="tpu_custom_call" | custom-call | tf_op jit(solution)/shard_map/pack/pallas_call | solution.py:504
  19.8 3.7 %all-to-all-start = ((f32[8,256,128]{2,1,0:T(8,128)}), f32[8,256,128]{2,1,0:T(8,128)S(1)}, u32[]{:S(2)}, u32[]{:S(2)}) async-start(f32[8,256,128]{2,1,0:T(8,128)} %bitcast.14), calls=%async_computation | async-start | bytes 2097152 | tf_op jit(solution)/shard_map/all_to_all | solution.py:611
  23.6 0.8 collective-permute-start.6
  24.5 0.7 collective-permute-start.11
  25.2 2.1 %collective-permute-done.6 = s32[8,128]{1,0:T(8,128)S(1)} collective-permute-done((s32[8,128]{1,0:T(8,128)S(1)}, s32[8,128]{1,0:T(8,128)S(1)}, u32[]{:S(2)}, u32[]{:S(2)}) %collective-permute-start.6) | collective-permute-done | bytes 4128 | tf_op jit(solution)/shard_map/ppermute | solution.py:533
  27.3 2.2 %collective-permute-start.7 = (s32[16,128]{1,0:T(8,128)S(1)}, s32[16,128]{1,0:T(8,128)S(1)}, u32[]{:S(2)}, u32[]{:S(2)}) collective-permute-start(s32[16,128]{1,0:T(8,128)S(1)} %pad_add_fusion), channel_id=1, source_target_pairs={{0,16},{8,24},{16,0},{24,8},{1,17},{9,25},{17,1},{25,9},{2,18},{10... | collective-permute-start | bytes 24584 | tf_op jit(solution)/shard_map/ppermute | solution.py:533
  29.5 3.0 %collective-permute-done.7 = s32[16,128]{1,0:T(8,128)S(1)} collective-permute-done((s32[16,128]{1,0:T(8,128)S(1)}, s32[16,128]{1,0:T(8,128)S(1)}, u32[]{:S(2)}, u32[]{:S(2)}) %collective-permute-start.7) | collective-permute-done | bytes 8224 | tf_op jit(solution)/shard_map/ppermute | solution.py:533
  32.8 5.6 %all-to-all-done = f32[8,256,128]{2,1,0:T(8,128)S(1)} async-done(((f32[8,256,128]{2,1,0:T(8,128)}), f32[8,256,128]{2,1,0:T(8,128)S(1)}, u32[]{:S(2)}, u32[]{:S(2)}) %all-to-all-start) | async-done | bytes 1048608 | tf_op jit(solution)/shard_map/all_to_all | solution.py:611
  38.4 1.1 assemble.1
  39.6 0.4 collective-permute-start.8
  39.9 0.7 collective-permute-start.9
  40.6 0.6 select_reduce_fusion.rest_0_.asked_ref
  41.3 0.7 edges.1
  42.0 0.9 collective-permute-start.12
  42.9 0.8 collective-permute-start.13
  43.7 2.9 %collective-permute-done.12.cola_ref = f32[176,128]{1,0:T(8,128)S(1)} collective-permute-done((f32[176,128]{1,0:T(8,128)S(1)}, f32[176,128]{1,0:T(8,128)S(1)}, u32[]{:S(2)}, u32[]{:S(2)}) %collective-permute-start.12) | collective-permute-done | bytes 90144 | tf_op jit(solution)/shard_map/ppermute | solution.py:523
  46.6 22.1 %image.1 = f32[2048,128]{1,0:T(8,128)S(1)} custom-call(s32[4,32]{1,0:T(4,128)S(1)} %get-tuple-element.28.index_ref, s32[8]{0:T(128)S(1)} %stack.27.me_ref.spot_ref, f32[8]{0:T(128)S(1)} %copy-done.4, f32[128,1024]{1,0:T(8,128)S(1)} %get-tuple-element.20.mask_ref, f32[64,1024]{1,0:T(8,128)S(1)} %collective-permute-done.8.rowa_ref, ...), custom_call_target="tpu_custom_call" | custom-call | tf_op jit(solution)/shard_map/image/pallas_call | solution.py:504
  68.7 40.3 %all_to_all.22 = f32[32,64,128]{2,1,0:T(8,128)S(1)} all-to-all(f32[32,64,128]{2,1,0:T(8,128)S(1)} %bitcast.33), channel_id=1, replica_groups=mesh['deep'=4,'core'=2,'col'=4] {'deep','core','col'}, dimensions={0} | all-to-all | bytes 2097152 | tf_op jit(solution)/shard_map/all_to_all | solution.py:676
  108.9 2.4 %step.1 = f32[256,128]{1,0:T(8,128)} custom-call(s32[32,8]{1,0:T(8,128)S(1)} %select_reduce_fusion.rest_0_.asked_ref, s32[8]{0:T(128)S(1)} %stack.27.me_ref.spot_ref, f32[256,128]{1,0:T(8,128)S(1)} %bitcast.37, f32[2048,128]{1,0:T(8,128)S(1)} %bitcast.35), custom_call_target="tpu_custom_call" | custom-call | tf_op jit(solution)/shard_map/step/pallas_call | solution.py:504
  (53 shorter events, 1.7 us)
Async XLA Ops:
  0.0 0.9 copy-start.1
  0.9 0.7 copy-start.3
  1.7 15.8 %collective-permute-start.5 = (f32[256,128]{1,0:T(8,128)S(1)}, f32[256,128]{1,0:T(8,128)S(1)}, u32[]{:S(2)}, u32[]{:S(2)}) collective-permute-start(f32[256,128]{1,0:T(8,128)S(1)} %get-tuple-element.17.rest_0_), channel_id=1, source_target_pairs={{0,24},{8,16},{16,8},{24,0},{1,25},{9,17},{17,9},{25,1},{2,26},{10... | collective-permute-start | bytes 393224 | tf_op jit(solution)/shard_map/ppermute | solution.py:570
  6.7 11.1 %collective-permute-start.4 = (f32[256,128]{1,0:T(8,128)S(1)}, f32[256,128]{1,0:T(8,128)S(1)}, u32[]{:S(2)}, u32[]{:S(2)}) collective-permute-start(f32[256,128]{1,0:T(8,128)S(1)} %get-tuple-element.17.rest_0_), channel_id=1, source_target_pairs={{0,16},{8,24},{16,0},{24,8},{1,17},{9,25},{17,1},{25,9},{2,18},{10... | collective-permute-start | bytes 393224 | tf_op jit(solution)/shard_map/ppermute | solution.py:570
  6.7 11.1 %collective-permute-start.3 = (f32[256,128]{1,0:T(8,128)S(1)}, f32[256,128]{1,0:T(8,128)S(1)}, u32[]{:S(2)}, u32[]{:S(2)}) collective-permute-start(f32[256,128]{1,0:T(8,128)S(1)} %get-tuple-element.17.rest_0_), channel_id=1, source_target_pairs={{0,8},{8,0},{16,24},{24,16},{1,9},{9,1},{17,25},{25,17},{2,10},{10... | collective-permute-start | bytes 393224 | tf_op jit(solution)/shard_map/ppermute | solution.py:570
  7.4 4.1 %collective-permute-start = (s32[1,128]{1,0:T(1,128)S(1)}, s32[1,128]{1,0:T(1,128)S(1)}, u32[]{:S(2)}, u32[]{:S(2)}) collective-permute-start(s32[1,128]{1,0:T(1,128)S(1)} %get-tuple-element.16), channel_id=1, source_target_pairs={{0,1},{1,0},{2,3},{3,2},{4,5},{5,4},{6,7},{7,6},{8,9},{9,8},{10,11... | collective-permute-start | bytes 1544 | tf_op jit(solution)/shard_map/ppermute | solution.py:533
  10.2 1.2 %copy-start.5 = (f32[8,65]{1,0:T(8,128)S(1)}, f32[8,65]{1,0:T(8,128)}, u32[]{:S(2)}) copy-start(f32[8,65]{1,0:T(8,128)} %param.10) | copy-start | bytes 6244
  10.2 1.2 %copy-start.6 = (f32[8,65]{1,0:T(8,128)S(1)}, f32[8,65]{1,0:T(8,128)}, u32[]{:S(2)}) copy-start(f32[8,65]{1,0:T(8,128)} %param.9) | copy-start | bytes 6244
  11.5 3.6 %collective-permute-start.1 = (s32[2,128]{1,0:T(2,128)S(1)}, s32[2,128]{1,0:T(2,128)S(1)}, u32[]{:S(2)}, u32[]{:S(2)}) collective-permute-start(s32[2,128]{1,0:T(2,128)S(1)} %pad_add_fusion.3), channel_id=1, source_target_pairs={{0,2},{1,3},{2,0},{3,1},{4,6},{5,7},{6,4},{7,5},{8,10},{9,11},{10,... | collective-permute-start | bytes 3080 | tf_op jit(solution)/shard_map/ppermute | solution.py:533
  15.2 1.2 %collective-permute-start.2 = (s32[4,128]{1,0:T(4,128)S(1)}, s32[4,128]{1,0:T(4,128)S(1)}, u32[]{:S(2)}, u32[]{:S(2)}) collective-permute-start(s32[4,128]{1,0:T(4,128)S(1)} %pad_add_fusion.2), channel_id=1, source_target_pairs={{0,4},{4,0},{1,5},{5,1},{2,6},{6,2},{3,7},{7,3},{8,12},{12,8},{9,1... | collective-permute-start | bytes 6152 | tf_op jit(solution)/shard_map/ppermute | solution.py:533
  19.8 18.6 %all-to-all-start = ((f32[8,256,128]{2,1,0:T(8,128)}), f32[8,256,128]{2,1,0:T(8,128)S(1)}, u32[]{:S(2)}, u32[]{:S(2)}) async-start(f32[8,256,128]{2,1,0:T(8,128)} %bitcast.14), calls=%async_computation | async-start | bytes 2097152 | tf_op jit(solution)/shard_map/all_to_all | solution.py:611
  23.6 3.7 %collective-permute-start.6 = (s32[8,128]{1,0:T(8,128)S(1)}, s32[8,128]{1,0:T(8,128)S(1)}, u32[]{:S(2)}, u32[]{:S(2)}) collective-permute-start(s32[8,128]{1,0:T(8,128)S(1)} %get-tuple-element.18), channel_id=1, source_target_pairs={{0,8},{8,0},{16,24},{24,16},{1,9},{9,1},{17,25},{25,17},{2,10},{10... | collective-permute-start | bytes 12296 | tf_op jit(solution)/shard_map/ppermute | solution.py:533
  24.4 16.8 %collective-permute-start.10 = (f32[32,1024]{1,0:T(8,128)S(1)}, f32[32,1024]{1,0:T(8,128)S(1)}, u32[]{:S(2)}, u32[]{:S(2)}) collective-permute-start(f32[32,1024]{1,0:T(8,128)S(1)} %get-tuple-element.23), channel_id=1, source_target_pairs={{0,4},{8,12},{16,20},{24,28},{4,0},{12,8},{20,16},{28,24},{1,5},{9... | collective-permute-start | bytes 393224 | tf_op jit(solution)/shard_map/ppermute | solution.py:523
  24.5 16.7 %collective-permute-start.11 = (f32[32,1024]{1,0:T(8,128)S(1)}, f32[32,1024]{1,0:T(8,128)S(1)}, u32[]{:S(2)}, u32[]{:S(2)}) collective-permute-start(f32[32,1024]{1,0:T(8,128)S(1)} %get-tuple-element.24), channel_id=1, source_target_pairs={{4,8},{12,16},{20,24},{8,4},{16,12},{24,20},{5,9},{13,17},{21,25},... | collective-permute-start | bytes 393224 | tf_op jit(solution)/shard_map/ppermute | solution.py:523
  27.3 5.2 %collective-permute-start.7 = (s32[16,128]{1,0:T(8,128)S(1)}, s32[16,128]{1,0:T(8,128)S(1)}, u32[]{:S(2)}, u32[]{:S(2)}) collective-permute-start(s32[16,128]{1,0:T(8,128)S(1)} %pad_add_fusion), channel_id=1, source_target_pairs={{0,16},{8,24},{16,0},{24,8},{1,17},{9,25},{17,1},{25,9},{2,18},{10... | collective-permute-start | bytes 24584 | tf_op jit(solution)/shard_map/ppermute | solution.py:533
  39.6 1.7 %copy-start = (f32[128,1024]{1,0:T(8,128)S(1)}, f32[128,1024]{1,0:T(8,128)}, u32[]{:S(2)}) copy-start(f32[128,1024]{1,0:T(8,128)} %own_ref.1) | copy-start | bytes 1572868
  39.6 1.7 %collective-permute-start.8 = (f32[64,1024]{1,0:T(8,128)S(1)}, f32[64,1024]{1,0:T(8,128)S(1)}, u32[]{:S(2)}, u32[]{:S(2)}) collective-permute-start(f32[64,1024]{1,0:T(8,128)S(1)} %get-tuple-element.21), channel_id=1, source_target_pairs={{0,4},{8,12},{16,20},{24,28},{4,0},{12,8},{20,16},{28,24},{1,5},{9... | collective-permute-start | bytes 786440 | tf_op jit(solution)/shard_map/ppermute | solution.py:523
  39.9 1.4 %collective-permute-start.9 = (f32[64,1024]{1,0:T(8,128)S(1)}, f32[64,1024]{1,0:T(8,128)S(1)}, u32[]{:S(2)}, u32[]{:S(2)}) collective-permute-start(f32[64,1024]{1,0:T(8,128)S(1)} %get-tuple-element.22), channel_id=1, source_target_pairs={{4,8},{12,16},{20,24},{8,4},{16,12},{24,20},{5,9},{13,17},{21,25},... | collective-permute-start | bytes 786440 | tf_op jit(solution)/shard_map/ppermute | solution.py:523
  42.0 4.6 %collective-permute-start.12 = (f32[176,128]{1,0:T(8,128)S(1)}, f32[176,128]{1,0:T(8,128)S(1)}, u32[]{:S(2)}, u32[]{:S(2)}) collective-permute-start(f32[176,128]{1,0:T(8,128)S(1)} %get-tuple-element.25), channel_id=1, source_target_pairs={{0,1},{2,3},{1,0},{3,2},{4,5},{6,7},{5,4},{7,6},{8,9},{10,11},{9,8... | collective-permute-start | bytes 270344 | tf_op jit(solution)/shard_map/ppermute | solution.py:523
  42.9 3.7 %copy-start.4 = (f32[8]{0:T(128)S(1)}, f32[8]{0:T(128)}, u32[]{:S(2)}) copy-start(f32[8]{0:T(128)} %weight_ref.1) | copy-start | bytes 100
  42.9 3.7 %collective-permute-start.13 = (f32[176,128]{1,0:T(8,128)S(1)}, f32[176,128]{1,0:T(8,128)S(1)}, u32[]{:S(2)}, u32[]{:S(2)}) collective-permute-start(f32[176,128]{1,0:T(8,128)S(1)} %get-tuple-element.26), channel_id=1, source_target_pairs={{1,2},{2,1},{5,6},{6,5},{9,10},{10,9},{13,14},{14,13},{17,18},{18,... | collective-permute-start | bytes 270344 | tf_op jit(solution)/shard_map/ppermute | solution.py:523
  68.7 40.3 %copy-start.2 = (f32[32,1024]{1,0:T(8,128)S(1)}, f32[32,1024]{1,0:T(8,128)}, u32[]{:S(2)}) copy-start(f32[32,1024]{1,0:T(8,128)} %param.6) | copy-start | bytes 393220

commit v8 on v6

--- a/solution.py
+++ b/solution.py
@@ -100,11 +100,9 @@
     return out
 
 
-def spread_kernel(cells_ref, instance_ref, out_ref, named_ref):
+def spread_kernel(cells_ref, out_ref):
     for c in range(out_ref.shape[0] // 8):
         out_ref[c * 8 : c * 8 + 8, :] = cells_ref[pl.ds((c // 8) * 64 + c % 8, 8, stride=8), :]
-    rows = [instance_ref[a : a + 1, :] for a in range(instance_ref.shape[0])]
-    named_ref[...] = jnp.concatenate(rows, axis=1)
 
 
 def pack_kernel(asked_ref, me_ref, *rest):
@@ -555,14 +553,8 @@
     f32 = lambda *shape: jax.ShapeDtypeStruct(shape, F32)
 
     flat = to_rows(cells)
-    ordered, named = kernel_call(
-        spread_kernel,
-        "spread",
-        [f32(slots * 8, LANES), jax.ShapeDtypeStruct((1, tiles_here), jnp.int32)],
-        [],
-        [],
-        [flat, instance_cell],
-    )
+    ordered = kernel_call(spread_kernel, "spread", f32(slots * 8, LANES), [], [], [flat])
+    named = instance_cell.reshape(1, -1)
     near = doubled(doubled(named, "col"), "core")
     levels = [ordered]
     for e in range(1, deep):

time: 108 us -> 107 us (level)
  waiting for transfers between devices: 16.8 us -> 18.2 us
  local copies, waits for them, and re-layouts: 2.54 us -> 1.44 us
  transfers between devices with their start and end apart: 15 -> 15, of which waited for: 7 -> 8; matrix products, arithmetic and copies ran while one was open for 4% -> 3% of each run, Pallas kernels for 1% -> 1%
where the time goes in v8:
time: 107 us
  blocking collectives  40.1 us (37%)
  Pallas kernels  24.4 us (23%)
  starting transfers between devices  19 us (18%)
  waiting for transfers between devices  18.2 us (17%)
  other arithmetic  3.22 us (3%)
  local copies, waits for them, and re-layouts  1.44 us (1%)
    all_to_all x1, blocking collectives, shards(): lax.all_to_all(returned, everyone, split_axis=0, concat_axis=0, tiled=True)  40.1 us
    pallas_call x6, Pallas kernels, kernel_call(): pl.pallas_call(body, out_shape=outs, in_specs=[pl.BlockSpec(memory_space=...  24.4 us
    ppermute x5, waiting for transfers between devices, doubled(): got = lax.ppermute(table, axis, [(i, i ^ bit) for i in range(count)])  8.52 us
    ppermute x5, starting transfers between devices, doubled(): got = lax.ppermute(table, axis, [(i, i ^ bit) for i in range(count)])  5.86 us
    all_to_all x1, waiting for transfers between devices, shards(): lax.all_to_all(packed, plane, split_axis=0, concat_axis=0, tiled=True)  5.85 us
    ppermute x3, starting transfers between devices, shards(): lax.ppermute(ordered, 'deep', [(i, i ^ e) for i in range(deep)])  5.76 us
    all_to_all x1, starting transfers between devices, shards(): lax.all_to_all(packed, plane, split_axis=0, concat_axis=0, tiled=True)  3.72 us
    ppermute x6, starting transfers between devices, exchange(): return lax.ppermute(x, axis, swap + [(j, i) for i, j in swap])  3.62 us
  transfers between devices with their start and end apart: 15, of which 8 were waited for; matrix products, arithmetic and copies ran while one was open for 3% of the time, Pallas kernels for 1%

profile of v8, /device:TPU:0, one launch (start us, length us, event | category | flops | bytes accessed | tf_op | source)
XLA Modules:
  0.0 106.6 jit_solution(10005403057579198858)
XLA Ops:
  0.0 0.9 copy-done.1
  0.9 5.1 %collective-permute-start.5 = (f32[256,128]{1,0:T(8,128)S(1)}, f32[256,128]{1,0:T(8,128)S(1)}, u32[]{:S(2)}, u32[]{:S(2)}) collective-permute-start(f32[256,128]{1,0:T(8,128)S(1)} %spread.1.rest_0_), channel_id=1, source_target_pairs={{0,24},{8,16},{16,8},{24,0},{1,25},{9,17},{17,9},{25,1},{2,26},{10... | collective-permute-start | bytes 393224 | tf_op jit(solution)/shard_map/ppermute | solution.py:561
  6.1 0.6 collective-permute-start.3
  6.8 1.6 %collective-permute-start = (s32[1,128]{1,0:T(1,128)S(1)}, s32[1,128]{1,0:T(1,128)S(1)}, u32[]{:S(2)}, u32[]{:S(2)}) collective-permute-start(s32[1,128]{1,0:T(1,128)S(1)} %concatenate.86), channel_id=1, source_target_pairs={{0,1},{1,0},{2,3},{3,2},{4,5},{5,4},{6,7},{7,6},{8,9},{9,8},{10,11... | collective-permute-start | bytes 1544 | tf_op jit(solution)/shard_map/ppermute | solution.py:530
  8.7 1.0 slice_select_fusion
  9.8 0.5 collective-permute-done
  10.3 1.7 %collective-permute-start.1 = (s32[2,128]{1,0:T(2,128)S(1)}, s32[2,128]{1,0:T(2,128)S(1)}, u32[]{:S(2)}, u32[]{:S(2)}) collective-permute-start(s32[2,128]{1,0:T(2,128)S(1)} %pad_add_fusion.3), channel_id=1, source_target_pairs={{0,2},{1,3},{2,0},{3,1},{4,6},{5,7},{6,4},{7,5},{8,10},{9,11},{10,... | collective-permute-start | bytes 3080 | tf_op jit(solution)/shard_map/ppermute | solution.py:530
  12.0 1.9 %collective-permute-done.1 = s32[2,128]{1,0:T(2,128)S(1)} collective-permute-done((s32[2,128]{1,0:T(2,128)S(1)}, s32[2,128]{1,0:T(2,128)S(1)}, u32[]{:S(2)}, u32[]{:S(2)}) %collective-permute-start.1) | collective-permute-done | bytes 1056 | tf_op jit(solution)/shard_map/ppermute | solution.py:530
  14.3 0.9 collective-permute-done.2
  15.2 0.3 reduce_window_sum.17
  15.5 0.6 select_reduce_fusion.1
  16.2 1.0 collective-permute-done.4.rest_2_
  17.1 2.0 %pack.1 = f32[2048,128]{1,0:T(8,128)} custom-call(s32[8,4,8]{2,1,0:T(4,128)S(1)} %bitcast.28, s32[8]{0:T(128)S(1)} %stack.27.me_ref.spot_ref, f32[256,128]{1,0:T(8,128)S(1)} %spread.1.rest_0_, f32[256,128]{1,0:T(8,128)S(1)} %collective-permute-done.3.rest_1_, f32[256,128]{1,0:T(8,128)S(1)} %collective-permute-done.4.rest_2_, ...), custom_call_target="tpu_custom_call" | custom-call | tf_op jit(solution)/shard_map/pack/pallas_call | solution.py:501
  19.1 3.7 %all-to-all-start = ((f32[8,256,128]{2,1,0:T(8,128)}), f32[8,256,128]{2,1,0:T(8,128)S(1)}, u32[]{:S(2)}, u32[]{:S(2)}) async-start(f32[8,256,128]{2,1,0:T(8,128)} %bitcast.12), calls=%async_computation | async-start | bytes 2097152 | tf_op jit(solution)/shard_map/all_to_all | solution.py:602
  22.9 0.5 collective-permute-start.6
  23.6 0.7 collective-permute-start.11
  24.3 2.3 %collective-permute-done.6 = s32[8,128]{1,0:T(8,128)S(1)} collective-permute-done((s32[8,128]{1,0:T(8,128)S(1)}, s32[8,128]{1,0:T(8,128)S(1)}, u32[]{:S(2)}, u32[]{:S(2)}) %collective-permute-start.6) | collective-permute-done | bytes 4128 | tf_op jit(solution)/shard_map/ppermute | solution.py:530
  26.6 2.0 %collective-permute-start.7 = (s32[16,128]{1,0:T(8,128)S(1)}, s32[16,128]{1,0:T(8,128)S(1)}, u32[]{:S(2)}, u32[]{:S(2)}) collective-permute-start(s32[16,128]{1,0:T(8,128)S(1)} %pad_add_fusion), channel_id=1, source_target_pairs={{0,16},{8,24},{16,0},{24,8},{1,17},{9,25},{17,1},{25,9},{2,18},{10... | collective-permute-start | bytes 24584 | tf_op jit(solution)/shard_map/ppermute | solution.py:530
  28.6 3.0 %collective-permute-done.7 = s32[16,128]{1,0:T(8,128)S(1)} collective-permute-done((s32[16,128]{1,0:T(8,128)S(1)}, s32[16,128]{1,0:T(8,128)S(1)}, u32[]{:S(2)}, u32[]{:S(2)}) %collective-permute-start.7) | collective-permute-done | bytes 8224 | tf_op jit(solution)/shard_map/ppermute | solution.py:530
  31.6 0.3 reduce_window_sum.18
  31.9 5.9 %all-to-all-done = f32[8,256,128]{2,1,0:T(8,128)S(1)} async-done(((f32[8,256,128]{2,1,0:T(8,128)}), f32[8,256,128]{2,1,0:T(8,128)S(1)}, u32[]{:S(2)}, u32[]{:S(2)}) %all-to-all-start) | async-done | bytes 1048608 | tf_op jit(solution)/shard_map/all_to_all | solution.py:602
  37.7 1.1 %assemble.1 = (f32[128,1024]{1,0:T(8,128)S(1)}, f32[64,1024]{1,0:T(8,128)S(1)}, f32[64,1024]{1,0:T(8,128)S(1)}) custom-call(s32[4,32]{1,0:T(4,128)S(1)} %get-tuple-element.23.index_ref, s32[8]{0:T(128)S(1)} %stack.27.me_ref.spot_ref, f32[2048,128]{1,0:T(8,128)S(1)} %bitcast.24), custom_call_target="tpu_custom_call" | custom-call | tf_op jit(solution)/shard_map/assemble/pallas_call | solution.py:501
  38.9 0.4 collective-permute-start.8
  39.2 0.7 collective-permute-start.9
  39.9 0.6 select_reduce_fusion.rest_0_.asked_ref
  40.6 0.7 edges.1
  41.3 0.9 collective-permute-start.12
  42.2 0.8 collective-permute-start.13
  43.0 2.9 %collective-permute-done.12.cola_ref = f32[176,128]{1,0:T(8,128)S(1)} collective-permute-done((f32[176,128]{1,0:T(8,128)S(1)}, f32[176,128]{1,0:T(8,128)S(1)}, u32[]{:S(2)}, u32[]{:S(2)}) %collective-permute-start.12) | collective-permute-done | bytes 90144 | tf_op jit(solution)/shard_map/ppermute | solution.py:520
  45.9 18.2 %image.1 = f32[2048,128]{1,0:T(8,128)S(1)} custom-call(s32[4,32]{1,0:T(4,128)S(1)} %get-tuple-element.24.index_ref, s32[8]{0:T(128)S(1)} %stack.27.me_ref.spot_ref, f32[8]{0:T(128)S(1)} %copy-done.3, f32[128,1024]{1,0:T(8,128)S(1)} %get-tuple-element.16.mask_ref, f32[64,1024]{1,0:T(8,128)S(1)} %collective-permute-done.8.rowa_ref, ...), custom_call_target="tpu_custom_call" | custom-call | tf_op jit(solution)/shard_map/image/pallas_call | solution.py:501
  64.1 40.1 %all_to_all.22 = f32[32,64,128]{2,1,0:T(8,128)S(1)} all-to-all(f32[32,64,128]{2,1,0:T(8,128)S(1)} %bitcast.23), channel_id=1, replica_groups=mesh['deep'=4,'core'=2,'col'=4] {'deep','core','col'}, dimensions={0} | all-to-all | bytes 2097152 | tf_op jit(solution)/shard_map/all_to_all | solution.py:664
  104.2 2.4 %step.1 = f32[256,128]{1,0:T(8,128)} custom-call(s32[32,8]{1,0:T(8,128)S(1)} %select_reduce_fusion.rest_0_.asked_ref, s32[8]{0:T(128)S(1)} %stack.27.me_ref.spot_ref, f32[256,128]{1,0:T(8,128)S(1)} %bitcast.27, f32[2048,128]{1,0:T(8,128)S(1)} %bitcast.25), custom_call_target="tpu_custom_call" | custom-call | tf_op jit(solution)/shard_map/step/pallas_call | solution.py:501
  (52 shorter events, 1.3 us)
Async XLA Ops:
  0.0 0.9 copy-start.1
  0.9 5.8 %copy-start.4 = (s32[4,32]{1,0:T(4,128)S(1)}, s32[4,32]{1,0:T(4,128)}, u32[]{:S(2)}) copy-start(s32[4,32]{1,0:T(4,128)} %param.7) | copy-start | bytes 1540
  0.9 15.2 %collective-permute-start.5 = (f32[256,128]{1,0:T(8,128)S(1)}, f32[256,128]{1,0:T(8,128)S(1)}, u32[]{:S(2)}, u32[]{:S(2)}) collective-permute-start(f32[256,128]{1,0:T(8,128)S(1)} %spread.1.rest_0_), channel_id=1, source_target_pairs={{0,24},{8,16},{16,8},{24,0},{1,25},{9,17},{17,9},{25,1},{2,26},{10... | collective-permute-start | bytes 393224 | tf_op jit(solution)/shard_map/ppermute | solution.py:561
  6.1 11.1 %collective-permute-start.4 = (f32[256,128]{1,0:T(8,128)S(1)}, f32[256,128]{1,0:T(8,128)S(1)}, u32[]{:S(2)}, u32[]{:S(2)}) collective-permute-start(f32[256,128]{1,0:T(8,128)S(1)} %spread.1.rest_0_), channel_id=1, source_target_pairs={{0,16},{8,24},{16,0},{24,8},{1,17},{9,25},{17,1},{25,9},{2,18},{10... | collective-permute-start | bytes 393224 | tf_op jit(solution)/shard_map/ppermute | solution.py:561
  6.1 11.1 %collective-permute-start.3 = (f32[256,128]{1,0:T(8,128)S(1)}, f32[256,128]{1,0:T(8,128)S(1)}, u32[]{:S(2)}, u32[]{:S(2)}) collective-permute-start(f32[256,128]{1,0:T(8,128)S(1)} %spread.1.rest_0_), channel_id=1, source_target_pairs={{0,8},{8,0},{16,24},{24,16},{1,9},{9,1},{17,25},{25,17},{2,10},{10... | collective-permute-start | bytes 393224 | tf_op jit(solution)/shard_map/ppermute | solution.py:561
  6.8 3.5 %collective-permute-start = (s32[1,128]{1,0:T(1,128)S(1)}, s32[1,128]{1,0:T(1,128)S(1)}, u32[]{:S(2)}, u32[]{:S(2)}) collective-permute-start(s32[1,128]{1,0:T(1,128)S(1)} %concatenate.86), channel_id=1, source_target_pairs={{0,1},{1,0},{2,3},{3,2},{4,5},{5,4},{6,7},{7,6},{8,9},{9,8},{10,11... | collective-permute-start | bytes 1544 | tf_op jit(solution)/shard_map/ppermute | solution.py:530
  8.7 1.0 copy-start.5
  8.7 1.0 copy-start.6
  10.3 3.6 %collective-permute-start.1 = (s32[2,128]{1,0:T(2,128)S(1)}, s32[2,128]{1,0:T(2,128)S(1)}, u32[]{:S(2)}, u32[]{:S(2)}) collective-permute-start(s32[2,128]{1,0:T(2,128)S(1)} %pad_add_fusion.3), channel_id=1, source_target_pairs={{0,2},{1,3},{2,0},{3,1},{4,6},{5,7},{6,4},{7,5},{8,10},{9,11},{10,... | collective-permute-start | bytes 3080 | tf_op jit(solution)/shard_map/ppermute | solution.py:530
  13.9 1.2 %collective-permute-start.2 = (s32[4,128]{1,0:T(4,128)S(1)}, s32[4,128]{1,0:T(4,128)S(1)}, u32[]{:S(2)}, u32[]{:S(2)}) collective-permute-start(s32[4,128]{1,0:T(4,128)S(1)} %pad_add_fusion.2), channel_id=1, source_target_pairs={{0,4},{4,0},{1,5},{5,1},{2,6},{6,2},{3,7},{7,3},{8,12},{12,8},{9,1... | collective-permute-start | bytes 6152 | tf_op jit(solution)/shard_map/ppermute | solution.py:530
  19.1 18.6 %all-to-all-start = ((f32[8,256,128]{2,1,0:T(8,128)}), f32[8,256,128]{2,1,0:T(8,128)S(1)}, u32[]{:S(2)}, u32[]{:S(2)}) async-start(f32[8,256,128]{2,1,0:T(8,128)} %bitcast.12), calls=%async_computation | async-start | bytes 2097152 | tf_op jit(solution)/shard_map/all_to_all | solution.py:602
  22.9 3.7 %collective-permute-start.6 = (s32[8,128]{1,0:T(8,128)S(1)}, s32[8,128]{1,0:T(8,128)S(1)}, u32[]{:S(2)}, u32[]{:S(2)}) collective-permute-start(s32[8,128]{1,0:T(8,128)S(1)} %get-tuple-element.14), channel_id=1, source_target_pairs={{0,8},{8,0},{16,24},{24,16},{1,9},{9,1},{17,25},{25,17},{2,10},{10... | collective-permute-start | bytes 12296 | tf_op jit(solution)/shard_map/ppermute | solution.py:530
  23.4 17.1 %collective-permute-start.10 = (f32[32,1024]{1,0:T(8,128)S(1)}, f32[32,1024]{1,0:T(8,128)S(1)}, u32[]{:S(2)}, u32[]{:S(2)}) collective-permute-start(f32[32,1024]{1,0:T(8,128)S(1)} %get-tuple-element.19), channel_id=1, source_target_pairs={{0,4},{8,12},{16,20},{24,28},{4,0},{12,8},{20,16},{28,24},{1,5},{9... | collective-permute-start | bytes 393224 | tf_op jit(solution)/shard_map/ppermute | solution.py:520
  23.6 16.9 %collective-permute-start.11 = (f32[32,1024]{1,0:T(8,128)S(1)}, f32[32,1024]{1,0:T(8,128)S(1)}, u32[]{:S(2)}, u32[]{:S(2)}) collective-permute-start(f32[32,1024]{1,0:T(8,128)S(1)} %get-tuple-element.20), channel_id=1, source_target_pairs={{4,8},{12,16},{20,24},{8,4},{16,12},{24,20},{5,9},{13,17},{21,25},... | collective-permute-start | bytes 393224 | tf_op jit(solution)/shard_map/ppermute | solution.py:520
  26.6 5.0 %collective-permute-start.7 = (s32[16,128]{1,0:T(8,128)S(1)}, s32[16,128]{1,0:T(8,128)S(1)}, u32[]{:S(2)}, u32[]{:S(2)}) collective-permute-start(s32[16,128]{1,0:T(8,128)S(1)} %pad_add_fusion), channel_id=1, source_target_pairs={{0,16},{8,24},{16,0},{24,8},{1,17},{9,25},{17,1},{25,9},{2,18},{10... | collective-permute-start | bytes 24584 | tf_op jit(solution)/shard_map/ppermute | solution.py:530
  38.9 1.7 %copy-start = (f32[128,1024]{1,0:T(8,128)S(1)}, f32[128,1024]{1,0:T(8,128)}, u32[]{:S(2)}) copy-start(f32[128,1024]{1,0:T(8,128)} %own_ref.1) | copy-start | bytes 1572868
  38.9 1.7 %collective-permute-start.8 = (f32[64,1024]{1,0:T(8,128)S(1)}, f32[64,1024]{1,0:T(8,128)S(1)}, u32[]{:S(2)}, u32[]{:S(2)}) collective-permute-start(f32[64,1024]{1,0:T(8,128)S(1)} %get-tuple-element.17), channel_id=1, source_target_pairs={{0,4},{8,12},{16,20},{24,28},{4,0},{12,8},{20,16},{28,24},{1,5},{9... | collective-permute-start | bytes 786440 | tf_op jit(solution)/shard_map/ppermute | solution.py:520
  39.2 1.4 %collective-permute-start.9 = (f32[64,1024]{1,0:T(8,128)S(1)}, f32[64,1024]{1,0:T(8,128)S(1)}, u32[]{:S(2)}, u32[]{:S(2)}) collective-permute-start(f32[64,1024]{1,0:T(8,128)S(1)} %get-tuple-element.18), channel_id=1, source_target_pairs={{4,8},{12,16},{20,24},{8,4},{16,12},{24,20},{5,9},{13,17},{21,25},... | collective-permute-start | bytes 786440 | tf_op jit(solution)/shard_map/ppermute | solution.py:520
  41.3 4.6 %collective-permute-start.12 = (f32[176,128]{1,0:T(8,128)S(1)}, f32[176,128]{1,0:T(8,128)S(1)}, u32[]{:S(2)}, u32[]{:S(2)}) collective-permute-start(f32[176,128]{1,0:T(8,128)S(1)} %get-tuple-element.21), channel_id=1, source_target_pairs={{0,1},{2,3},{1,0},{3,2},{4,5},{6,7},{5,4},{7,6},{8,9},{10,11},{9,8... | collective-permute-start | bytes 270344 | tf_op jit(solution)/shard_map/ppermute | solution.py:520
  42.2 3.7 %copy-start.3 = (f32[8]{0:T(128)S(1)}, f32[8]{0:T(128)}, u32[]{:S(2)}) copy-start(f32[8]{0:T(128)} %weight_ref.1) | copy-start | bytes 100
  42.2 3.7 %collective-permute-start.13 = (f32[176,128]{1,0:T(8,128)S(1)}, f32[176,128]{1,0:T(8,128)S(1)}, u32[]{:S(2)}, u32[]{:S(2)}) collective-permute-start(f32[176,128]{1,0:T(8,128)S(1)} %get-tuple-element.22), channel_id=1, source_target_pairs={{1,2},{2,1},{5,6},{6,5},{9,10},{10,9},{13,14},{14,13},{17,18},{18,... | collective-permute-start | bytes 270344 | tf_op jit(solution)/shard_map/ppermute | solution.py:520
  64.1 40.1 %copy-start.2 = (f32[32,1024]{1,0:T(8,128)S(1)}, f32[32,1024]{1,0:T(8,128)}, u32[]{:S(2)}) copy-start(f32[32,1024]{1,0:T(8,128)} %param.6) | copy-start | bytes 393220

commit v9 on v8

--- a/solution.py
+++ b/solution.py
@@ -197,7 +197,10 @@
 
 def edges_kernel(spot_ref, mask_ref, rowa_ref, rowb_ref, target_ref, ttop_ref, tbottom_ref, *rest):
     cola_ref, colb_ref, pack_ref = rest[-3:]
-    odd_row, odd_col = spot_ref[6] > 0, spot_ref[7] > 0
+
+    def odd(n, x, y):
+        return jnp.where(jnp.broadcast_to(spot_ref[n : n + 1, :], x.shape) > 0, x, y)
+
     height, breadth = mask_ref.shape
     wide = 2 * HALF
     half = height // 2
@@ -207,7 +210,7 @@
 
     def halves(lanes):
         one, other = rowa_ref[:, lanes], rowb_ref[:, lanes]
-        top, bottom = jnp.where(odd_row, one, other), jnp.where(odd_row, other, one)
+        top, bottom = odd(6, one, other), odd(6, other, one)
         upper = jnp.concatenate([top, mask_ref[:half, lanes]], axis=0)
         return upper, jnp.concatenate([mask_ref[half:, lanes], bottom], axis=0)
 
@@ -215,8 +218,8 @@
     left = jnp.where(lane < wide, upper, pltpu.roll(lower, wide, 1))
     upper, lower = halves(tail)
     right = jnp.where(lane < wide, pltpu.roll(upper, wide, 1), lower)
-    cola_ref[:packed, :] = jnp.where(odd_col, left, right)
-    colb_ref[:packed, :] = jnp.where(odd_col, right, left)
+    cola_ref[:packed, :] = odd(7, left, right)
+    colb_ref[:packed, :] = odd(7, right, left)
 
     quarter = (height + 2 * HALF) // 4
 
@@ -236,8 +239,8 @@
         for part in range(1, 4):
             piece = jnp.where(part_of == part, pack_ref[side, part], piece)
         sides.append(piece)
-    cola_ref[packed:, :] = jnp.where(odd_col, sides[0], sides[1])
-    colb_ref[packed:, :] = jnp.where(odd_col, sides[1], sides[0])
+    cola_ref[packed:, :] = odd(7, sides[0], sides[1])
+    colb_ref[packed:, :] = odd(7, sides[1], sides[0])
 
 
 def image_kernel(
@@ -632,8 +635,8 @@
         "edges",
         [edge, edge],
         [pltpu.VMEM((2, 4, quarter, LANES), F32)],
-        [me],
-        [mask, rowa, rowb, target, above, below],
+        [],
+        [jnp.broadcast_to(me[:, None], (8, LANES)), mask, rowa, rowb, target, above, below],
         [wanted],
     )
     cola, colb = pairs(cola, colb, "col")

time: 107 us -> 106 us (level)
  transfers between devices with their start and end apart: 15 -> 15, of which waited for: 8 -> 8; matrix products, arithmetic and copies ran while one was open for 3% -> 4% of each run, Pallas kernels for 1% -> 1%
where the time goes in v9:
time: 106 us
  blocking collectives  40.1 us (38%)
  Pallas kernels  23.8 us (22%)
  starting transfers between devices  19 us (18%)
  waiting for transfers between devices  18.2 us (17%)
  other arithmetic  3.22 us (3%)
  local copies, waits for them, and re-layouts  1.51 us (1%)
    all_to_all x1, blocking collectives, shards(): lax.all_to_all(returned, everyone, split_axis=0, concat_axis=0, tiled=True)  40.1 us
    pallas_call x6, Pallas kernels, kernel_call(): pl.pallas_call(body, out_shape=outs, in_specs=[pl.BlockSpec(memory_space=...  23.8 us
    ppermute x5, waiting for transfers between devices, doubled(): got = lax.ppermute(table, axis, [(i, i ^ bit) for i in range(count)])  8.52 us
    ppermute x5, starting transfers between devices, doubled(): got = lax.ppermute(table, axis, [(i, i ^ bit) for i in range(count)])  5.86 us
    all_to_all x1, waiting for transfers between devices, shards(): lax.all_to_all(packed, plane, split_axis=0, concat_axis=0, tiled=True)  5.85 us
    ppermute x3, starting transfers between devices, shards(): lax.ppermute(ordered, 'deep', [(i, i ^ e) for i in range(deep)])  5.76 us
    all_to_all x1, starting transfers between devices, shards(): lax.all_to_all(packed, plane, split_axis=0, concat_axis=0, tiled=True)  3.72 us
    ppermute x6, starting transfers between devices, exchange(): return lax.ppermute(x, axis, swap + [(j, i) for i, j in swap])  3.63 us
  transfers between devices with their start and end apart: 15, of which 8 were waited for; matrix products, arithmetic and copies ran while one was open for 4% of the time, Pallas kernels for 1%

profile of v9, /device:TPU:0, one launch (start us, length us, event | category | flops | bytes accessed | tf_op | source)
XLA Modules:
  0.0 106.1 jit_solution(11578985186584335124)
XLA Ops:
  0.0 0.9 copy-done.1
  0.9 5.1 %collective-permute-start.5 = (f32[256,128]{1,0:T(8,128)S(1)}, f32[256,128]{1,0:T(8,128)S(1)}, u32[]{:S(2)}, u32[]{:S(2)}) collective-permute-start(f32[256,128]{1,0:T(8,128)S(1)} %spread.1.rest_0_), channel_id=1, source_target_pairs={{0,24},{8,16},{16,8},{24,0},{1,25},{9,17},{17,9},{25,1},{2,26},{10... | collective-permute-start | bytes 393224 | tf_op jit(solution)/shard_map/ppermute | solution.py:564
  6.1 0.6 collective-permute-start.3
  6.8 1.6 %collective-permute-start = (s32[1,128]{1,0:T(1,128)S(1)}, s32[1,128]{1,0:T(1,128)S(1)}, u32[]{:S(2)}, u32[]{:S(2)}) collective-permute-start(s32[1,128]{1,0:T(1,128)S(1)} %concatenate.86), channel_id=1, source_target_pairs={{0,1},{1,0},{2,3},{3,2},{4,5},{5,4},{6,7},{7,6},{8,9},{9,8},{10,11... | collective-permute-start | bytes 1544 | tf_op jit(solution)/shard_map/ppermute | solution.py:533
  8.7 1.0 slice_select_fusion
  9.8 0.5 collective-permute-done
  10.3 1.7 %collective-permute-start.1 = (s32[2,128]{1,0:T(2,128)S(1)}, s32[2,128]{1,0:T(2,128)S(1)}, u32[]{:S(2)}, u32[]{:S(2)}) collective-permute-start(s32[2,128]{1,0:T(2,128)S(1)} %pad_add_fusion.3), channel_id=1, source_target_pairs={{0,2},{1,3},{2,0},{3,1},{4,6},{5,7},{6,4},{7,5},{8,10},{9,11},{10,... | collective-permute-start | bytes 3080 | tf_op jit(solution)/shard_map/ppermute | solution.py:533
  12.0 1.9 %collective-permute-done.1 = s32[2,128]{1,0:T(2,128)S(1)} collective-permute-done((s32[2,128]{1,0:T(2,128)S(1)}, s32[2,128]{1,0:T(2,128)S(1)}, u32[]{:S(2)}, u32[]{:S(2)}) %collective-permute-start.1) | collective-permute-done | bytes 1056 | tf_op jit(solution)/shard_map/ppermute | solution.py:533
  14.3 0.9 collective-permute-done.2
  15.2 0.3 reduce_window_sum.17
  15.5 0.6 select_reduce_fusion.1
  16.2 1.0 collective-permute-done.4.rest_2_
  17.1 2.0 %pack.1 = f32[2048,128]{1,0:T(8,128)} custom-call(s32[8,4,8]{2,1,0:T(4,128)S(1)} %bitcast.28, s32[8]{0:T(128)S(1)} %stack.27.me_ref.spot_ref, f32[256,128]{1,0:T(8,128)S(1)} %spread.1.rest_0_, f32[256,128]{1,0:T(8,128)S(1)} %collective-permute-done.3.rest_1_, f32[256,128]{1,0:T(8,128)S(1)} %collective-permute-done.4.rest_2_, ...), custom_call_target="tpu_custom_call" | custom-call | tf_op jit(solution)/shard_map/pack/pallas_call | solution.py:504
  19.1 3.7 %all-to-all-start = ((f32[8,256,128]{2,1,0:T(8,128)}), f32[8,256,128]{2,1,0:T(8,128)S(1)}, u32[]{:S(2)}, u32[]{:S(2)}) async-start(f32[8,256,128]{2,1,0:T(8,128)} %bitcast.12), calls=%async_computation | async-start | bytes 2097152 | tf_op jit(solution)/shard_map/all_to_all | solution.py:605
  22.9 0.5 collective-permute-start.6
  23.4 0.2 collective-permute-start.10
  23.6 0.7 collective-permute-start.11
  24.3 2.3 %collective-permute-done.6 = s32[8,128]{1,0:T(8,128)S(1)} collective-permute-done((s32[8,128]{1,0:T(8,128)S(1)}, s32[8,128]{1,0:T(8,128)S(1)}, u32[]{:S(2)}, u32[]{:S(2)}) %collective-permute-start.6) | collective-permute-done | bytes 4128 | tf_op jit(solution)/shard_map/ppermute | solution.py:533
  26.6 2.0 %collective-permute-start.7 = (s32[16,128]{1,0:T(8,128)S(1)}, s32[16,128]{1,0:T(8,128)S(1)}, u32[]{:S(2)}, u32[]{:S(2)}) collective-permute-start(s32[16,128]{1,0:T(8,128)S(1)} %pad_add_fusion), channel_id=1, source_target_pairs={{0,16},{8,24},{16,0},{24,8},{1,17},{9,25},{17,1},{25,9},{2,18},{10... | collective-permute-start | bytes 24584 | tf_op jit(solution)/shard_map/ppermute | solution.py:533
  28.6 3.0 %collective-permute-done.7 = s32[16,128]{1,0:T(8,128)S(1)} collective-permute-done((s32[16,128]{1,0:T(8,128)S(1)}, s32[16,128]{1,0:T(8,128)S(1)}, u32[]{:S(2)}, u32[]{:S(2)}) %collective-permute-start.7) | collective-permute-done | bytes 8224 | tf_op jit(solution)/shard_map/ppermute | solution.py:533
  31.6 0.3 reduce_window_sum.18
  31.9 5.9 %all-to-all-done = f32[8,256,128]{2,1,0:T(8,128)S(1)} async-done(((f32[8,256,128]{2,1,0:T(8,128)}), f32[8,256,128]{2,1,0:T(8,128)S(1)}, u32[]{:S(2)}, u32[]{:S(2)}) %all-to-all-start) | async-done | bytes 1048608 | tf_op jit(solution)/shard_map/all_to_all | solution.py:605
  37.7 1.1 %assemble.1 = (f32[128,1024]{1,0:T(8,128)S(1)}, f32[64,1024]{1,0:T(8,128)S(1)}, f32[64,1024]{1,0:T(8,128)S(1)}) custom-call(s32[4,32]{1,0:T(4,128)S(1)} %get-tuple-element.23.index_ref, s32[8]{0:T(128)S(1)} %stack.27.me_ref.spot_ref, f32[2048,128]{1,0:T(8,128)S(1)} %bitcast.24), custom_call_target="tpu_custom_call" | custom-call | tf_op jit(solution)/shard_map/assemble/pallas_call | solution.py:504
  38.9 0.4 collective-permute-start.8
  39.2 0.7 collective-permute-start.9
  39.9 0.6 select_reduce_fusion.rest_0_.asked_ref
  40.8 0.9 collective-permute-start.12
  41.8 0.8 collective-permute-start.13
  42.5 2.9 %collective-permute-done.12.cola_ref = f32[176,128]{1,0:T(8,128)S(1)} collective-permute-done((f32[176,128]{1,0:T(8,128)S(1)}, f32[176,128]{1,0:T(8,128)S(1)}, u32[]{:S(2)}, u32[]{:S(2)}) %collective-permute-start.12) | collective-permute-done | bytes 90144 | tf_op jit(solution)/shard_map/ppermute | solution.py:523
  45.4 18.2 %image.1 = f32[2048,128]{1,0:T(8,128)S(1)} custom-call(s32[4,32]{1,0:T(4,128)S(1)} %get-tuple-element.24.index_ref, s32[8]{0:T(128)S(1)} %stack.27.me_ref.spot_ref, f32[8]{0:T(128)S(1)} %copy-done.3, f32[128,1024]{1,0:T(8,128)S(1)} %get-tuple-element.16.mask_ref, f32[64,1024]{1,0:T(8,128)S(1)} %collective-permute-done.8.rowa_ref, ...), custom_call_target="tpu_custom_call" | custom-call | tf_op jit(solution)/shard_map/image/pallas_call | solution.py:504
  63.6 40.1 %all_to_all.22 = f32[32,64,128]{2,1,0:T(8,128)S(1)} all-to-all(f32[32,64,128]{2,1,0:T(8,128)S(1)} %bitcast.23), channel_id=1, replica_groups=mesh['deep'=4,'core'=2,'col'=4] {'deep','core','col'}, dimensions={0} | all-to-all | bytes 2097152 | tf_op jit(solution)/shard_map/all_to_all | solution.py:667
  103.7 2.4 %step.1 = f32[256,128]{1,0:T(8,128)} custom-call(s32[32,8]{1,0:T(8,128)S(1)} %select_reduce_fusion.rest_0_.asked_ref, s32[8]{0:T(128)S(1)} %stack.27.me_ref.spot_ref, f32[256,128]{1,0:T(8,128)S(1)} %bitcast.27, f32[2048,128]{1,0:T(8,128)S(1)} %bitcast.25), custom_call_target="tpu_custom_call" | custom-call | tf_op jit(solution)/shard_map/step/pallas_call | solution.py:504
  (53 shorter events, 1.3 us)
Async XLA Ops:
  0.0 0.9 copy-start.1
  0.9 5.8 %copy-start.4 = (s32[4,32]{1,0:T(4,128)S(1)}, s32[4,32]{1,0:T(4,128)}, u32[]{:S(2)}) copy-start(s32[4,32]{1,0:T(4,128)} %param.7) | copy-start | bytes 1540
  0.9 15.2 %collective-permute-start.5 = (f32[256,128]{1,0:T(8,128)S(1)}, f32[256,128]{1,0:T(8,128)S(1)}, u32[]{:S(2)}, u32[]{:S(2)}) collective-permute-start(f32[256,128]{1,0:T(8,128)S(1)} %spread.1.rest_0_), channel_id=1, source_target_pairs={{0,24},{8,16},{16,8},{24,0},{1,25},{9,17},{17,9},{25,1},{2,26},{10... | collective-permute-start | bytes 393224 | tf_op jit(solution)/shard_map/ppermute | solution.py:564
  6.1 11.1 %collective-permute-start.4 = (f32[256,128]{1,0:T(8,128)S(1)}, f32[256,128]{1,0:T(8,128)S(1)}, u32[]{:S(2)}, u32[]{:S(2)}) collective-permute-start(f32[256,128]{1,0:T(8,128)S(1)} %spread.1.rest_0_), channel_id=1, source_target_pairs={{0,16},{8,24},{16,0},{24,8},{1,17},{9,25},{17,1},{25,9},{2,18},{10... | collective-permute-start | bytes 393224 | tf_op jit(solution)/shard_map/ppermute | solution.py:564
  6.1 11.1 %collective-permute-start.3 = (f32[256,128]{1,0:T(8,128)S(1)}, f32[256,128]{1,0:T(8,128)S(1)}, u32[]{:S(2)}, u32[]{:S(2)}) collective-permute-start(f32[256,128]{1,0:T(8,128)S(1)} %spread.1.rest_0_), channel_id=1, source_target_pairs={{0,8},{8,0},{16,24},{24,16},{1,9},{9,1},{17,25},{25,17},{2,10},{10... | collective-permute-start | bytes 393224 | tf_op jit(solution)/shard_map/ppermute | solution.py:564
  6.8 3.5 %collective-permute-start = (s32[1,128]{1,0:T(1,128)S(1)}, s32[1,128]{1,0:T(1,128)S(1)}, u32[]{:S(2)}, u32[]{:S(2)}) collective-permute-start(s32[1,128]{1,0:T(1,128)S(1)} %concatenate.86), channel_id=1, source_target_pairs={{0,1},{1,0},{2,3},{3,2},{4,5},{5,4},{6,7},{7,6},{8,9},{9,8},{10,11... | collective-permute-start | bytes 1544 | tf_op jit(solution)/shard_map/ppermute | solution.py:533
  8.7 1.0 copy-start.5
  8.7 1.0 copy-start.6
  10.3 3.6 %collective-permute-start.1 = (s32[2,128]{1,0:T(2,128)S(1)}, s32[2,128]{1,0:T(2,128)S(1)}, u32[]{:S(2)}, u32[]{:S(2)}) collective-permute-start(s32[2,128]{1,0:T(2,128)S(1)} %pad_add_fusion.3), channel_id=1, source_target_pairs={{0,2},{1,3},{2,0},{3,1},{4,6},{5,7},{6,4},{7,5},{8,10},{9,11},{10,... | collective-permute-start | bytes 3080 | tf_op jit(solution)/shard_map/ppermute | solution.py:533
  13.9 1.2 %collective-permute-start.2 = (s32[4,128]{1,0:T(4,128)S(1)}, s32[4,128]{1,0:T(4,128)S(1)}, u32[]{:S(2)}, u32[]{:S(2)}) collective-permute-start(s32[4,128]{1,0:T(4,128)S(1)} %pad_add_fusion.2), channel_id=1, source_target_pairs={{0,4},{4,0},{1,5},{5,1},{2,6},{6,2},{3,7},{7,3},{8,12},{12,8},{9,1... | collective-permute-start | bytes 6152 | tf_op jit(solution)/shard_map/ppermute | solution.py:533
  19.1 18.6 %all-to-all-start = ((f32[8,256,128]{2,1,0:T(8,128)}), f32[8,256,128]{2,1,0:T(8,128)S(1)}, u32[]{:S(2)}, u32[]{:S(2)}) async-start(f32[8,256,128]{2,1,0:T(8,128)} %bitcast.12), calls=%async_computation | async-start | bytes 2097152 | tf_op jit(solution)/shard_map/all_to_all | solution.py:605
  22.9 3.7 %collective-permute-start.6 = (s32[8,128]{1,0:T(8,128)S(1)}, s32[8,128]{1,0:T(8,128)S(1)}, u32[]{:S(2)}, u32[]{:S(2)}) collective-permute-start(s32[8,128]{1,0:T(8,128)S(1)} %get-tuple-element.14), channel_id=1, source_target_pairs={{0,8},{8,0},{16,24},{24,16},{1,9},{9,1},{17,25},{25,17},{2,10},{10... | collective-permute-start | bytes 12296 | tf_op jit(solution)/shard_map/ppermute | solution.py:533
  23.4 17.1 %collective-permute-start.10 = (f32[32,1024]{1,0:T(8,128)S(1)}, f32[32,1024]{1,0:T(8,128)S(1)}, u32[]{:S(2)}, u32[]{:S(2)}) collective-permute-start(f32[32,1024]{1,0:T(8,128)S(1)} %get-tuple-element.19), channel_id=1, source_target_pairs={{0,4},{8,12},{16,20},{24,28},{4,0},{12,8},{20,16},{28,24},{1,5},{9... | collective-permute-start | bytes 393224 | tf_op jit(solution)/shard_map/ppermute | solution.py:523
  23.6 16.9 %collective-permute-start.11 = (f32[32,1024]{1,0:T(8,128)S(1)}, f32[32,1024]{1,0:T(8,128)S(1)}, u32[]{:S(2)}, u32[]{:S(2)}) collective-permute-start(f32[32,1024]{1,0:T(8,128)S(1)} %get-tuple-element.20), channel_id=1, source_target_pairs={{4,8},{12,16},{20,24},{8,4},{16,12},{24,20},{5,9},{13,17},{21,25},... | collective-permute-start | bytes 393224 | tf_op jit(solution)/shard_map/ppermute | solution.py:523
  26.6 5.0 %collective-permute-start.7 = (s32[16,128]{1,0:T(8,128)S(1)}, s32[16,128]{1,0:T(8,128)S(1)}, u32[]{:S(2)}, u32[]{:S(2)}) collective-permute-start(s32[16,128]{1,0:T(8,128)S(1)} %pad_add_fusion), channel_id=1, source_target_pairs={{0,16},{8,24},{16,0},{24,8},{1,17},{9,25},{17,1},{25,9},{2,18},{10... | collective-permute-start | bytes 24584 | tf_op jit(solution)/shard_map/ppermute | solution.py:533
  38.9 1.8 %copy-start = (f32[128,1024]{1,0:T(8,128)S(1)}, f32[128,1024]{1,0:T(8,128)}, u32[]{:S(2)}) copy-start(f32[128,1024]{1,0:T(8,128)} %own_ref.1) | copy-start | bytes 1572868
  38.9 1.7 %collective-permute-start.8 = (f32[64,1024]{1,0:T(8,128)S(1)}, f32[64,1024]{1,0:T(8,128)S(1)}, u32[]{:S(2)}, u32[]{:S(2)}) collective-permute-start(f32[64,1024]{1,0:T(8,128)S(1)} %get-tuple-element.17), channel_id=1, source_target_pairs={{0,4},{8,12},{16,20},{24,28},{4,0},{12,8},{20,16},{28,24},{1,5},{9... | collective-permute-start | bytes 786440 | tf_op jit(solution)/shard_map/ppermute | solution.py:523
  39.2 1.4 %collective-permute-start.9 = (f32[64,1024]{1,0:T(8,128)S(1)}, f32[64,1024]{1,0:T(8,128)S(1)}, u32[]{:S(2)}, u32[]{:S(2)}) collective-permute-start(f32[64,1024]{1,0:T(8,128)S(1)} %get-tuple-element.18), channel_id=1, source_target_pairs={{4,8},{12,16},{20,24},{8,4},{16,12},{24,20},{5,9},{13,17},{21,25},... | collective-permute-start | bytes 786440 | tf_op jit(solution)/shard_map/ppermute | solution.py:523
  40.8 4.6 %collective-permute-start.12 = (f32[176,128]{1,0:T(8,128)S(1)}, f32[176,128]{1,0:T(8,128)S(1)}, u32[]{:S(2)}, u32[]{:S(2)}) collective-permute-start(f32[176,128]{1,0:T(8,128)S(1)} %get-tuple-element.21), channel_id=1, source_target_pairs={{0,1},{2,3},{1,0},{3,2},{4,5},{6,7},{5,4},{7,6},{8,9},{10,11},{9,8... | collective-permute-start | bytes 270344 | tf_op jit(solution)/shard_map/ppermute | solution.py:523
  41.7 3.7 %copy-start.3 = (f32[8]{0:T(128)S(1)}, f32[8]{0:T(128)}, u32[]{:S(2)}) copy-start(f32[8]{0:T(128)} %weight_ref.1) | copy-start | bytes 100
  41.8 3.7 %collective-permute-start.13 = (f32[176,128]{1,0:T(8,128)S(1)}, f32[176,128]{1,0:T(8,128)S(1)}, u32[]{:S(2)}, u32[]{:S(2)}) collective-permute-start(f32[176,128]{1,0:T(8,128)S(1)} %get-tuple-element.22), channel_id=1, source_target_pairs={{1,2},{2,1},{5,6},{6,5},{9,10},{10,9},{13,14},{14,13},{17,18},{18,... | collective-permute-start | bytes 270344 | tf_op jit(solution)/shard_map/ppermute | solution.py:523
  63.6 40.1 %copy-start.2 = (f32[32,1024]{1,0:T(8,128)S(1)}, f32[32,1024]{1,0:T(8,128)}, u32[]{:S(2)}) copy-start(f32[32,1024]{1,0:T(8,128)} %param.6) | copy-start | bytes 393220

commit v10 on v9

--- a/solution.py
+++ b/solution.py
@@ -592,7 +592,6 @@
         [pltpu.VMEM((size, LANES), F32), pltpu.SemaphoreType.DMA((peers,))],
         [asked, me],
         levels,
-        [waves],
         out_space=pl.ANY,
     )
     odd = me[6] > 0

time: 106 us -> 106 us (level)
  transfers between devices with their start and end apart: 15 -> 15, of which waited for: 8 -> 8; matrix products, arithmetic and copies ran while one was open for 4% -> 3% of each run, Pallas kernels for 1% -> 1%
where the time goes in v10:
time: 106 us
  blocking collectives  40 us (38%)
  Pallas kernels  23.8 us (22%)
  starting transfers between devices  18.8 us (18%)
  waiting for transfers between devices  18.4 us (17%)
  other arithmetic  3.2 us (3%)
  local copies, waits for them, and re-layouts  1.51 us (1%)
    all_to_all x1, blocking collectives, shards(): lax.all_to_all(returned, everyone, split_axis=0, concat_axis=0, tiled=True)  40 us
    pallas_call x6, Pallas kernels, kernel_call(): pl.pallas_call(body, out_shape=outs, in_specs=[pl.BlockSpec(memory_space=...  23.8 us
    ppermute x5, waiting for transfers between devices, doubled(): got = lax.ppermute(table, axis, [(i, i ^ bit) for i in range(count)])  8.63 us
    all_to_all x1, waiting for transfers between devices, shards(): lax.all_to_all(packed, plane, split_axis=0, concat_axis=0, tiled=True)  5.84 us
    ppermute x5, starting transfers between devices, doubled(): got = lax.ppermute(table, axis, [(i, i ^ bit) for i in range(count)])  5.8 us
    ppermute x3, starting transfers between devices, shards(): lax.ppermute(ordered, 'deep', [(i, i ^ e) for i in range(deep)])  5.76 us
    all_to_all x1, starting transfers between devices, shards(): lax.all_to_all(packed, plane, split_axis=0, concat_axis=0, tiled=True)  3.72 us
    ppermute x6, starting transfers between devices, exchange(): return lax.ppermute(x, axis, swap + [(j, i) for i, j in swap])  3.49 us
  transfers between devices with their start and end apart: 15, of which 8 were waited for; matrix products, arithmetic and copies ran while one was open for 3% of the time, Pallas kernels for 1%

profile of v10, /device:TPU:0, one launch (start us, length us, event | category | flops | bytes accessed | tf_op | source)
XLA Modules:
  0.0 106.0 jit_solution(18348982704615135866)
XLA Ops:
  0.0 0.9 copy-done.1
  0.9 5.1 %collective-permute-start.5 = (f32[256,128]{1,0:T(8,128)S(1)}, f32[256,128]{1,0:T(8,128)S(1)}, u32[]{:S(2)}, u32[]{:S(2)}) collective-permute-start(f32[256,128]{1,0:T(8,128)S(1)} %spread.1.rest_0_), channel_id=1, source_target_pairs={{0,24},{8,16},{16,8},{24,0},{1,25},{9,17},{17,9},{25,1},{2,26},{10... | collective-permute-start | bytes 393224 | tf_op jit(solution)/shard_map/ppermute | solution.py:564
  6.1 0.6 collective-permute-start.3
  6.8 1.6 %collective-permute-start = (s32[1,128]{1,0:T(1,128)S(1)}, s32[1,128]{1,0:T(1,128)S(1)}, u32[]{:S(2)}, u32[]{:S(2)}) collective-permute-start(s32[1,128]{1,0:T(1,128)S(1)} %concatenate.86), channel_id=1, source_target_pairs={{0,1},{1,0},{2,3},{3,2},{4,5},{5,4},{6,7},{7,6},{8,9},{9,8},{10,11... | collective-permute-start | bytes 1544 | tf_op jit(solution)/shard_map/ppermute | solution.py:533
  8.5 1.0 slice_select_fusion
  9.8 0.5 collective-permute-done
  10.3 1.7 %collective-permute-start.1 = (s32[2,128]{1,0:T(2,128)S(1)}, s32[2,128]{1,0:T(2,128)S(1)}, u32[]{:S(2)}, u32[]{:S(2)}) collective-permute-start(s32[2,128]{1,0:T(2,128)S(1)} %pad_add_fusion.3), channel_id=1, source_target_pairs={{0,2},{1,3},{2,0},{3,1},{4,6},{5,7},{6,4},{7,5},{8,10},{9,11},{10,... | collective-permute-start | bytes 3080 | tf_op jit(solution)/shard_map/ppermute | solution.py:533
  12.0 1.9 %collective-permute-done.1 = s32[2,128]{1,0:T(2,128)S(1)} collective-permute-done((s32[2,128]{1,0:T(2,128)S(1)}, s32[2,128]{1,0:T(2,128)S(1)}, u32[]{:S(2)}, u32[]{:S(2)}) %collective-permute-start.1) | collective-permute-done | bytes 1056 | tf_op jit(solution)/shard_map/ppermute | solution.py:533
  14.2 0.9 collective-permute-done.2
  15.2 0.3 reduce_window_sum.17
  15.5 0.6 select_reduce_fusion.1
  16.2 1.0 collective-permute-done.4.rest_2_
  17.1 2.0 %pack.1 = f32[2048,128]{1,0:T(8,128)} custom-call(s32[8,4,8]{2,1,0:T(4,128)S(1)} %bitcast.28, s32[8]{0:T(128)S(1)} %stack.27.me_ref.spot_ref, f32[256,128]{1,0:T(8,128)S(1)} %spread.1.rest_0_, f32[256,128]{1,0:T(8,128)S(1)} %collective-permute-done.3.rest_1_, f32[256,128]{1,0:T(8,128)S(1)} %collective-permute-done.4.rest_2_, ...), custom_call_target="tpu_custom_call" | custom-call | tf_op jit(solution)/shard_map/pack/pallas_call | solution.py:504
  19.2 3.7 %all-to-all-start = ((f32[8,256,128]{2,1,0:T(8,128)}), f32[8,256,128]{2,1,0:T(8,128)S(1)}, u32[]{:S(2)}, u32[]{:S(2)}) async-start(f32[8,256,128]{2,1,0:T(8,128)} %bitcast.12), calls=%async_computation | async-start | bytes 2097152 | tf_op jit(solution)/shard_map/all_to_all | solution.py:604
  23.0 0.4 collective-permute-start.6
  23.4 0.2 collective-permute-start.10
  23.7 0.7 collective-permute-start.11
  24.3 2.3 %collective-permute-done.6 = s32[8,128]{1,0:T(8,128)S(1)} collective-permute-done((s32[8,128]{1,0:T(8,128)S(1)}, s32[8,128]{1,0:T(8,128)S(1)}, u32[]{:S(2)}, u32[]{:S(2)}) %collective-permute-start.6) | collective-permute-done | bytes 4128 | tf_op jit(solution)/shard_map/ppermute | solution.py:533
  26.6 2.0 %collective-permute-start.7 = (s32[16,128]{1,0:T(8,128)S(1)}, s32[16,128]{1,0:T(8,128)S(1)}, u32[]{:S(2)}, u32[]{:S(2)}) collective-permute-start(s32[16,128]{1,0:T(8,128)S(1)} %pad_add_fusion), channel_id=1, source_target_pairs={{0,16},{8,24},{16,0},{24,8},{1,17},{9,25},{17,1},{25,9},{2,18},{10... | collective-permute-start | bytes 24584 | tf_op jit(solution)/shard_map/ppermute | solution.py:533
  28.6 3.0 %collective-permute-done.7 = s32[16,128]{1,0:T(8,128)S(1)} collective-permute-done((s32[16,128]{1,0:T(8,128)S(1)}, s32[16,128]{1,0:T(8,128)S(1)}, u32[]{:S(2)}, u32[]{:S(2)}) %collective-permute-start.7) | collective-permute-done | bytes 8224 | tf_op jit(solution)/shard_map/ppermute | solution.py:533
  31.6 0.3 reduce_window_sum.18
  31.9 5.8 %all-to-all-done = f32[8,256,128]{2,1,0:T(8,128)S(1)} async-done(((f32[8,256,128]{2,1,0:T(8,128)}), f32[8,256,128]{2,1,0:T(8,128)S(1)}, u32[]{:S(2)}, u32[]{:S(2)}) %all-to-all-start) | async-done | bytes 1048608 | tf_op jit(solution)/shard_map/all_to_all | solution.py:604
  37.8 1.1 %assemble.1 = (f32[128,1024]{1,0:T(8,128)S(1)}, f32[64,1024]{1,0:T(8,128)S(1)}, f32[64,1024]{1,0:T(8,128)S(1)}) custom-call(s32[4,32]{1,0:T(4,128)S(1)} %get-tuple-element.23.index_ref, s32[8]{0:T(128)S(1)} %stack.27.me_ref.spot_ref, f32[2048,128]{1,0:T(8,128)S(1)} %bitcast.24), custom_call_target="tpu_custom_call" | custom-call | tf_op jit(solution)/shard_map/assemble/pallas_call | solution.py:504
  38.9 0.4 collective-permute-start.8
  39.3 0.7 collective-permute-start.9
  39.9 0.6 select_reduce_fusion.rest_0_.asked_ref
  40.8 0.9 collective-permute-start.12
  41.8 0.7 collective-permute-start.13
  42.5 3.0 %collective-permute-done.12.cola_ref = f32[176,128]{1,0:T(8,128)S(1)} collective-permute-done((f32[176,128]{1,0:T(8,128)S(1)}, f32[176,128]{1,0:T(8,128)S(1)}, u32[]{:S(2)}, u32[]{:S(2)}) %collective-permute-start.12) | collective-permute-done | bytes 90144 | tf_op jit(solution)/shard_map/ppermute | solution.py:523
  45.4 18.2 %image.1 = f32[2048,128]{1,0:T(8,128)S(1)} custom-call(s32[4,32]{1,0:T(4,128)S(1)} %get-tuple-element.24.index_ref, s32[8]{0:T(128)S(1)} %stack.27.me_ref.spot_ref, f32[8]{0:T(128)S(1)} %copy-done.3, f32[128,1024]{1,0:T(8,128)S(1)} %get-tuple-element.16.mask_ref, f32[64,1024]{1,0:T(8,128)S(1)} %collective-permute-done.8.rowa_ref, ...), custom_call_target="tpu_custom_call" | custom-call | tf_op jit(solution)/shard_map/image/pallas_call | solution.py:504
  63.7 40.0 %all_to_all.22 = f32[32,64,128]{2,1,0:T(8,128)S(1)} all-to-all(f32[32,64,128]{2,1,0:T(8,128)S(1)} %bitcast.23), channel_id=1, replica_groups=mesh['deep'=4,'core'=2,'col'=4] {'deep','core','col'}, dimensions={0} | all-to-all | bytes 2097152 | tf_op jit(solution)/shard_map/all_to_all | solution.py:666
  103.6 2.4 %step.1 = f32[256,128]{1,0:T(8,128)} custom-call(s32[32,8]{1,0:T(8,128)S(1)} %select_reduce_fusion.rest_0_.asked_ref, s32[8]{0:T(128)S(1)} %stack.27.me_ref.spot_ref, f32[256,128]{1,0:T(8,128)S(1)} %bitcast.27, f32[2048,128]{1,0:T(8,128)S(1)} %bitcast.25), custom_call_target="tpu_custom_call" | custom-call | tf_op jit(solution)/shard_map/step/pallas_call | solution.py:504
  (53 shorter events, 1.3 us)
Async XLA Ops:
  0.0 0.9 copy-start.1
  0.9 5.8 %copy-start.4 = (s32[4,32]{1,0:T(4,128)S(1)}, s32[4,32]{1,0:T(4,128)}, u32[]{:S(2)}) copy-start(s32[4,32]{1,0:T(4,128)} %param.7) | copy-start | bytes 1540
  0.9 15.2 %collective-permute-start.5 = (f32[256,128]{1,0:T(8,128)S(1)}, f32[256,128]{1,0:T(8,128)S(1)}, u32[]{:S(2)}, u32[]{:S(2)}) collective-permute-start(f32[256,128]{1,0:T(8,128)S(1)} %spread.1.rest_0_), channel_id=1, source_target_pairs={{0,24},{8,16},{16,8},{24,0},{1,25},{9,17},{17,9},{25,1},{2,26},{10... | collective-permute-start | bytes 393224 | tf_op jit(solution)/shard_map/ppermute | solution.py:564
  6.1 11.1 %collective-permute-start.4 = (f32[256,128]{1,0:T(8,128)S(1)}, f32[256,128]{1,0:T(8,128)S(1)}, u32[]{:S(2)}, u32[]{:S(2)}) collective-permute-start(f32[256,128]{1,0:T(8,128)S(1)} %spread.1.rest_0_), channel_id=1, source_target_pairs={{0,16},{8,24},{16,0},{24,8},{1,17},{9,25},{17,1},{25,9},{2,18},{10... | collective-permute-start | bytes 393224 | tf_op jit(solution)/shard_map/ppermute | solution.py:564
  6.1 11.1 %collective-permute-start.3 = (f32[256,128]{1,0:T(8,128)S(1)}, f32[256,128]{1,0:T(8,128)S(1)}, u32[]{:S(2)}, u32[]{:S(2)}) collective-permute-start(f32[256,128]{1,0:T(8,128)S(1)} %spread.1.rest_0_), channel_id=1, source_target_pairs={{0,8},{8,0},{16,24},{24,16},{1,9},{9,1},{17,25},{25,17},{2,10},{10... | collective-permute-start | bytes 393224 | tf_op jit(solution)/shard_map/ppermute | solution.py:564
  6.8 3.5 %collective-permute-start = (s32[1,128]{1,0:T(1,128)S(1)}, s32[1,128]{1,0:T(1,128)S(1)}, u32[]{:S(2)}, u32[]{:S(2)}) collective-permute-start(s32[1,128]{1,0:T(1,128)S(1)} %concatenate.86), channel_id=1, source_target_pairs={{0,1},{1,0},{2,3},{3,2},{4,5},{5,4},{6,7},{7,6},{8,9},{9,8},{10,11... | collective-permute-start | bytes 1544 | tf_op jit(solution)/shard_map/ppermute | solution.py:533
  10.3 3.6 %collective-permute-start.1 = (s32[2,128]{1,0:T(2,128)S(1)}, s32[2,128]{1,0:T(2,128)S(1)}, u32[]{:S(2)}, u32[]{:S(2)}) collective-permute-start(s32[2,128]{1,0:T(2,128)S(1)} %pad_add_fusion.3), channel_id=1, source_target_pairs={{0,2},{1,3},{2,0},{3,1},{4,6},{5,7},{6,4},{7,5},{8,10},{9,11},{10,... | collective-permute-start | bytes 3080 | tf_op jit(solution)/shard_map/ppermute | solution.py:533
  13.9 1.2 %collective-permute-start.2 = (s32[4,128]{1,0:T(4,128)S(1)}, s32[4,128]{1,0:T(4,128)S(1)}, u32[]{:S(2)}, u32[]{:S(2)}) collective-permute-start(s32[4,128]{1,0:T(4,128)S(1)} %pad_add_fusion.2), channel_id=1, source_target_pairs={{0,4},{4,0},{1,5},{5,1},{2,6},{6,2},{3,7},{7,3},{8,12},{12,8},{9,1... | collective-permute-start | bytes 6152 | tf_op jit(solution)/shard_map/ppermute | solution.py:533
  19.1 3.8 %copy-start.5 = (f32[8,65]{1,0:T(8,128)S(1)}, f32[8,65]{1,0:T(8,128)}, u32[]{:S(2)}) copy-start(f32[8,65]{1,0:T(8,128)} %param.10) | copy-start | bytes 6244
  19.1 3.7 %copy-start.6 = (f32[8,65]{1,0:T(8,128)S(1)}, f32[8,65]{1,0:T(8,128)}, u32[]{:S(2)}) copy-start(f32[8,65]{1,0:T(8,128)} %param.9) | copy-start | bytes 6244
  19.2 18.6 %all-to-all-start = ((f32[8,256,128]{2,1,0:T(8,128)}), f32[8,256,128]{2,1,0:T(8,128)S(1)}, u32[]{:S(2)}, u32[]{:S(2)}) async-start(f32[8,256,128]{2,1,0:T(8,128)} %bitcast.12), calls=%async_computation | async-start | bytes 2097152 | tf_op jit(solution)/shard_map/all_to_all | solution.py:604
  23.0 3.6 %collective-permute-start.6 = (s32[8,128]{1,0:T(8,128)S(1)}, s32[8,128]{1,0:T(8,128)S(1)}, u32[]{:S(2)}, u32[]{:S(2)}) collective-permute-start(s32[8,128]{1,0:T(8,128)S(1)} %get-tuple-element.14), channel_id=1, source_target_pairs={{0,8},{8,0},{16,24},{24,16},{1,9},{9,1},{17,25},{25,17},{2,10},{10... | collective-permute-start | bytes 12296 | tf_op jit(solution)/shard_map/ppermute | solution.py:533
  23.4 17.1 %collective-permute-start.10 = (f32[32,1024]{1,0:T(8,128)S(1)}, f32[32,1024]{1,0:T(8,128)S(1)}, u32[]{:S(2)}, u32[]{:S(2)}) collective-permute-start(f32[32,1024]{1,0:T(8,128)S(1)} %get-tuple-element.19), channel_id=1, source_target_pairs={{0,4},{8,12},{16,20},{24,28},{4,0},{12,8},{20,16},{28,24},{1,5},{9... | collective-permute-start | bytes 393224 | tf_op jit(solution)/shard_map/ppermute | solution.py:523
  23.7 16.9 %collective-permute-start.11 = (f32[32,1024]{1,0:T(8,128)S(1)}, f32[32,1024]{1,0:T(8,128)S(1)}, u32[]{:S(2)}, u32[]{:S(2)}) collective-permute-start(f32[32,1024]{1,0:T(8,128)S(1)} %get-tuple-element.20), channel_id=1, source_target_pairs={{4,8},{12,16},{20,24},{8,4},{16,12},{24,20},{5,9},{13,17},{21,25},... | collective-permute-start | bytes 393224 | tf_op jit(solution)/shard_map/ppermute | solution.py:523
  26.6 5.0 %collective-permute-start.7 = (s32[16,128]{1,0:T(8,128)S(1)}, s32[16,128]{1,0:T(8,128)S(1)}, u32[]{:S(2)}, u32[]{:S(2)}) collective-permute-start(s32[16,128]{1,0:T(8,128)S(1)} %pad_add_fusion), channel_id=1, source_target_pairs={{0,16},{8,24},{16,0},{24,8},{1,17},{9,25},{17,1},{25,9},{2,18},{10... | collective-permute-start | bytes 24584 | tf_op jit(solution)/shard_map/ppermute | solution.py:533
  38.9 1.8 %copy-start = (f32[128,1024]{1,0:T(8,128)S(1)}, f32[128,1024]{1,0:T(8,128)}, u32[]{:S(2)}) copy-start(f32[128,1024]{1,0:T(8,128)} %own_ref.1) | copy-start | bytes 1572868
  38.9 1.7 %collective-permute-start.8 = (f32[64,1024]{1,0:T(8,128)S(1)}, f32[64,1024]{1,0:T(8,128)S(1)}, u32[]{:S(2)}, u32[]{:S(2)}) collective-permute-start(f32[64,1024]{1,0:T(8,128)S(1)} %get-tuple-element.17), channel_id=1, source_target_pairs={{0,4},{8,12},{16,20},{24,28},{4,0},{12,8},{20,16},{28,24},{1,5},{9... | collective-permute-start | bytes 786440 | tf_op jit(solution)/shard_map/ppermute | solution.py:523
  39.3 1.4 %collective-permute-start.9 = (f32[64,1024]{1,0:T(8,128)S(1)}, f32[64,1024]{1,0:T(8,128)S(1)}, u32[]{:S(2)}, u32[]{:S(2)}) collective-permute-start(f32[64,1024]{1,0:T(8,128)S(1)} %get-tuple-element.18), channel_id=1, source_target_pairs={{4,8},{12,16},{20,24},{8,4},{16,12},{24,20},{5,9},{13,17},{21,25},... | collective-permute-start | bytes 786440 | tf_op jit(solution)/shard_map/ppermute | solution.py:523
  40.8 4.6 %collective-permute-start.12 = (f32[176,128]{1,0:T(8,128)S(1)}, f32[176,128]{1,0:T(8,128)S(1)}, u32[]{:S(2)}, u32[]{:S(2)}) collective-permute-start(f32[176,128]{1,0:T(8,128)S(1)} %get-tuple-element.21), channel_id=1, source_target_pairs={{0,1},{2,3},{1,0},{3,2},{4,5},{6,7},{5,4},{7,6},{8,9},{10,11},{9,8... | collective-permute-start | bytes 270344 | tf_op jit(solution)/shard_map/ppermute | solution.py:523
  41.8 3.7 %collective-permute-start.13 = (f32[176,128]{1,0:T(8,128)S(1)}, f32[176,128]{1,0:T(8,128)S(1)}, u32[]{:S(2)}, u32[]{:S(2)}) collective-permute-start(f32[176,128]{1,0:T(8,128)S(1)} %get-tuple-element.22), channel_id=1, source_target_pairs={{1,2},{2,1},{5,6},{6,5},{9,10},{10,9},{13,14},{14,13},{17,18},{18,... | collective-permute-start | bytes 270344 | tf_op jit(solution)/shard_map/ppermute | solution.py:523
  42.4 3.0 %copy-start.3 = (f32[8]{0:T(128)S(1)}, f32[8]{0:T(128)}, u32[]{:S(2)}) copy-start(f32[8]{0:T(128)} %weight_ref.1) | copy-start | bytes 100
  63.7 40.0 %copy-start.2 = (f32[32,1024]{1,0:T(8,128)S(1)}, f32[32,1024]{1,0:T(8,128)}, u32[]{:S(2)}) copy-start(f32[32,1024]{1,0:T(8,128)} %param.6) | copy-start | bytes 393220
